TPU v7x, 256 devices: a whole 4x4x8 slice. The times are simulated.
256 devices in a mesh: dp: 32 (over z, x_hi, core), tensor: 8 (over y, x_lo).
Axes of the slice: x: 4 (x_hi: 2, x_lo: 2; x = x_hi * 2 + x_lo), y: 4, z: 8, core: 2. Of those that a mesh axis runs over, the one named last changes fastest.
Arguments:
- x_ckpt: bfloat16 [4096, 5120], P(('dp', 'tensor')), may hold values from -6 to 6
- d_out: bfloat16 [4096, 5120], P(('dp', 'tensor')), may hold values from -24 to 24
- norm_gain: bfloat16 [5120], replicated, may hold values from 0.099609375 to 1.8984375
- w_query: bfloat16 [5120, 3072], P('dp', 'tensor'), may hold values from -0.078125 to 0.078125
- w_key: bfloat16 [5120, 1024], P('dp', 'tensor'), may hold values from -0.078125 to 0.078125
- w_value: bfloat16 [5120, 1024], P('dp', 'tensor'), may hold values from -0.078125 to 0.078125
- w_out: bfloat16 [3072, 5120], P('tensor', 'dp'), may hold values from -0.109375 to 0.109375
- key_cache: bfloat16 [32, 1024, 1024], P('dp', None, 'tensor')
- value_cache: bfloat16 [32, 1024, 1024], P('dp', None, 'tensor'), may hold values from -6 to 6
- slab_start: int32 [32], P('dp'), may hold values from 0 to 8191
- prefix_len: int32 [32], P('dp'), may hold values from 128 to 1024, as said below
Outputs:
- d_input: bfloat16 [4096, 5120], P(('dp', 'tensor'))
- grad_query: bfloat16 [5120, 3072], P('dp', 'tensor')
- grad_key: bfloat16 [5120, 1024], P('dp', 'tensor')
- grad_value: bfloat16 [5120, 1024], P('dp', 'tensor')
- grad_out: bfloat16 [3072, 5120], P('tensor', 'dp')
- grad_gain: float32 [5120], P(('dp', 'tensor'))
Inputs may be any that keep to these rules, and one draw needn't show every extreme that they name: `prefix_len`: one data group has all 1024 slots live in every draw.
All inputs are finite; a program needn't handle non-finite values.
Results may differ from a plain program's by a relative error of at most 0.03.
Values may be sent and summed in bfloat16 or wider, within the bound.
No kernel may reach another device: no remote copies, remote signals or barrier semaphores. Data moves between devices by JAX's collectives and lax.ppermute only.
A program may use at most 128 MiB of HBM per device.

v0:
```python
import math

import jax
import jax.numpy as jnp
from jax import lax
from jax.sharding import PartitionSpec as P

HD = 128
QPER = 3


EPS = 1e-06
THETA = 1000000.0


def angle_tables(start, count, width):
    positions = (start + jnp.arange(count, dtype=jnp.int32)).astype(jnp.float32)
    freqs = jnp.power(
        jnp.float32(THETA), jnp.arange(width // 2, dtype=jnp.float32) * (-2.0 / width)
    )
    phase = positions[:, None] * freqs[None, :]
    return (jnp.cos(phase)[:, None, :], jnp.sin(phase)[:, None, :])


def rotate(vectors, cosine, sine):
    half = vectors.shape[-1] // 2
    first = vectors[..., :half]
    second = vectors[..., half:]
    return jnp.concatenate(
        [first * cosine - second * sine, second * cosine + first * sine], axis=-1
    )


def unrotate(vectors, cosine, sine):
    half = vectors.shape[-1] // 2
    first = vectors[..., :half]
    second = vectors[..., half:]
    return jnp.concatenate(
        [first * cosine + second * sine, second * cosine - first * sine], axis=-1
    )


def contract_rows(left, right):
    return lax.dot_general(
        left, right, (((0,), (0,)), ((), ())), preferred_element_type=jnp.float32
    )


def contract_cols(left, right):
    return lax.dot_general(
        left, right, (((1,), (1,)), ((), ())), preferred_element_type=jnp.float32
    )


def body(
    x_ckpt,
    d_out,
    norm_gain,
    w_query,
    w_key,
    w_value,
    w_out,
    key_cache,
    value_cache,
    slab_start,
    prefix_len,
):
    whole_x, whole_dy = (
        lax.all_gather(x_ckpt, "tensor", axis=0, tiled=True),
        lax.all_gather(d_out, "tensor", axis=0, tiled=True),
    )
    wq, wk, wv = (
        lax.all_gather(w_query, "dp", axis=0, tiled=True),
        lax.all_gather(w_key, "dp", axis=0, tiled=True),
        lax.all_gather(w_value, "dp", axis=0, tiled=True),
    )
    rows = whole_x.shape[0]
    head = HD
    group = QPER
    kv_local = wk.shape[1] // head
    q_cols = wq.shape[1]
    kv_cols = wk.shape[1]
    query_rows = group * rows
    norm_weight = norm_gain.astype(jnp.float32)
    input_float = whole_x.astype(jnp.float32)
    reciprocal_root_mean = lax.rsqrt(
        jnp.mean(input_float * input_float, axis=1, keepdims=True) + EPS
    )
    normalized_rows = (input_float * reciprocal_root_mean * norm_weight).astype(jnp.bfloat16)
    raw_q = jnp.dot(normalized_rows, wq, preferred_element_type=jnp.float32)
    raw_k = jnp.dot(normalized_rows, wk, preferred_element_type=jnp.float32)
    raw_v = jnp.dot(normalized_rows, wv, preferred_element_type=jnp.float32)
    cosine, sine = angle_tables(slab_start[0], rows, head)
    queries = rotate(raw_q.reshape(rows, kv_local * group, head), cosine, sine).astype(jnp.bfloat16)
    keys_new = rotate(raw_k.reshape(rows, kv_local, head), cosine, sine).astype(jnp.bfloat16)
    values_new = raw_v.reshape(rows, kv_local, head).astype(jnp.bfloat16)
    query_mat = (
        queries.reshape(rows, kv_local, group, head)
        .transpose(1, 2, 0, 3)
        .reshape(kv_local, query_rows, head)
    )
    prefix = key_cache.shape[1]
    block = min(prefix, 1024)
    count_blocks = prefix // block
    key_blocks = key_cache.reshape(count_blocks, block, kv_local, head)
    value_blocks = value_cache.reshape(count_blocks, block, kv_local, head)
    bases = jnp.arange(count_blocks, dtype=jnp.int32) * block
    limit = prefix_len[0]
    token_of_row = jnp.arange(query_rows, dtype=jnp.int32) % rows
    slab_valid = (jnp.arange(rows, dtype=jnp.int32)[None, :] <= token_of_row[:, None])[None]

    def block_scores(keys, base):
        scores = jnp.einsum(
            "grd,jgd->grj", query_mat, keys, preferred_element_type=jnp.float32
        ) / math.sqrt(head)
        valid = base + jnp.arange(keys.shape[0], dtype=jnp.int32) < limit
        return (scores, valid[None, None, :])

    slab_scores = jnp.einsum(
        "grd,ugd->gru", query_mat, keys_new, preferred_element_type=jnp.float32
    ) / math.sqrt(head)
    first_top = jnp.max(jnp.where(slab_valid, slab_scores, -jnp.inf), axis=-1)
    first_total = jnp.sum(
        jnp.where(slab_valid, jnp.exp(slab_scores - first_top[..., None]), 0.0), axis=-1
    )

    def stats_step(carry, blocks):
        top, total = carry
        keys, base = blocks
        scores, valid = block_scores(keys, base)
        new_top = jnp.maximum(top, jnp.max(jnp.where(valid, scores, -jnp.inf), axis=-1))
        total = total * jnp.exp(top - new_top) + jnp.sum(
            jnp.where(valid, jnp.exp(scores - new_top[..., None]), 0.0), axis=-1
        )
        return ((new_top, total), None)

    (top, total), _ = lax.scan(stats_step, (first_top, first_total), (key_blocks, bases))

    def weights_of(scores, valid):
        return jnp.where(valid, jnp.exp(scores - top[..., None]), 0.0) / total[..., None]

    slab_weights = weights_of(slab_scores, slab_valid)
    slab_probs = slab_weights.astype(jnp.bfloat16)
    first_sum = jnp.einsum(
        "gru,ugd->grd", slab_probs, values_new, preferred_element_type=jnp.float32
    )

    def value_step(accum, blocks):
        keys, vals, base = blocks
        scores, valid = block_scores(keys, base)
        probs = weights_of(scores, valid).astype(jnp.bfloat16)
        return (
            accum + jnp.einsum("grj,jgd->grd", probs, vals, preferred_element_type=jnp.float32),
            None,
        )

    attended_sum, _ = lax.scan(value_step, first_sum, (key_blocks, value_blocks, bases))
    attended_mat = attended_sum.astype(jnp.bfloat16)
    attended_flat = (
        attended_mat.reshape(kv_local, group, rows, head)
        .transpose(2, 0, 1, 3)
        .reshape(rows, q_cols)
    )
    columns = whole_dy
    d_attended = contract_cols(columns, lax.all_gather(w_out, "dp", axis=1, tiled=True)).astype(
        jnp.bfloat16
    )
    d_att_mat = (
        d_attended.reshape(rows, kv_local, group, head)
        .transpose(1, 2, 0, 3)
        .reshape(kv_local, query_rows, head)
    )
    delta = jnp.sum(d_att_mat.astype(jnp.float32) * attended_mat.astype(jnp.float32), axis=-1)

    def score_grads(weights, d_probs):
        return (weights * (d_probs - delta[..., None]) / math.sqrt(head)).astype(jnp.bfloat16)

    slab_dprobs = jnp.einsum(
        "grd,ugd->gru", d_att_mat, values_new, preferred_element_type=jnp.float32
    )
    slab_ds = score_grads(slab_weights, slab_dprobs)
    first_dq = jnp.einsum("gru,ugd->grd", slab_ds, keys_new, preferred_element_type=jnp.float32)
    dk_rot = jnp.einsum("gru,grd->ugd", slab_ds, query_mat, preferred_element_type=jnp.float32)
    dv_new = jnp.einsum("gru,grd->ugd", slab_probs, d_att_mat, preferred_element_type=jnp.float32)

    def grad_step(accum, blocks):
        keys, vals, base = blocks
        scores, valid = block_scores(keys, base)
        weights = weights_of(scores, valid)
        d_probs = jnp.einsum("grd,jgd->grj", d_att_mat, vals, preferred_element_type=jnp.float32)
        d_scores = score_grads(weights, d_probs)
        return (
            accum + jnp.einsum("grj,jgd->grd", d_scores, keys, preferred_element_type=jnp.float32),
            None,
        )

    dq_rot, _ = lax.scan(grad_step, first_dq, (key_blocks, value_blocks, bases))
    dq_heads = (
        dq_rot.reshape(kv_local, group, rows, head)
        .transpose(2, 0, 1, 3)
        .reshape(rows, kv_local * group, head)
    )
    dq = unrotate(dq_heads, cosine, sine).astype(jnp.bfloat16).reshape(rows, q_cols)
    dk = unrotate(dk_rot, cosine, sine).astype(jnp.bfloat16).reshape(rows, kv_cols)
    dv = dv_new.astype(jnp.bfloat16).reshape(rows, kv_cols)
    stacked = jnp.concatenate([dq, dk, dv], axis=1)
    stacked_cols = stacked.shape[1]
    columns = whole_dy
    shares = lax.psum_scatter(
        jnp.concatenate(
            [contract_rows(normalized_rows, stacked), contract_rows(columns, attended_flat)], axis=1
        ).astype(jnp.bfloat16),
        "dp",
        scatter_dimension=0,
        tiled=True,
    ).astype(jnp.float32)
    proj_share = shares[:, :stacked_cols]
    out_share = shares[:, stacked_cols:]
    total_term = contract_cols(dq, wq)
    total_term = total_term + contract_cols(dk, wk)
    normalized_gradient = lax.psum_scatter(
        total_term + contract_cols(dv, wv), "tensor", scatter_dimension=0, tiled=True
    )
    own_x = x_ckpt.astype(jnp.float32)
    own_inv = lax.rsqrt(jnp.mean(own_x * own_x, axis=1, keepdims=True) + EPS)
    own_hat = own_x * own_inv
    weighted_rows = normalized_gradient * norm_weight
    d_input = (
        d_out.astype(jnp.float32)
        + own_inv
        * (weighted_rows - own_hat * jnp.mean(weighted_rows * own_hat, axis=1, keepdims=True))
    ).astype(jnp.bfloat16)
    norm_weight_piece = jnp.sum(normalized_gradient * own_hat, axis=0)
    grad_gain = lax.psum_scatter(
        norm_weight_piece, ("dp", "tensor"), scatter_dimension=0, tiled=True
    )
    grad_query = proj_share[:, :q_cols].astype(jnp.bfloat16)
    grad_key = proj_share[:, q_cols : q_cols + kv_cols].astype(jnp.bfloat16)
    grad_value = proj_share[:, q_cols + kv_cols :].astype(jnp.bfloat16)
    grad_out = out_share.T.astype(jnp.bfloat16)
    return (d_input, grad_query, grad_key, grad_value, grad_out, grad_gain)


def solution(mesh):
    placed = (
        P(("dp", "tensor"), None),
        P(("dp", "tensor"), None),
        P(),
        P("dp", "tensor"),
        P("dp", "tensor"),
        P("dp", "tensor"),
        P("tensor", "dp"),
        P("dp", None, "tensor"),
        P("dp", None, "tensor"),
        P("dp"),
        P("dp"),
    )
    return jax.shard_map(
        body,
        mesh=mesh,
        in_specs=placed,
        out_specs=(
            P(("dp", "tensor"), None),
            P("dp", "tensor"),
            P("dp", "tensor"),
            P("dp", "tensor"),
            P("tensor", "dp"),
            P(("dp", "tensor")),
        ),
        check_vma=False,
    )
```

profile of v0, /device:TPU:8, one launch (start us, length us, event | category | flops | bytes accessed | tf_op | source)
XLA Modules:
  0.0 689.1 jit_solution(12026547702366770460)
XLA Ops:
  7.2 0.7 all-gather.7.cloned.1.call-update
  7.9 0.0 all-gather.11.cloned.1.call-start
  8.0 0.7 all-gather.11.cloned.1.call-update
  8.7 0.7 all-gather.17.cloned.1.call-update
  9.4 0.0 all-gather.13.cloned.1.call-start
  9.4 0.5 all-gather.13.cloned.1.call-update
  10.0 0.0 all-gather.15.cloned.1.call-start
  10.0 0.5 all-gather.15.cloned.1.call-update
  10.6 0.5 all-gather.9.cloned.1.call-update
  11.1 0.0 reduce-scatter.5.cloned.1.call-start
  12.5 0.7 convert_element_type.105
  13.2 0.6 iota_compare_fusion.1
  13.8 0.2 multiply_cosine_fusion.1
  14.0 40.7 %all-gather.7.cloned.1.call-done = bf16[128,5120]{1,0:T(8,128)(2,1)} async-done(((bf16[16,5120]{1,0:T(8,128)(2,1)}), bf16[128,5120]{1,0:T(8,128)(2,1)}) %all-gather.7.cloned.1.call-update) | async-done | bytes 1310736 | tf_op jit(solution)/shard_map/all_gather | solution.py:69
  54.7 1.6 fusion.1
  56.3 80.5 %all-gather.11.cloned.1.call-done = bf16[5120,128]{1,0:T(8,128)(2,1)} async-done(((bf16[160,128]{1,0:T(8,128)(2,1)}), bf16[5120,128]{1,0:T(8,128)(2,1)}) %all-gather.11.cloned.1.call-update) | async-done | bytes 1310736 | tf_op jit(solution)/shard_map/all_gather | solution.py:74
  136.9 2.4 convolution_bitcast_fusion.1
  139.3 0.2 fusion.65
  139.5 74.9 %all-gather.17.cloned.1.call-done = bf16[5120,128]{1,0:T(8,128)(2,1)} async-done(((bf16[160,128]{1,0:T(8,128)(2,1)}), bf16[5120,128]{1,0:T(8,128)(2,1)}) %all-gather.17.cloned.1.call-update) | async-done | bytes 1310736 | tf_op jit(solution)/shard_map/all_gather | solution.py:75
  214.5 2.5 convolution_convert_fusion.4
  217.0 37.7 %all-gather.13.cloned.1.call-done = bf16[128,5120]{1,0:T(8,128)(2,1)} async-done(((bf16[16,5120]{1,0:T(8,128)(2,1)}), bf16[128,5120]{1,0:T(8,128)(2,1)}) %all-gather.13.cloned.1.call-update) | async-done | bytes 1310736 | tf_op jit(solution)/shard_map/all_gather | solution.py:70
  254.7 89.8 %all-gather.15.cloned.1.call-done = bf16[384,5120]{0,1:T(8,128)(2,1)} async-done(((bf16[384,160]{0,1:T(8,128)(2,1)}), bf16[384,5120]{0,1:T(8,128)(2,1)}) %all-gather.15.cloned.1.call-update) | async-done | bytes 3932176 | tf_op jit(solution)/shard_map/all_gather | solution.py:165
  344.5 3.4 convolution_convert_fusion.2
  347.9 0.1 copy.40
  348.0 0.8 copy.41
  348.8 81.1 %all-gather.9.cloned.1.call-done = bf16[5120,384]{1,0:T(8,128)(2,1)} async-done(((bf16[160,384]{1,0:T(8,128)(2,1)}), bf16[5120,384]{1,0:T(8,128)(2,1)}) %all-gather.9.cloned.1.call-update) | async-done | bytes 3932176 | tf_op jit(solution)/shard_map/all_gather | solution.py:73
  429.9 3.8 fusion.79
  433.7 0.1 copy.39
  433.9 0.2 select_reduce_fusion.2
  434.1 0.1 select_reduce_fusion.1
  434.2 0.5 select_reduce_fusion
  434.7 1.1 fusion.6
  435.8 0.8 fusion.11
  436.7 0.5 fusion.13
  437.2 0.3 copy-done.20
  437.4 1.5 multiply_reduce_fusion
  438.9 2.3 fusion.4
  441.2 1.2 fusion.9
  442.4 0.2 convolution_bitcast_fusion
  442.7 1.2 convolution_add_fusion.2
  443.8 0.2 fusion.63
  444.0 0.1 copy.43
  444.3 0.5 fusion.58
  444.8 1.6 copy-done.3
  446.4 1.4 convolution_add_fusion
  447.8 2.0 convolution_add_fusion.1
  449.8 0.2 reduce-scatter.7.cloned.1.call-start
  450.1 0.6 copy-done.10
  450.7 0.1 copy.44
  450.8 0.4 copy-done.2
  451.2 1.2 fusion
  452.4 2.0 convolution_convert_fusion
  454.3 4.8 pad_maximum_fusion
  459.2 14.4 %copy.51 = bf16[5120,1024]{1,0:T(8,128)(2,1)} copy(bf16[5120,1024]{0,1:T(8,128)(2,1)} %pad_maximum_fusion) | data formatting | bytes 20971520
  473.6 0.9 copy-done.4
  474.5 0.2 fusion.25
  474.7 35.1 %reduce-scatter.5.cloned.1.call-done = f32[16,5120]{1,0:T(8,128)} async-done(((f32[128,5120]{1,0:T(8,128)}), f32[16,5120]{1,0:T(8,128)}) %reduce-scatter.5.cloned.1.call-update) | async-done | bytes 327696 | tf_op jit(solution)/shard_map/reduce_scatter | solution.py:221
  509.8 1.2 fusion.24
  511.1 81.0 %all-reduce = f32[5120]{0:T(1024)S(1)} all-reduce(f32[5120]{0:T(1024)S(1)} %get-tuple-element.96), channel_id=4, replica_groups=mesh['dp'=32,'tensor'=8] {'dp','tensor'}, use_global_device_ids=true, to_apply=%region_11.12.clone | all-reduce | flops 5120 | bytes 40960
  592.1 0.6 dynamic-slice.2
  592.7 1.8 fusion.23
  594.4 84.7 %reduce-scatter.7.cloned.1.call-done = bf16[160,1024]{1,0:T(8,128)(2,1)} async-done(((bf16[5120,1024]{1,0:T(8,128)(2,1)}), bf16[160,1024]{1,0:T(8,128)(2,1)}) %reduce-scatter.7.cloned.1.call-update) | async-done | bytes 327696
  679.2 1.4 fusion.81
  680.6 1.7 slice_bitcast_fusion
  (54 shorter events, 0.4 us)
Async XLA Ops:
  7.2 427.0 %copy-start = (bf16[1,1024,128]{2,1,0:T(8,128)(2,1)S(1)}, bf16[1,1024,128]{2,1,0:T(8,128)(2,1)}, u32[]{:S(2)}) copy-start(bf16[1,1024,128]{2,1,0:T(8,128)(2,1)} %param.18) | copy-start | bytes 786436
  7.2 47.5 %all-gather.7.cloned.1.call-start = ((), (), s32[]{:S(2)}) async-start(), calls=%async_computation.2 | async-start | bytes 1474560 | tf_op jit(solution)/shard_map/all_gather | solution.py:69
  7.9 128.9 %all-gather.11.cloned.1.call-start = ((), (), s32[]{:S(2)}) async-start(), calls=%async_computation.4 | async-start | bytes 1351680 | tf_op jit(solution)/shard_map/all_gather | solution.py:74
  8.7 205.8 %all-gather.17.cloned.1.call-start = ((), (), s32[]{:S(2)}) async-start(), calls=%async_computation.7 | async-start | bytes 1351680 | tf_op jit(solution)/shard_map/all_gather | solution.py:75
  9.4 245.3 %all-gather.13.cloned.1.call-start = ((), (), s32[]{:S(2)}) async-start(), calls=%async_computation.5 | async-start | bytes 1474560 | tf_op jit(solution)/shard_map/all_gather | solution.py:70
  10.0 334.6 %all-gather.15.cloned.1.call-start = ((), (), s32[]{:S(2)}) async-start(), calls=%async_computation.6 | async-start | bytes 4055040 | tf_op jit(solution)/shard_map/all_gather | solution.py:165
  10.6 419.3 %all-gather.9.cloned.1.call-start = ((), (), s32[]{:S(2)}) async-start(), calls=%async_computation.3 | async-start | bytes 4055040 | tf_op jit(solution)/shard_map/all_gather | solution.py:73
  11.1 498.7 %reduce-scatter.5.cloned.1.call-start = ((), (), s32[]{:S(2)}) async-start(), calls=%async_computation.8 | async-start | bytes 2949120 | tf_op jit(solution)/shard_map/reduce_scatter | solution.py:221
  13.2 126.1 %copy-start.12 = (f32[128]{0:T(128)}, f32[128]{0:T(128)S(1)}, u32[]{:S(2)}) copy-start(f32[128]{0:T(128)S(1)} %add_convert_fusion.2) | copy-start | bytes 1540
  56.3 373.5 %copy-start.17 = (f32[128]{0:T(128)}, f32[128]{0:T(128)S(1)}, u32[]{:S(2)}) copy-start(f32[128]{0:T(128)S(1)} %add_rsqrt_fusion) | copy-start | bytes 1540
  56.3 158.1 %copy-start.1 = (bf16[128,5120]{1,0:T(8,128)(2,1)S(1)}, bf16[128,5120]{1,0:T(8,128)(2,1)}, u32[]{:S(2)}) copy-start(bf16[128,5120]{1,0:T(8,128)(2,1)} %all-gather.7.cloned.1.call-done) | copy-start | bytes 3932164
  139.5 294.3 %copy-start.8 = (bf16[128,64]{0,1:T(8,128)(2,1)}, bf16[128,64]{0,1:T(8,128)(2,1)S(1)}, u32[]{:S(2)}) copy-start(bf16[128,64]{0,1:T(8,128)(2,1)S(1)} %get-tuple-element.109) | copy-start | bytes 49156
  348.8 85.4 %copy-start.14 = (pred[1024]{0:T(1024)(128)(4,1)S(1)}, pred[1024]{0:T(1024)(128)(4,1)}, u32[]{:S(2)}) copy-start(pred[1024]{0:T(1024)(128)(4,1)} %iota_compare_fusion.1) | copy-start | bytes 3076
  434.2 1.6 copy-start.11
  434.7 2.0 copy-start.15
  434.7 2.0 copy-start.19
  435.8 1.4 copy-start.16
  436.7 0.8 copy-start.20
  441.2 2.6 copy-start.13
  441.2 3.0 copy-start.5
  444.2 2.1 copy-start.3
  446.4 1.4 copy-start.6
  446.4 1.4 copy-start.9
  449.8 0.9 copy-start.10
  449.8 1.4 copy-start.2
  449.8 229.4 %reduce-scatter.7.cloned.1.call-start = ((), (), s32[]{:S(2)}) async-start(), calls=%async_computation.9 | async-start | bytes 10813440
  451.2 1.2 copy-start.18
  473.6 0.9 copy-start.4
  473.6 119.1 %copy-start.7 = (bf16[16,5120]{1,0:T(8,128)(2,1)S(1)}, bf16[16,5120]{1,0:T(8,128)(2,1)}, u32[]{:S(2)}) copy-start(bf16[16,5120]{1,0:T(8,128)(2,1)} %param.12) | copy-start | bytes 491524
Sparse Core Ops, SparseCore 0:
  9.8 44.8 all-gather.6
  57.4 79.3 all-gather.10
  139.6 74.8 all-gather.16
  216.1 38.5 all-gather.12
  257.3 87.1 all-gather.14
  347.2 82.6 all-gather.8
  450.0 59.8 reduce-scatter.4
  514.3 164.8 reduce-scatter.6
where the time goes:
time: 690 us; the launch traced here: 689 us
  waiting for transfers between devices  528 us (77%)
  blocking collectives  81 us (12%)
  matrix products  27.5 us (4%)
  local copies, waits for them, and re-layouts  23.2 us (3%)
  between operations  15.8 us (2%)
  other arithmetic  12.9 us (2%)
    all_gather x1, waiting for transfers between devices, body(): lax.all_gather(w_out, 'dp', axis=1, tiled=True)  89.8 us
    unnamed x9, waiting for transfers between devices  88.4 us
    all_gather x1, waiting for transfers between devices, body(): lax.all_gather(w_query, 'dp', axis=0, tiled=True)  81.1 us
    unnamed x1, blocking collectives  81 us
    all_gather x1, waiting for transfers between devices, body(): lax.all_gather(w_key, 'dp', axis=0, tiled=True)  80.5 us
    all_gather x1, waiting for transfers between devices, body(): lax.all_gather(w_value, 'dp', axis=0, tiled=True)  74.9 us
    all_gather x1, waiting for transfers between devices, body(): lax.all_gather(x_ckpt, 'tensor', axis=0, tiled=True)  40.7 us
    all_gather x1, waiting for transfers between devices, body(): lax.all_gather(d_out, 'tensor', axis=0, tiled=True)  37.7 us
  transfers between devices with their start and end apart: 8, of which 8 were waited for; matrix products, arithmetic and copies ran while one was open for 6% of the time, Pallas kernels for 0%

commit v1 on v0

v1 whole, which is shorter than its diff:
```python
import functools
import math

import jax
import jax.numpy as jnp
from jax import lax
from jax.experimental import pallas as pl
from jax.experimental.pallas import tpu as pltpu
from jax.sharding import Mesh
from jax.sharding import PartitionSpec as P

HD = 128
QPER = 3
EPS = 1e-06
THETA = 1000000.0

Z = 8
Q = 4
T = 8
QUARTER = ("xh", "c")
HEADS = ("y", "xl")
PLANE = ("xh", "c", "y", "xl")
VMEM = 48 * 1024 * 1024
F32 = jnp.float32
BF16 = jnp.bfloat16


def call(kernel, outs, n_in, smem=0, scratch=(), flops=0, nbytes=0, trans=0):
    specs = [pl.BlockSpec(memory_space=pltpu.SMEM)] * smem
    specs += [pl.BlockSpec(memory_space=pltpu.VMEM)] * (n_in - smem)
    return pl.pallas_call(
        kernel,
        out_shape=outs,
        in_specs=specs,
        out_specs=jax.tree.map(lambda _: pl.BlockSpec(memory_space=pltpu.VMEM), outs),
        scratch_shapes=list(scratch),
        compiler_params=pltpu.CompilerParams(vmem_limit_bytes=VMEM),
        cost_estimate=pl.CostEstimate(flops=flops, bytes_accessed=nbytes, transcendentals=trans),
    )


def sds(shape, dtype=BF16):
    return jax.ShapeDtypeStruct(shape, dtype)


def dot(a, b, ca, cb):
    return lax.dot_general(a, b, (((ca,), (cb,)), ((), ())), preferred_element_type=F32)


def prep_weights(wq, wk, wv, wo, qkv, wot):
    qkv[:, :384] = wq[...]
    qkv[:, 384:512] = wk[...]
    qkv[:, 512:640] = wv[...]
    wot[...] = wo[...].T


def prep_tokens(z_ref, x, dy, gain, n_out, o_out):
    z = z_ref[0]
    xf = x[...].astype(F32)
    inv = lax.rsqrt(jnp.mean(xf * xf, axis=1, keepdims=True) + EPS)
    for s in range(Z):
        start = pl.multiple_of(lax.rem(z + (Z - s), Z) * 640, 128)
        piece = x[:, pl.ds(start, 640)].astype(F32) * inv
        piece = (piece * gain[:, pl.ds(start, 640)].astype(F32)).astype(BF16)
        grad = dy[:, pl.ds(start, 640)]
        for q in range(Q):
            n = piece[:, 160 * q : 160 * (q + 1)]
            o = grad[:, 160 * q : 160 * (q + 1)]
            for t in range(T):
                n_out[q, t, :, 160 * s : 160 * (s + 1)] = n
                o_out[q, t, :, 160 * s : 160 * (s + 1)] = o


def project(tokens, *refs):
    blocks, out, w = refs[:Z], refs[Z], refs[Z + 1]
    for s in range(Z):
        w[160 * s : 160 * (s + 1), :] = blocks[s][...]
    for r in range(4):
        rows = slice(128 * r, 128 * (r + 1))
        out[r] = dot(tokens[rows, :], w[...], 1, 0).astype(BF16)


def heads_to_rows(a):
    return jnp.concatenate([a[:, HD * h : HD * (h + 1)] for h in range(QPER)], axis=0)


def rows_to_heads(a):
    n = a.shape[0] // QPER
    return jnp.concatenate([a[n * h : n * (h + 1), :] for h in range(QPER)], axis=1)


def attend(limit_ref, parts, cosf, sinf, kc, vc, q_out, k_out, v_out, w_out, att_out):
    raw = parts[0].astype(F32) + parts[1].astype(F32) + parts[2].astype(F32) + parts[3].astype(F32)
    cos, sin = cosf[...], sinf[...]

    def rotate(v):
        return v * cos + jnp.roll(v, HD // 2, axis=1) * sin

    q = jnp.concatenate(
        [rotate(raw[:, HD * h : HD * (h + 1)]) for h in range(QPER)], axis=0
    ).astype(BF16)
    k = rotate(raw[:, 384:512]).astype(BF16)
    v = raw[:, 512:640].astype(BF16)
    q_out[...] = q
    k_out[...] = k
    v_out[...] = v
    rows, slots, new = q.shape[0], kc.shape[0], k.shape[0]
    scale = 1.0 / math.sqrt(HD)
    old_s = dot(q, kc[...], 1, 1) * scale
    new_s = dot(q, k, 1, 1) * scale
    old_ok = lax.broadcasted_iota(jnp.int32, (rows, slots), 1) < limit_ref[0]
    token = lax.rem(lax.broadcasted_iota(jnp.int32, (rows, new), 0), new)
    new_ok = lax.broadcasted_iota(jnp.int32, (rows, new), 1) <= token
    old_s = jnp.where(old_ok, old_s, -jnp.inf)
    new_s = jnp.where(new_ok, new_s, -jnp.inf)
    top = jnp.maximum(
        jnp.max(old_s, axis=1, keepdims=True), jnp.max(new_s, axis=1, keepdims=True)
    )
    old_e = jnp.exp(old_s - top)
    new_e = jnp.exp(new_s - top)
    total = jnp.sum(old_e, axis=1, keepdims=True) + jnp.sum(new_e, axis=1, keepdims=True)
    share = 1.0 / total
    old_w = old_e * share
    new_w = new_e * share
    w_out[:, :slots] = old_w
    w_out[:, slots:] = new_w
    att = dot(old_w.astype(BF16), vc[...], 1, 0) + dot(new_w.astype(BF16), v, 1, 0)
    att_out[...] = rows_to_heads(att.astype(BF16))


def attend_grad(parts, att, w, q, k, v, cosf, sinf, kc, vc, out):
    da = parts[0].astype(F32) + parts[1].astype(F32) + parts[2].astype(F32) + parts[3].astype(F32)
    da = heads_to_rows(da.astype(BF16))
    at = heads_to_rows(att[...])
    delta = jnp.sum(da.astype(F32) * at.astype(F32), axis=1, keepdims=True)
    slots = kc.shape[0]
    scale = 1.0 / math.sqrt(HD)
    old_d = dot(da, vc[...], 1, 1)
    new_d = dot(da, v[...], 1, 1)
    new_w = w[:, slots:]
    old_ds = (w[:, :slots] * (old_d - delta) * scale).astype(BF16)
    new_ds = (new_w * (new_d - delta) * scale).astype(BF16)
    dq = dot(old_ds, kc[...], 1, 0) + dot(new_ds, k[...], 1, 0)
    dk = dot(new_ds, q[...], 0, 0)
    dv = dot(new_w.astype(BF16), da, 0, 0)
    cos, sin = cosf[...], sinf[...]

    def unrotate(a):
        return a * cos - jnp.roll(a, HD // 2, axis=1) * sin

    for h in range(QPER):
        out[:, HD * h : HD * (h + 1)] = unrotate(dq[128 * h : 128 * (h + 1), :]).astype(BF16)
    out[:, 384:512] = unrotate(dk).astype(BF16)
    out[:, 512:640] = dv.astype(BF16)


def weight_grad(tokens, cot, out, c):
    for xh in range(2):
        for core in range(2):
            g = 2 * xh + core
            c[128 * g : 128 * (g + 1), :] = cot[core, xh]
    for s in range(Z):
        part = tokens[:, 160 * s : 160 * (s + 1)]
        out[s] = dot(part, c[...], 0, 0).astype(BF16)


def input_grad(tokens, cot, *refs):
    blocks, out, gain_out, w = refs[:Z], refs[Z], refs[Z + 1], refs[Z + 2]
    for s in range(Z):
        w[160 * s : 160 * (s + 1), :] = blocks[s][...]
    total = jnp.zeros((1, Z * 160), F32)
    for xh in range(2):
        for core in range(2):
            g = 2 * xh + core
            rows = slice(128 * g, 128 * (g + 1))
            dn = dot(cot[core, xh], w[...], 1, 1)
            out[rows, :] = dn.astype(BF16)
            total = total + jnp.sum(dn * tokens[rows, :].astype(F32), axis=0, keepdims=True)
    gain_out[...] = total


def finish(z_ref, parts, x, dy, gain, out, dn):
    z = z_ref[0]
    sums = []
    for q in range(Q):
        a = parts[q, 0].astype(F32)
        for t in range(1, T):
            a = a + parts[q, t].astype(F32)
        sums.append(a)
    for s in range(Z):
        start = pl.multiple_of(lax.rem(z + (Z - s), Z) * 640, 128)
        dn[:, pl.ds(start, 640)] = jnp.concatenate(
            [sums[q][:, 160 * s : 160 * (s + 1)] for q in range(Q)], axis=1
        )
    xf = x[...].astype(F32)
    inv = lax.rsqrt(jnp.mean(xf * xf, axis=1, keepdims=True) + EPS)
    xhat = xf * inv
    scaled = dn[...] * gain[...].astype(F32)
    mean = jnp.mean(scaled * xhat, axis=1, keepdims=True)
    out[...] = (dy[...].astype(F32) + inv * (scaled - xhat * mean)).astype(BF16)


def shift(a, by):
    return lax.ppermute(a, "z", [(i, (i + by) % Z) for i in range(Z)])


def ring_gather(a):
    blocks = [None] * Z
    blocks[0] = ahead = back = a
    for k in range(1, 5):
        ahead = shift(ahead, 1)
        blocks[k] = ahead
        if k < 4:
            back = shift(back, -1)
            blocks[Z - k] = back
    return blocks


def ring_scatter(g):
    def add(a, b):
        return (a.astype(F32) + b.astype(F32)).astype(BF16)

    back, ahead = g[4], g[5]
    for k in range(1, 5):
        back = shift(back, -1)
        if k < 4:
            back = add(back, g[4 - k])
            ahead = shift(ahead, 1)
            if k < 3:
                ahead = add(ahead, g[5 + k])
    return g[0].astype(F32) + back.astype(F32) + ahead.astype(F32)


def body(x, dy, gain, wq, wk, wv, wo, kc, vc, slab_start, prefix_len):
    z = lax.axis_index("z").astype(jnp.int32)
    zs = z.reshape(1)
    gain_row = gain.reshape(1, -1)
    kc, vc = kc.reshape(1024, HD), vc.reshape(1024, HD)

    wqkv, wot = call(
        prep_weights, (sds((160, 640)), sds((160, 384))), 4, nbytes=1 << 20
    )(wq, wk, wv, wo)
    w_blocks = ring_gather(wqkv)
    n_send, o_send = call(
        prep_tokens, (sds((Q, T, 16, 1280)), sds((Q, T, 16, 1280))), 4, smem=1, nbytes=3 << 20
    )(zs, x, dy, gain_row)

    def spread(a):
        return lax.all_to_all(a.reshape(Q * T, 16, 1280), PLANE, 0, 0).reshape(512, 1280)

    n_all = spread(n_send)
    o_all = spread(o_send)
    o_blocks = ring_gather(wot)

    positions = (slab_start[0] + jnp.arange(128, dtype=jnp.int32)).astype(F32)
    freqs = jnp.power(F32(THETA), jnp.arange(HD // 2, dtype=F32) * (-2.0 / HD))
    phase = positions[:, None] * freqs[None, :]
    cos, sin = jnp.cos(phase), jnp.sin(phase)
    cosf = jnp.concatenate([cos, cos], axis=1)
    sinf = jnp.concatenate([-sin, sin], axis=1)

    def projected(tokens, blocks):
        cols = blocks[0].shape[1]
        part = call(
            project,
            sds((Q, 128, cols)),
            1 + Z,
            scratch=[pltpu.VMEM((1280, cols), BF16)],
            flops=2 * 512 * 1280 * cols,
            nbytes=4 << 20,
        )(tokens, *blocks)
        return lax.all_to_all(part, QUARTER, 0, 0)

    qkv_parts = projected(n_all, w_blocks)
    q, k, v, w, att = call(
        attend,
        (sds((384, HD)), sds((128, HD)), sds((128, HD)), sds((384, 1152), F32), sds((128, 384))),
        6,
        smem=1,
        flops=4 * 384 * 1152 * HD,
        nbytes=4 << 20,
        trans=384 * 1152,
    )(prefix_len, qkv_parts, cosf, sinf, kc, vc)

    def gather4(a):
        return lax.all_gather(lax.all_gather(a, "xh"), "c")

    att4 = gather4(att)

    def grads(tokens, cot):
        cols = cot.shape[-1]
        return call(
            weight_grad,
            sds((Z, 160, cols)),
            2,
            scratch=[pltpu.VMEM((512, cols), BF16)],
            flops=2 * 512 * 1280 * cols,
            nbytes=4 << 20,
        )(tokens, cot)

    da_parts = projected(o_all, o_blocks)
    g_out = grads(o_all, att4)
    out_sum = ring_scatter(g_out)
    dqkv = call(
        attend_grad, sds((128, 640)), 10, flops=6 * 384 * 1152 * HD, nbytes=4 << 20
    )(da_parts, att, w, q, k, v, cosf, sinf, kc, vc)
    dqkv4 = gather4(dqkv)
    g_qkv = grads(n_all, dqkv4)
    qkv_sum = ring_scatter(g_qkv)
    dn, gain_part = call(
        input_grad,
        (sds((512, 1280)), sds((1, 1280), F32)),
        2 + Z,
        scratch=[pltpu.VMEM((1280, 640), BF16)],
        flops=2 * 512 * 1280 * 640,
        nbytes=4 << 20,
    )(n_all, dqkv4, *w_blocks)
    dn_parts = lax.all_to_all(dn.reshape(Q * T, 16, 1280), PLANE, 0, 0)
    d_input = call(
        finish, sds((16, 5120)), 5, smem=1, scratch=[pltpu.VMEM((16, 5120), F32)], nbytes=2 << 20
    )(zs, dn_parts.reshape(Q, T, 16, 1280), x, dy, gain_row)

    by_s = gain_part.reshape(Z, T, 20)[::-1]
    by_z = lax.dynamic_slice_in_dim(jnp.concatenate([by_s, by_s], axis=0), Z - 1 - z, Z, axis=0)
    pieces = lax.all_to_all(by_z.reshape(Z * T, 20), ("z",) + HEADS, 0, 0, tiled=True)
    own = (z * Q + lax.axis_index(QUARTER)) * T + lax.axis_index(HEADS)
    own_gain = lax.dynamic_slice_in_dim(gain, own * 20, 20).astype(F32)
    grad_gain = jnp.sum(pieces, axis=0) / own_gain

    grads_qkv = qkv_sum.astype(BF16)
    return (
        d_input,
        grads_qkv[:, :384],
        grads_qkv[:, 384:512],
        grads_qkv[:, 512:640],
        out_sum.astype(BF16).T,
        grad_gain,
    )


def solution(mesh):
    fine = Mesh(mesh.devices.reshape(8, 2, 2, 4, 2), ("z", "xh", "c", "y", "xl"))
    dp = ("z", "xh", "c")
    both = dp + HEADS
    return jax.shard_map(
        body,
        mesh=fine,
        in_specs=(
            P(both, None),
            P(both, None),
            P(),
            P(dp, HEADS),
            P(dp, HEADS),
            P(dp, HEADS),
            P(HEADS, dp),
            P(dp, None, HEADS),
            P(dp, None, HEADS),
            P(dp),
            P(dp),
        ),
        out_specs=(
            P(both, None),
            P(dp, HEADS),
            P(dp, HEADS),
            P(dp, HEADS),
            P(HEADS, dp),
            P(both),
        ),
        check_vma=False,
    )
```

time: 690 us -> 218 us (0.32)
  waiting for transfers between devices: 528 us -> 43.4 us
  starting transfers between devices: 0.49 us -> 69.8 us
  blocking collectives: 81 us -> 45.9 us
  matrix products: 27.5 us -> 0 us
  Pallas kernels: 0 us -> 15.2 us
  between operations: 15.8 us -> 2.47 us
    all_gather x6 -> x0, waiting for transfers between devices: 405 us -> none  [the longest x1 89.8 us: body(): lax.all_gather(w_out, 'dp', axis=1, tiled=True)]
    unnamed x9 -> x0, waiting for transfers between devices: 88.4 us -> none
    unnamed x1 -> x0, blocking collectives: 81 us -> none
    ppermute x0 -> x28, starting transfers between devices: none -> 39.7 us  [shift(): return lax.ppermute(a, 'z', [(i, (i + by) % Z) for i in range(Z)])]
    ppermute x0 -> x28, waiting for transfers between devices: none -> 38.7 us  [shift(): return lax.ppermute(a, 'z', [(i, (i + by) % Z) for i in range(Z)])]
    reduce_scatter x1 -> x0, waiting for transfers between devices: 35.1 us -> none  [body(): lax.psum_scatter(total_term + contract_cols(dv, wv), 'tensor', scatter_di...]
    all_to_all x0 -> x5, starting transfers between devices: none -> 30.1 us  [the longest x2 8.75 us: projected(): return lax.all_to_all(part, QUARTER, 0, 0)]
    dot_general x18 -> x0, matrix products: 27.5 us -> none  [the longest x4 7.31 us: contract_cols(): lax.dot_general(left, right, (((1,), (1,)), ((), ())), preferred_element_...]
  transfers between devices with their start and end apart: 8 -> 33, of which waited for: 8 -> 14; matrix products, arithmetic and copies ran while one was open for 6% -> 6% of each run, Pallas kernels for 0% -> 4%
where the time goes in v1:
time: 218 us; the launch traced here: 217 us
  starting transfers between devices  69.8 us (32%)
  blocking collectives  45.9 us (21%)
  waiting for transfers between devices  43.4 us (20%)
  local copies, waits for them, and re-layouts  29.9 us (14%)
  Pallas kernels  15.2 us (7%)
  other arithmetic  10 us (5%)
  between operations  2.47 us (1%)
    ppermute x28, starting transfers between devices, shift(): return lax.ppermute(a, 'z', [(i, (i + by) % Z) for i in range(Z)])  39.7 us
    ppermute x28, waiting for transfers between devices, shift(): return lax.ppermute(a, 'z', [(i, (i + by) % Z) for i in range(Z)])  38.7 us
    all_to_all x1, blocking collectives, spread(): lax.all_to_all(a.reshape(Q * T, 16, 1280), PLANE, 0, 0).reshape(512, 1280)  26 us
    unnamed x107, local copies, waits for them, and re-layouts  25.4 us
    all_gather x4, blocking collectives, gather4(): return lax.all_gather(lax.all_gather(a, 'xh'), 'c')  19.9 us
    all_to_all x2, starting transfers between devices, projected(): return lax.all_to_all(part, QUARTER, 0, 0)  8.75 us
    all_to_all x1, starting transfers between devices, body(): lax.all_to_all(by_z.reshape(Z * T, 20), ('z',) + HEADS, 0, 0, tiled=True)  8.71 us
    all_to_all x1, starting transfers between devices, body(): dn_parts = lax.all_to_all(dn.reshape(Q * T, 16, 1280), PLANE, 0, 0)  6.94 us
  transfers between devices with their start and end apart: 33, of which 14 were waited for; matrix products, arithmetic and copies ran while one was open for 6% of the time, Pallas kernels for 4%

profile of v1, /device:TPU:8, one launch (start us, length us, event | category | flops | bytes accessed | tf_op | source)
XLA Modules:
  0.0 216.8 jit_solution(7625695751140450189)
XLA Ops:
  1.4 0.9 copy-done.27
  2.3 0.9 copy-done.29
  3.6 26.0 %all_to_all.34 = bf16[32,16,1280]{2,1,0:T(8,128)(2,1)S(1)} all-to-all(bf16[32,16,1280]{2,1,0:T(8,128)(2,1)S(1)} %bitcast.97), channel_id=1, replica_groups=mesh['z'=8,'xh'=2,'c'=2,'y'=4,'xl'=2] {'xh','c','y','xl'}, dimensions={0} | all-to-all | bytes 2621440 | tf_op jit(solution)/shard_map/all_to_all | solution.py:249
  29.7 5.7 %all-to-all-start.1 = ((bf16[32,16,1280]{2,1,0:T(8,128)(2,1)}), bf16[32,16,1280]{2,1,0:T(8,128)(2,1)S(1)}, u32[]{:S(2)}, u32[]{:S(2)}) async-start(bf16[32,16,1280]{2,1,0:T(8,128)(2,1)} %bitcast.96), calls=%async_computation.1 | async-start | bytes 2621440 | tf_op jit(solution)/shard_map/all_to_all | solution.py:249
  35.7 2.0 collective-permute-start.7
  37.7 4.0 %collective-permute-start.11 = (bf16[160,640]{1,0:T(8,128)(2,1)S(1)}, bf16[160,640]{1,0:T(8,128)(2,1)S(1)}, u32[]{:S(2)}, u32[]{:S(2)}) collective-permute-start(bf16[160,640]{1,0:T(8,128)(2,1)S(1)} %get-tuple-element.20.refs_0_), channel_id=1, source_target_pairs={{0,224},{32,0},{64,32},{96,64},{128,96},{160,128},{192,160},{224,1... | collective-permute-start | bytes 614408 | tf_op jit(solution)/shard_map/ppermute | solution.py:204
  41.7 5.3 %collective-permute-done.7.refs_1_ = bf16[160,640]{1,0:T(8,128)(2,1)S(1)} collective-permute-done((bf16[160,640]{1,0:T(8,128)(2,1)S(1)}, bf16[160,640]{1,0:T(8,128)(2,1)S(1)}, u32[]{:S(2)}, u32[]{:S(2)}) %collective-permute-start.7) | collective-permute-done | bytes 204832 | tf_op jit(solution)/shard_map/ppermute | solution.py:204
  47.0 3.2 %collective-permute-start.12 = (bf16[160,640]{1,0:T(8,128)(2,1)S(1)}, bf16[160,640]{1,0:T(8,128)(2,1)S(1)}, u32[]{:S(2)}, u32[]{:S(2)}) collective-permute-start(bf16[160,640]{1,0:T(8,128)(2,1)S(1)} %collective-permute-done.11.refs_7_), channel_id=1, source_target_pairs={{0,224},{32,0},{64,32},{96,64},{128,96},{160,128},{192,160},{224,1... | collective-permute-start | bytes 614408 | tf_op jit(solution)/shard_map/ppermute | solution.py:204
  50.2 4.6 %collective-permute-done.8.refs_2_ = bf16[160,640]{1,0:T(8,128)(2,1)S(1)} collective-permute-done((bf16[160,640]{1,0:T(8,128)(2,1)S(1)}, bf16[160,640]{1,0:T(8,128)(2,1)S(1)}, u32[]{:S(2)}, u32[]{:S(2)}) %collective-permute-start.8) | collective-permute-done | bytes 204832 | tf_op jit(solution)/shard_map/ppermute | solution.py:204
  54.8 3.2 %collective-permute-start.13 = (bf16[160,640]{1,0:T(8,128)(2,1)S(1)}, bf16[160,640]{1,0:T(8,128)(2,1)S(1)}, u32[]{:S(2)}, u32[]{:S(2)}) collective-permute-start(bf16[160,640]{1,0:T(8,128)(2,1)S(1)} %collective-permute-done.12.refs_6_), channel_id=1, source_target_pairs={{0,224},{32,0},{64,32},{96,64},{128,96},{160,128},{192,160},{224,1... | collective-permute-start | bytes 614408 | tf_op jit(solution)/shard_map/ppermute | solution.py:204
  58.1 3.7 %collective-permute-done.9.refs_3_ = bf16[160,640]{1,0:T(8,128)(2,1)S(1)} collective-permute-done((bf16[160,640]{1,0:T(8,128)(2,1)S(1)}, bf16[160,640]{1,0:T(8,128)(2,1)S(1)}, u32[]{:S(2)}, u32[]{:S(2)}) %collective-permute-start.9) | collective-permute-done | bytes 204832 | tf_op jit(solution)/shard_map/ppermute | solution.py:204
  61.8 3.3 %collective-permute-start.4 = (bf16[160,384]{1,0:T(8,128)(2,1)S(1)}, bf16[160,384]{1,0:T(8,128)(2,1)}, u32[]{:S(2)}, u32[]{:S(2)}) collective-permute-start(bf16[160,384]{1,0:T(8,128)(2,1)S(1)} %get-tuple-element.19.refs_0_), channel_id=1, source_target_pairs={{0,224},{32,0},{64,32},{96,64},{128,96},{160,128},{192,160},{224,1... | collective-permute-start | bytes 368648 | tf_op jit(solution)/shard_map/ppermute | solution.py:204
  65.1 5.1 %collective-permute-done.refs_1_ = bf16[160,384]{1,0:T(8,128)(2,1)S(1)} collective-permute-done((bf16[160,384]{1,0:T(8,128)(2,1)S(1)}, bf16[160,384]{1,0:T(8,128)(2,1)S(1)}, u32[]{:S(2)}, u32[]{:S(2)}) %collective-permute-start) | collective-permute-done | bytes 122912 | tf_op jit(solution)/shard_map/ppermute | solution.py:204
  70.2 2.1 shard_map.157
  77.8 4.3 %all-to-all-start.3 = ((bf16[4,128,640]{2,1,0:T(8,128)(2,1)}), bf16[4,128,640]{2,1,0:T(8,128)(2,1)S(1)}, u32[]{:S(2)}, u32[]{:S(2)}) async-start(bf16[4,128,640]{2,1,0:T(8,128)(2,1)} %shard_map.157), calls=%async_computation.3 | async-start | bytes 1310720 | tf_op jit(solution)/shard_map/all_to_all | solution.py:272
  82.1 3.2 %collective-permute-start.5 = (bf16[160,384]{1,0:T(8,128)(2,1)}, bf16[160,384]{1,0:T(8,128)(2,1)S(1)}, u32[]{:S(2)}, u32[]{:S(2)}) collective-permute-start(bf16[160,384]{1,0:T(8,128)(2,1)} %collective-permute-done.4.refs_7_), channel_id=1, source_target_pairs={{0,224},{32,0},{64,32},{96,64},{128,96},{160,128},{192,160},{224,1... | collective-permute-start | bytes 368648 | tf_op jit(solution)/shard_map/ppermute | solution.py:204
  85.4 3.6 %collective-permute-done.5.refs_6_ = bf16[160,384]{1,0:T(8,128)(2,1)S(1)} collective-permute-done((bf16[160,384]{1,0:T(8,128)(2,1)}, bf16[160,384]{1,0:T(8,128)(2,1)S(1)}, u32[]{:S(2)}, u32[]{:S(2)}) %collective-permute-start.5) | collective-permute-done | bytes 122912 | tf_op jit(solution)/shard_map/ppermute | solution.py:204
  88.9 3.6 %collective-permute-start.6 = (bf16[160,384]{1,0:T(8,128)(2,1)S(1)}, bf16[160,384]{1,0:T(8,128)(2,1)S(1)}, u32[]{:S(2)}, u32[]{:S(2)}) collective-permute-start(bf16[160,384]{1,0:T(8,128)(2,1)S(1)} %collective-permute-done.5.refs_6_), channel_id=1, source_target_pairs={{0,224},{32,0},{64,32},{96,64},{128,96},{160,128},{192,160},{224,1... | collective-permute-start | bytes 368648 | tf_op jit(solution)/shard_map/ppermute | solution.py:204
  93.2 1.8 collective-permute-done.6.refs_5_
  95.0 3.6 %collective-permute-done.3.refs_4_ = bf16[160,384]{1,0:T(8,128)(2,1)S(1)} collective-permute-done((bf16[160,384]{1,0:T(8,128)(2,1)S(1)}, bf16[160,384]{1,0:T(8,128)(2,1)S(1)}, u32[]{:S(2)}, u32[]{:S(2)}) %collective-permute-start.3) | collective-permute-done | bytes 122912 | tf_op jit(solution)/shard_map/ppermute | solution.py:204
  98.6 0.9 copy-done.41
  99.5 0.9 copy-done.43
  100.4 1.9 shard_map.156
  103.0 4.4 %all-to-all-start.2 = ((bf16[4,128,384]{2,1,0:T(8,128)(2,1)}), bf16[4,128,384]{2,1,0:T(8,128)(2,1)}, u32[]{:S(2)}, u32[]{:S(2)}) async-start(bf16[4,128,384]{2,1,0:T(8,128)(2,1)} %copy-done.5), calls=%async_computation.2 | async-start | bytes 786432 | tf_op jit(solution)/shard_map/all_to_all | solution.py:272
  107.5 1.0 fusion.16
  109.1 1.0 pad_maximum_fusion
  110.2 1.0 copy-done.9
  111.2 1.5 shard_map.158
  112.7 1.2 copy-done.3
  115.8 7.4 %all-gather.2 = bf16[256,384]{1,0:T(8,128)(2,1)S(1)} all-gather(bf16[128,384]{1,0:T(8,128)(2,1)S(1)} %get-tuple-element.21.att), channel_id=4, replica_groups=mesh['z'=8,'xh'=2,'c'=2,'y'=4,'xl'=2] {'xh'}, dimensions={0}, use_global_device_ids=true | all-gather | bytes 294912 | tf_op jit(solution)/shard_map/all_gather | solution.py:286
  123.8 1.5 copy-done.4
  125.3 0.9 copy-done.10
  128.0 0.9 copy-done.36
  131.3 2.0 shard_map.159
  133.2 8.0 %all-gather = bf16[256,640]{1,0:T(8,128)(2,1)S(1)} all-gather(bf16[128,640]{1,0:T(8,128)(2,1)S(1)} %shard_map.159), channel_id=2, replica_groups=mesh['z'=8,'xh'=2,'c'=2,'y'=4,'xl'=2] {'xh'}, dimensions={0}, use_global_device_ids=true | all-gather | bytes 491520 | tf_op jit(solution)/shard_map/all_gather | solution.py:286
  141.2 2.3 %all-gather.1 = bf16[4,128,640]{2,1,0:T(8,128)(2,1)S(1)} all-gather(bf16[2,128,640]{2,1,0:T(8,128)(2,1)S(1)} %bitcast.102), channel_id=3, replica_groups=mesh['z'=8,'xh'=2,'c'=2,'y'=4,'xl'=2] {'c'}, dimensions={0}, use_global_device_ids=true | all-gather | bytes 983040 | tf_op jit(solution)/shard_map/all_gather | solution.py:286
  143.5 2.3 %shard_map.162 = bf16[8,160,640]{2,1,0:T(8,128)(2,1)S(1)} custom-call(bf16[512,1280]{1,0:T(8,128)(2,1)S(1)} %bitcast.87, bf16[2,2,128,640]{3,2,1,0:T(8,128)(2,1)S(1)} %bitcast.91), custom_call_target="tpu_custom_call" | custom-call | flops 838860800 | bytes 4194304 | tf_op jit(solution)/shard_map/pallas_call | solution.py:292
  145.8 1.2 copy-done
  147.7 2.0 collective-permute-start.18
  149.7 2.2 %all-gather.3 = bf16[4,128,384]{2,1,0:T(8,128)(2,1)S(1)} all-gather(bf16[2,128,384]{2,1,0:T(8,128)(2,1)S(1)} %bitcast.103), channel_id=5, replica_groups=mesh['z'=8,'xh'=2,'c'=2,'y'=4,'xl'=2] {'c'}, dimensions={0}, use_global_device_ids=true | all-gather | bytes 589824 | tf_op jit(solution)/shard_map/all_gather | solution.py:286
  151.9 1.6 shard_map.163
  153.6 1.0 copy-done.2
  154.6 2.3 %shard_map.160 = (bf16[512,1280]{1,0:T(8,128)(2,1)S(1)}, f32[1,1280]{1,0:T(1,128)S(1)}) custom-call(bf16[512,1280]{1,0:T(8,128)(2,1)S(1)} %bitcast.88, bf16[2,2,128,640]{3,2,1,0:T(8,128)(2,1)S(1)} %bitcast.92, bf16[160,640]{1,0:T(8,128)(2,1)S(1)} %copy-done.12, bf16[160,640]{1,0:T(8,128)(2,1)S(1)} %copy-done.14, bf16[160,640]{1,0:T(8,128)(2,1)S(1)} %copy-done.18, ...), custom_call_target="tpu_custom_call" | custom-call | flops 838860800 | bytes 4194304 | tf_op jit(solution)/shard_map/pallas_call | solution.py:310
  156.9 1.0 copy-done.6
  158.8 8.7 %all-to-all-start.5 = ((f32[64,1,20]{2,1,0:T(1,128)}), f32[64,1,20]{2,1,0:T(1,128)S(1)}, u32[]{:S(2)}, u32[]{:S(2)}) async-start(f32[64,1,20]{2,1,0:T(1,128)} %bitcast.31), calls=%async_computation.5 | async-start | bytes 65536 | tf_op jit(solution)/shard_map/all_to_all | solution.py:325
  167.5 1.7 slice_bitcast_fusion.14
  169.2 3.0 %collective-permute-start.21 = (bf16[160,384]{1,0:T(8,128)(2,1)}, bf16[160,384]{1,0:T(8,128)(2,1)}, u32[]{:S(2)}, u32[]{:S(2)}) collective-permute-start(bf16[160,384]{1,0:T(8,128)(2,1)} %get-tuple-element.38), channel_id=1, source_target_pairs={{0,224},{32,0},{64,32},{96,64},{128,96},{160,128},{192,160},{224,1... | collective-permute-start | bytes 368648 | tf_op jit(solution)/shard_map/ppermute | solution.py:204
  172.1 4.7 %all-to-all-done.5 = f32[64,1,20]{2,1,0:T(1,128)S(1)} async-done(((f32[64,1,20]{2,1,0:T(1,128)}), f32[64,1,20]{2,1,0:T(1,128)S(1)}, u32[]{:S(2)}, u32[]{:S(2)}) %all-to-all-start.5) | async-done | bytes 5152 | tf_op jit(solution)/shard_map/all_to_all | solution.py:325
  176.9 6.9 %all-to-all-start.4 = ((bf16[32,16,1280]{2,1,0:T(8,128)(2,1)}), bf16[32,16,1280]{2,1,0:T(8,128)(2,1)S(1)}, u32[]{:S(2)}, u32[]{:S(2)}) async-start(bf16[32,16,1280]{2,1,0:T(8,128)(2,1)} %bitcast.95), calls=%async_computation.4 | async-start | bytes 2621440 | tf_op jit(solution)/shard_map/all_to_all | solution.py:318
  183.9 1.3 convert_divide_fusion
  185.2 1.0 fusion.11
  186.8 1.0 fusion.4
  188.5 3.9 %collective-permute-done.22 = bf16[160,384]{1,0:T(8,128)(2,1)S(1)} collective-permute-done((bf16[160,384]{1,0:T(8,128)(2,1)S(1)}, bf16[160,384]{1,0:T(8,128)(2,1)S(1)}, u32[]{:S(2)}, u32[]{:S(2)}) %collective-permute-start.22) | collective-permute-done | bytes 122912 | tf_op jit(solution)/shard_map/ppermute | solution.py:204
  192.4 1.0 fusion.10
  193.4 1.8 collective-permute-start.23
  195.6 1.2 collective-permute-done.15
  196.9 1.8 collective-permute-start.16
  199.2 2.8 %collective-permute-done.26 = bf16[160,384]{1,0:T(8,128)(2,1)S(1)} collective-permute-done((bf16[160,384]{1,0:T(8,128)(2,1)S(1)}, bf16[160,384]{1,0:T(8,128)(2,1)S(1)}, u32[]{:S(2)}, u32[]{:S(2)}) %collective-permute-start.26) | collective-permute-done | bytes 122912 | tf_op jit(solution)/shard_map/ppermute | solution.py:204
  201.9 1.0 fusion.9
  203.1 3.2 %collective-permute-start.24 = (bf16[160,384]{1,0:T(8,128)(2,1)S(1)}, bf16[160,384]{1,0:T(8,128)(2,1)S(1)}, u32[]{:S(2)}, u32[]{:S(2)}) collective-permute-start(bf16[160,384]{1,0:T(8,128)(2,1)S(1)} %get-tuple-element.34), channel_id=1, source_target_pairs={{0,224},{32,0},{64,32},{96,64},{128,96},{160,128},{192,160},{224,1... | collective-permute-start | bytes 368648 | tf_op jit(solution)/shard_map/ppermute | solution.py:204
  207.2 3.2 %collective-permute-start.17 = (bf16[160,640]{1,0:T(8,128)(2,1)S(1)}, bf16[160,640]{1,0:T(8,128)(2,1)S(1)}, u32[]{:S(2)}, u32[]{:S(2)}) collective-permute-start(bf16[160,640]{1,0:T(8,128)(2,1)S(1)} %get-tuple-element.28), channel_id=1, source_target_pairs={{0,224},{32,0},{64,32},{96,64},{128,96},{160,128},{192,160},{224,1... | collective-permute-start | bytes 614408 | tf_op jit(solution)/shard_map/ppermute | solution.py:204
  210.5 1.6 fusion.14
  212.1 2.1 collective-permute-done.20
  215.6 1.1 shard_map.161
  (147 shorter events, 20.6 us)
Async XLA Ops:
  1.4 28.3 %copy-start.37 = (bf16[1,5120]{1,0:T(2,128)(2,1)}, bf16[1,5120]{1,0:T(2,128)(2,1)S(1)}, u32[]{:S(2)}) copy-start(bf16[1,5120]{1,0:T(2,128)(2,1)S(1)} %reshape.84.gain) | copy-start | bytes 30724
  1.4 0.9 copy-start.27
  3.6 26.1 %copy-start.7 = (bf16[4,8,16,1280]{3,2,1,0:T(8,128)(2,1)}, bf16[4,8,16,1280]{3,2,1,0:T(8,128)(2,1)S(1)}, u32[]{:S(2)}) copy-start(bf16[4,8,16,1280]{3,2,1,0:T(8,128)(2,1)S(1)} %get-tuple-element.18) | copy-start | bytes 3932164
  29.7 5.7 %copy-start.52 = (bf16[384,160]{0,1:T(8,128)(2,1)S(1)}, bf16[384,160]{0,1:T(8,128)(2,1)}, u32[]{:S(2)}) copy-start(bf16[384,160]{0,1:T(8,128)(2,1)} %param.17) | copy-start | bytes 368644
  29.7 5.9 %copy-start.39 = (bf16[160,384]{1,0:T(8,128)(2,1)S(1)}, bf16[160,384]{1,0:T(8,128)(2,1)}, u32[]{:S(2)}) copy-start(bf16[160,384]{1,0:T(8,128)(2,1)} %wq.1) | copy-start | bytes 368644
  29.7 5.9 %copy-start.46 = (bf16[160,128]{1,0:T(8,128)(2,1)S(1)}, bf16[160,128]{1,0:T(8,128)(2,1)}, u32[]{:S(2)}) copy-start(bf16[160,128]{1,0:T(8,128)(2,1)} %wk.1) | copy-start | bytes 122884
  29.7 5.9 %copy-start.47 = (bf16[160,128]{1,0:T(8,128)(2,1)S(1)}, bf16[160,128]{1,0:T(8,128)(2,1)}, u32[]{:S(2)}) copy-start(bf16[160,128]{1,0:T(8,128)(2,1)} %wv.1) | copy-start | bytes 122884
  29.7 48.1 %all-to-all-start.1 = ((bf16[32,16,1280]{2,1,0:T(8,128)(2,1)}), bf16[32,16,1280]{2,1,0:T(8,128)(2,1)S(1)}, u32[]{:S(2)}, u32[]{:S(2)}) async-start(bf16[32,16,1280]{2,1,0:T(8,128)(2,1)} %bitcast.96), calls=%async_computation.1 | async-start | bytes 2621440 | tf_op jit(solution)/shard_map/all_to_all | solution.py:249
  35.7 36.7 %copy-start.40 = (bf16[160,384]{1,0:T(8,128)(2,1)}, bf16[160,384]{1,0:T(8,128)(2,1)S(1)}, u32[]{:S(2)}) copy-start(bf16[160,384]{1,0:T(8,128)(2,1)S(1)} %get-tuple-element.19.refs_0_) | copy-start | bytes 368644
  35.7 11.3 %collective-permute-start.7 = (bf16[160,640]{1,0:T(8,128)(2,1)S(1)}, bf16[160,640]{1,0:T(8,128)(2,1)S(1)}, u32[]{:S(2)}, u32[]{:S(2)}) collective-permute-start(bf16[160,640]{1,0:T(8,128)(2,1)S(1)} %get-tuple-element.20.refs_0_), channel_id=1, source_target_pairs={{0,32},{32,64},{64,96},{96,128},{128,160},{160,192},{192,224},{224... | collective-permute-start | bytes 614408 | tf_op jit(solution)/shard_map/ppermute | solution.py:204
  37.7 9.3 %collective-permute-start.11 = (bf16[160,640]{1,0:T(8,128)(2,1)S(1)}, bf16[160,640]{1,0:T(8,128)(2,1)S(1)}, u32[]{:S(2)}, u32[]{:S(2)}) collective-permute-start(bf16[160,640]{1,0:T(8,128)(2,1)S(1)} %get-tuple-element.20.refs_0_), channel_id=1, source_target_pairs={{0,224},{32,0},{64,32},{96,64},{128,96},{160,128},{192,160},{224,1... | collective-permute-start | bytes 614408 | tf_op jit(solution)/shard_map/ppermute | solution.py:204
  47.0 7.8 %collective-permute-start.8 = (bf16[160,640]{1,0:T(8,128)(2,1)S(1)}, bf16[160,640]{1,0:T(8,128)(2,1)S(1)}, u32[]{:S(2)}, u32[]{:S(2)}) collective-permute-start(bf16[160,640]{1,0:T(8,128)(2,1)S(1)} %collective-permute-done.7.refs_1_), channel_id=1, source_target_pairs={{0,32},{32,64},{64,96},{96,128},{128,160},{160,192},{192,224},{224... | collective-permute-start | bytes 614408 | tf_op jit(solution)/shard_map/ppermute | solution.py:204
  47.0 7.8 %collective-permute-start.12 = (bf16[160,640]{1,0:T(8,128)(2,1)S(1)}, bf16[160,640]{1,0:T(8,128)(2,1)S(1)}, u32[]{:S(2)}, u32[]{:S(2)}) collective-permute-start(bf16[160,640]{1,0:T(8,128)(2,1)S(1)} %collective-permute-done.11.refs_7_), channel_id=1, source_target_pairs={{0,224},{32,0},{64,32},{96,64},{128,96},{160,128},{192,160},{224,1... | collective-permute-start | bytes 614408 | tf_op jit(solution)/shard_map/ppermute | solution.py:204
  54.8 7.0 %collective-permute-start.9 = (bf16[160,640]{1,0:T(8,128)(2,1)S(1)}, bf16[160,640]{1,0:T(8,128)(2,1)S(1)}, u32[]{:S(2)}, u32[]{:S(2)}) collective-permute-start(bf16[160,640]{1,0:T(8,128)(2,1)S(1)} %collective-permute-done.8.refs_2_), channel_id=1, source_target_pairs={{0,32},{32,64},{64,96},{96,128},{128,160},{160,192},{192,224},{224... | collective-permute-start | bytes 614408 | tf_op jit(solution)/shard_map/ppermute | solution.py:204
  54.8 15.4 %collective-permute-start.13 = (bf16[160,640]{1,0:T(8,128)(2,1)S(1)}, bf16[160,640]{1,0:T(8,128)(2,1)S(1)}, u32[]{:S(2)}, u32[]{:S(2)}) collective-permute-start(bf16[160,640]{1,0:T(8,128)(2,1)S(1)} %collective-permute-done.12.refs_6_), channel_id=1, source_target_pairs={{0,224},{32,0},{64,32},{96,64},{128,96},{160,128},{192,160},{224,1... | collective-permute-start | bytes 614408 | tf_op jit(solution)/shard_map/ppermute | solution.py:204
  61.8 8.4 %collective-permute-start.10 = (bf16[160,640]{1,0:T(8,128)(2,1)S(1)}, bf16[160,640]{1,0:T(8,128)(2,1)S(1)}, u32[]{:S(2)}, u32[]{:S(2)}) collective-permute-start(bf16[160,640]{1,0:T(8,128)(2,1)S(1)} %collective-permute-done.9.refs_3_), channel_id=1, source_target_pairs={{0,32},{32,64},{64,96},{96,128},{128,160},{160,192},{192,224},{224... | collective-permute-start | bytes 614408 | tf_op jit(solution)/shard_map/ppermute | solution.py:204
  61.8 8.4 %collective-permute-start = (bf16[160,384]{1,0:T(8,128)(2,1)S(1)}, bf16[160,384]{1,0:T(8,128)(2,1)S(1)}, u32[]{:S(2)}, u32[]{:S(2)}) collective-permute-start(bf16[160,384]{1,0:T(8,128)(2,1)S(1)} %get-tuple-element.19.refs_0_), channel_id=1, source_target_pairs={{0,32},{32,64},{64,96},{96,128},{128,160},{160,192},{192,224},{224... | collective-permute-start | bytes 368648 | tf_op jit(solution)/shard_map/ppermute | solution.py:204
  61.8 20.3 %collective-permute-start.4 = (bf16[160,384]{1,0:T(8,128)(2,1)S(1)}, bf16[160,384]{1,0:T(8,128)(2,1)}, u32[]{:S(2)}, u32[]{:S(2)}) collective-permute-start(bf16[160,384]{1,0:T(8,128)(2,1)S(1)} %get-tuple-element.19.refs_0_), channel_id=1, source_target_pairs={{0,224},{32,0},{64,32},{96,64},{128,96},{160,128},{192,160},{224,1... | collective-permute-start | bytes 368648 | tf_op jit(solution)/shard_map/ppermute | solution.py:204
  70.2 2.1 copy-start.42
  70.2 15.2 %collective-permute-start.1 = (bf16[160,384]{1,0:T(8,128)(2,1)S(1)}, bf16[160,384]{1,0:T(8,128)(2,1)}, u32[]{:S(2)}, u32[]{:S(2)}) collective-permute-start(bf16[160,384]{1,0:T(8,128)(2,1)S(1)} %collective-permute-done.refs_1_), channel_id=1, source_target_pairs={{0,32},{32,64},{64,96},{96,128},{128,160},{160,192},{192,224},{224... | collective-permute-start | bytes 368648 | tf_op jit(solution)/shard_map/ppermute | solution.py:204
  77.8 25.2 %all-to-all-start.3 = ((bf16[4,128,640]{2,1,0:T(8,128)(2,1)}), bf16[4,128,640]{2,1,0:T(8,128)(2,1)S(1)}, u32[]{:S(2)}, u32[]{:S(2)}) async-start(bf16[4,128,640]{2,1,0:T(8,128)(2,1)} %shard_map.157), calls=%async_computation.3 | async-start | bytes 1310720 | tf_op jit(solution)/shard_map/all_to_all | solution.py:272
  82.1 6.8 %collective-permute-start.5 = (bf16[160,384]{1,0:T(8,128)(2,1)}, bf16[160,384]{1,0:T(8,128)(2,1)S(1)}, u32[]{:S(2)}, u32[]{:S(2)}) collective-permute-start(bf16[160,384]{1,0:T(8,128)(2,1)} %collective-permute-done.4.refs_7_), channel_id=1, source_target_pairs={{0,224},{32,0},{64,32},{96,64},{128,96},{160,128},{192,160},{224,1... | collective-permute-start | bytes 368648 | tf_op jit(solution)/shard_map/ppermute | solution.py:204
  85.4 7.2 %collective-permute-start.2 = (bf16[160,384]{1,0:T(8,128)(2,1)}, bf16[160,384]{1,0:T(8,128)(2,1)S(1)}, u32[]{:S(2)}, u32[]{:S(2)}) collective-permute-start(bf16[160,384]{1,0:T(8,128)(2,1)} %collective-permute-done.1.refs_2_), channel_id=1, source_target_pairs={{0,32},{32,64},{64,96},{96,128},{128,160},{160,192},{192,224},{224... | collective-permute-start | bytes 368648 | tf_op jit(solution)/shard_map/ppermute | solution.py:204
  88.9 6.1 %collective-permute-start.6 = (bf16[160,384]{1,0:T(8,128)(2,1)S(1)}, bf16[160,384]{1,0:T(8,128)(2,1)S(1)}, u32[]{:S(2)}, u32[]{:S(2)}) collective-permute-start(bf16[160,384]{1,0:T(8,128)(2,1)S(1)} %collective-permute-done.5.refs_6_), channel_id=1, source_target_pairs={{0,224},{32,0},{64,32},{96,64},{128,96},{160,128},{192,160},{224,1... | collective-permute-start | bytes 368648 | tf_op jit(solution)/shard_map/ppermute | solution.py:204
  92.5 6.1 %collective-permute-start.3 = (bf16[160,384]{1,0:T(8,128)(2,1)S(1)}, bf16[160,384]{1,0:T(8,128)(2,1)S(1)}, u32[]{:S(2)}, u32[]{:S(2)}) collective-permute-start(bf16[160,384]{1,0:T(8,128)(2,1)S(1)} %collective-permute-done.2.refs_3_), channel_id=1, source_target_pairs={{0,32},{32,64},{64,96},{96,128},{128,160},{160,192},{192,224},{224... | collective-permute-start | bytes 368648 | tf_op jit(solution)/shard_map/ppermute | solution.py:204
  100.4 9.8 %copy-start.8 = (bf16[1,1024,128]{2,1,0:T(8,128)(2,1)S(1)}, bf16[1,1024,128]{2,1,0:T(8,128)(2,1)}, u32[]{:S(2)}) copy-start(bf16[1,1024,128]{2,1,0:T(8,128)(2,1)} %param.18) | copy-start | bytes 786436
  103.0 20.8 %all-to-all-start.2 = ((bf16[4,128,384]{2,1,0:T(8,128)(2,1)}), bf16[4,128,384]{2,1,0:T(8,128)(2,1)}, u32[]{:S(2)}, u32[]{:S(2)}) async-start(bf16[4,128,384]{2,1,0:T(8,128)(2,1)} %copy-done.5), calls=%async_computation.2 | async-start | bytes 786432 | tf_op jit(solution)/shard_map/all_to_all | solution.py:272
  110.2 2.5 %copy-start.31 = (f32[128,128]{1,0:T(8,128)}, f32[128,128]{1,0:T(8,128)S(1)}, u32[]{:S(2)}) copy-start(f32[128,128]{1,0:T(8,128)S(1)} %get-tuple-element.45.cosf) | copy-start | bytes 196612
  110.2 5.6 %copy-start.33 = (f32[128,128]{1,0:T(8,128)}, f32[128,128]{1,0:T(8,128)S(1)}, u32[]{:S(2)}) copy-start(f32[128,128]{1,0:T(8,128)S(1)} %get-tuple-element.46.sinf) | copy-start | bytes 196612
  110.2 1.0 copy-start.9
  112.7 1.2 copy-start.3
  123.8 1.5 copy-start.4
  125.3 0.9 copy-start.10
  145.8 1.2 copy-start
  147.7 39.1 %collective-permute-start.14 = (bf16[160,640]{1,0:T(8,128)(2,1)}, bf16[160,640]{1,0:T(8,128)(2,1)}, u32[]{:S(2)}, u32[]{:S(2)}) collective-permute-start(bf16[160,640]{1,0:T(8,128)(2,1)} %get-tuple-element.32), channel_id=1, source_target_pairs={{0,224},{32,0},{64,32},{96,64},{128,96},{160,128},{192,160},{224,1... | collective-permute-start | bytes 614408 | tf_op jit(solution)/shard_map/ppermute | solution.py:204
  147.7 47.9 %collective-permute-start.18 = (bf16[160,640]{1,0:T(8,128)(2,1)S(1)}, bf16[160,640]{1,0:T(8,128)(2,1)S(1)}, u32[]{:S(2)}, u32[]{:S(2)}) collective-permute-start(bf16[160,640]{1,0:T(8,128)(2,1)S(1)} %get-tuple-element.33), channel_id=1, source_target_pairs={{0,32},{32,64},{64,96},{96,128},{128,160},{160,192},{192,224},{224... | collective-permute-start | bytes 614408 | tf_op jit(solution)/shard_map/ppermute | solution.py:204
  149.7 4.9 %copy-start.12 = (bf16[160,640]{1,0:T(8,128)(2,1)S(1)}, bf16[160,640]{1,0:T(8,128)(2,1)}, u32[]{:S(2)}) copy-start(bf16[160,640]{1,0:T(8,128)(2,1)} %copy-done.11) | copy-start | bytes 614404
  149.7 4.9 %copy-start.14 = (bf16[160,640]{1,0:T(8,128)(2,1)S(1)}, bf16[160,640]{1,0:T(8,128)(2,1)}, u32[]{:S(2)}) copy-start(bf16[160,640]{1,0:T(8,128)(2,1)} %copy-done.13) | copy-start | bytes 614404
  149.7 4.9 %copy-start.16 = (bf16[160,640]{1,0:T(8,128)(2,1)S(1)}, bf16[160,640]{1,0:T(8,128)(2,1)}, u32[]{:S(2)}) copy-start(bf16[160,640]{1,0:T(8,128)(2,1)} %copy-done.15) | copy-start | bytes 614404
  149.7 4.9 %copy-start.18 = (bf16[160,640]{1,0:T(8,128)(2,1)S(1)}, bf16[160,640]{1,0:T(8,128)(2,1)}, u32[]{:S(2)}) copy-start(bf16[160,640]{1,0:T(8,128)(2,1)} %copy-done.17) | copy-start | bytes 614404
  149.7 4.9 %copy-start.20 = (bf16[160,640]{1,0:T(8,128)(2,1)S(1)}, bf16[160,640]{1,0:T(8,128)(2,1)}, u32[]{:S(2)}) copy-start(bf16[160,640]{1,0:T(8,128)(2,1)} %copy-done.19) | copy-start | bytes 614404
  149.7 4.9 %copy-start.22 = (bf16[160,640]{1,0:T(8,128)(2,1)S(1)}, bf16[160,640]{1,0:T(8,128)(2,1)}, u32[]{:S(2)}) copy-start(bf16[160,640]{1,0:T(8,128)(2,1)} %copy-done.21) | copy-start | bytes 614404
  149.7 4.9 %copy-start.24 = (bf16[160,640]{1,0:T(8,128)(2,1)S(1)}, bf16[160,640]{1,0:T(8,128)(2,1)}, u32[]{:S(2)}) copy-start(bf16[160,640]{1,0:T(8,128)(2,1)} %copy-done.23) | copy-start | bytes 614404
  149.7 4.9 %copy-start.26 = (bf16[160,640]{1,0:T(8,128)(2,1)S(1)}, bf16[160,640]{1,0:T(8,128)(2,1)}, u32[]{:S(2)}) copy-start(bf16[160,640]{1,0:T(8,128)(2,1)} %copy-done.25) | copy-start | bytes 614404
  153.6 1.0 copy-start.2
  156.9 1.1 copy-start.6
  158.8 18.1 %all-to-all-start.5 = ((f32[64,1,20]{2,1,0:T(1,128)}), f32[64,1,20]{2,1,0:T(1,128)S(1)}, u32[]{:S(2)}, u32[]{:S(2)}) async-start(f32[64,1,20]{2,1,0:T(1,128)} %bitcast.31), calls=%async_computation.5 | async-start | bytes 65536 | tf_op jit(solution)/shard_map/all_to_all | solution.py:325
  169.2 17.6 %copy-start.1 = (bf16[8,160,640]{2,1,0:T(8,128)(2,1)S(1)}, bf16[8,160,640]{2,1,0:T(8,128)(2,1)}, u32[]{:S(2)}) copy-start(bf16[8,160,640]{2,1,0:T(8,128)(2,1)} %copy-done) | copy-start | bytes 4915204
  169.2 16.0 %collective-permute-start.21 = (bf16[160,384]{1,0:T(8,128)(2,1)}, bf16[160,384]{1,0:T(8,128)(2,1)}, u32[]{:S(2)}, u32[]{:S(2)}) collective-permute-start(bf16[160,384]{1,0:T(8,128)(2,1)} %get-tuple-element.38), channel_id=1, source_target_pairs={{0,224},{32,0},{64,32},{96,64},{128,96},{160,128},{192,160},{224,1... | collective-permute-start | bytes 368648 | tf_op jit(solution)/shard_map/ppermute | solution.py:204
  172.1 16.4 %collective-permute-start.25 = (bf16[160,384]{1,0:T(8,128)(2,1)}, bf16[160,384]{1,0:T(8,128)(2,1)S(1)}, u32[]{:S(2)}, u32[]{:S(2)}) collective-permute-start(bf16[160,384]{1,0:T(8,128)(2,1)} %get-tuple-element.39), channel_id=1, source_target_pairs={{0,32},{32,64},{64,96},{96,128},{128,160},{160,192},{192,224},{224... | collective-permute-start | bytes 368648 | tf_op jit(solution)/shard_map/ppermute | solution.py:204
  176.9 38.7 %all-to-all-start.4 = ((bf16[32,16,1280]{2,1,0:T(8,128)(2,1)}), bf16[32,16,1280]{2,1,0:T(8,128)(2,1)S(1)}, u32[]{:S(2)}, u32[]{:S(2)}) async-start(bf16[32,16,1280]{2,1,0:T(8,128)(2,1)} %bitcast.95), calls=%async_computation.4 | async-start | bytes 2621440 | tf_op jit(solution)/shard_map/all_to_all | solution.py:318
  186.2 6.2 %collective-permute-start.22 = (bf16[160,384]{1,0:T(8,128)(2,1)S(1)}, bf16[160,384]{1,0:T(8,128)(2,1)S(1)}, u32[]{:S(2)}, u32[]{:S(2)}) collective-permute-start(bf16[160,384]{1,0:T(8,128)(2,1)S(1)} %fusion.11), channel_id=1, source_target_pairs={{0,224},{32,0},{64,32},{96,64},{128,96},{160,128},{192,160},{224,1... | collective-permute-start | bytes 368648 | tf_op jit(solution)/shard_map/ppermute | solution.py:204
  187.7 9.1 %collective-permute-start.15 = (bf16[160,640]{1,0:T(8,128)(2,1)S(1)}, bf16[160,640]{1,0:T(8,128)(2,1)S(1)}, u32[]{:S(2)}, u32[]{:S(2)}) collective-permute-start(bf16[160,640]{1,0:T(8,128)(2,1)S(1)} %fusion.4), channel_id=1, source_target_pairs={{0,224},{32,0},{64,32},{96,64},{128,96},{160,128},{192,160},{224,1... | collective-permute-start | bytes 614408 | tf_op jit(solution)/shard_map/ppermute | solution.py:204
  193.4 5.7 %collective-permute-start.23 = (bf16[160,384]{1,0:T(8,128)(2,1)S(1)}, bf16[160,384]{1,0:T(8,128)(2,1)S(1)}, u32[]{:S(2)}, u32[]{:S(2)}) collective-permute-start(bf16[160,384]{1,0:T(8,128)(2,1)S(1)} %get-tuple-element.36), channel_id=1, source_target_pairs={{0,224},{32,0},{64,32},{96,64},{128,96},{160,128},{192,160},{224,1... | collective-permute-start | bytes 368648 | tf_op jit(solution)/shard_map/ppermute | solution.py:204
  195.2 6.7 %collective-permute-start.26 = (bf16[160,384]{1,0:T(8,128)(2,1)S(1)}, bf16[160,384]{1,0:T(8,128)(2,1)S(1)}, u32[]{:S(2)}, u32[]{:S(2)}) collective-permute-start(bf16[160,384]{1,0:T(8,128)(2,1)S(1)} %get-tuple-element.37), channel_id=1, source_target_pairs={{0,32},{32,64},{64,96},{96,128},{128,160},{160,192},{192,224},{224... | collective-permute-start | bytes 368648 | tf_op jit(solution)/shard_map/ppermute | solution.py:204
  196.9 9.4 %collective-permute-start.16 = (bf16[160,640]{1,0:T(8,128)(2,1)S(1)}, bf16[160,640]{1,0:T(8,128)(2,1)S(1)}, u32[]{:S(2)}, u32[]{:S(2)}) collective-permute-start(bf16[160,640]{1,0:T(8,128)(2,1)S(1)} %get-tuple-element.30), channel_id=1, source_target_pairs={{0,224},{32,0},{64,32},{96,64},{128,96},{160,128},{192,160},{224,1... | collective-permute-start | bytes 614408 | tf_op jit(solution)/shard_map/ppermute | solution.py:204
  198.7 8.4 %collective-permute-start.19 = (bf16[160,640]{1,0:T(8,128)(2,1)S(1)}, bf16[160,640]{1,0:T(8,128)(2,1)S(1)}, u32[]{:S(2)}, u32[]{:S(2)}) collective-permute-start(bf16[160,640]{1,0:T(8,128)(2,1)S(1)} %get-tuple-element.31), channel_id=1, source_target_pairs={{0,32},{32,64},{64,96},{96,128},{128,160},{160,192},{192,224},{224... | collective-permute-start | bytes 614408 | tf_op jit(solution)/shard_map/ppermute | solution.py:204
  203.0 12.6 %copy-start.28 = (bf16[16,5120]{1,0:T(8,128)(2,1)S(1)}, bf16[16,5120]{1,0:T(8,128)(2,1)}, u32[]{:S(2)}) copy-start(bf16[16,5120]{1,0:T(8,128)(2,1)} %x.3) | copy-start | bytes 491524
  203.0 12.6 %copy-start.30 = (bf16[16,5120]{1,0:T(8,128)(2,1)S(1)}, bf16[16,5120]{1,0:T(8,128)(2,1)}, u32[]{:S(2)}) copy-start(bf16[16,5120]{1,0:T(8,128)(2,1)} %dy.3) | copy-start | bytes 491524
  203.0 12.6 %copy-start.38 = (bf16[1,5120]{1,0:T(2,128)(2,1)S(1)}, bf16[1,5120]{1,0:T(2,128)(2,1)}, u32[]{:S(2)}) copy-start(bf16[1,5120]{1,0:T(2,128)(2,1)} %copy-done.37) | copy-start | bytes 30724
  203.0 7.5 %collective-permute-start.27 = (bf16[160,384]{1,0:T(8,128)(2,1)S(1)}, bf16[160,384]{1,0:T(8,128)(2,1)S(1)}, u32[]{:S(2)}, u32[]{:S(2)}) collective-permute-start(bf16[160,384]{1,0:T(8,128)(2,1)S(1)} %get-tuple-element.35), channel_id=1, source_target_pairs={{0,32},{32,64},{64,96},{96,128},{128,160},{160,192},{192,224},{224... | collective-permute-start | bytes 368648 | tf_op jit(solution)/shard_map/ppermute | solution.py:204
  203.1 7.4 %collective-permute-start.24 = (bf16[160,384]{1,0:T(8,128)(2,1)S(1)}, bf16[160,384]{1,0:T(8,128)(2,1)S(1)}, u32[]{:S(2)}, u32[]{:S(2)}) collective-permute-start(bf16[160,384]{1,0:T(8,128)(2,1)S(1)} %get-tuple-element.34), channel_id=1, source_target_pairs={{0,224},{32,0},{64,32},{96,64},{128,96},{160,128},{192,160},{224,1... | collective-permute-start | bytes 368648 | tf_op jit(solution)/shard_map/ppermute | solution.py:204
  207.1 7.0 %collective-permute-start.20 = (bf16[160,640]{1,0:T(8,128)(2,1)S(1)}, bf16[160,640]{1,0:T(8,128)(2,1)S(1)}, u32[]{:S(2)}, u32[]{:S(2)}) collective-permute-start(bf16[160,640]{1,0:T(8,128)(2,1)S(1)} %get-tuple-element.29), channel_id=1, source_target_pairs={{0,32},{32,64},{64,96},{96,128},{128,160},{160,192},{192,224},{224... | collective-permute-start | bytes 614408 | tf_op jit(solution)/shard_map/ppermute | solution.py:204
  207.2 7.0 %collective-permute-start.17 = (bf16[160,640]{1,0:T(8,128)(2,1)S(1)}, bf16[160,640]{1,0:T(8,128)(2,1)S(1)}, u32[]{:S(2)}, u32[]{:S(2)}) collective-permute-start(bf16[160,640]{1,0:T(8,128)(2,1)S(1)} %get-tuple-element.28), channel_id=1, source_target_pairs={{0,224},{32,0},{64,32},{96,64},{128,96},{160,128},{192,160},{224,1... | collective-permute-start | bytes 614408 | tf_op jit(solution)/shard_map/ppermute | solution.py:204
  (22 other events, 16.5 us)

commit v2 on v1

v2 whole, which is shorter than its diff:
```python
import math

import jax
import jax.numpy as jnp
from jax import lax
from jax.experimental import pallas as pl
from jax.experimental.pallas import tpu as pltpu
from jax.sharding import Mesh
from jax.sharding import PartitionSpec as P

HD = 128
QPER = 3
EPS = 1e-06
THETA = 1000000.0

Z = 8
Q = 4
T = 8
QUARTER = ("xh", "c")
HEADS = ("y", "xl")
PLANE = ("xh", "c", "y", "xl")
VMEM = 16 * 1024 * 1024
ALL = 60 * 1024 * 1024
F32 = jnp.float32
BF16 = jnp.bfloat16


def call(
    kernel, outs, shapes, smem=0, far=0, far_out=0, scratch=(), flops=0, nbytes=0, trans=0, grant=VMEM
):
    near = len(shapes) - smem - far
    return pl.pallas_call(
        kernel,
        out_shape=tuple(outs),
        in_specs=[pl.BlockSpec(memory_space=pltpu.SMEM)] * smem
        + [pl.BlockSpec()] * near
        + [pl.BlockSpec(memory_space=pltpu.HBM)] * far,
        out_specs=tuple([pl.BlockSpec()] * (len(outs) - far_out))
        + tuple([pl.BlockSpec(memory_space=pltpu.HBM)] * far_out),
        scratch_shapes=list(scratch),
        compiler_params=pltpu.CompilerParams(vmem_limit_bytes=grant),
        cost_estimate=pl.CostEstimate(flops=flops, bytes_accessed=nbytes, transcendentals=trans),
    )


def sds(shape, dtype=BF16):
    return jax.ShapeDtypeStruct(shape, dtype)


def run(kernel, outs, args, **kw):
    return call(kernel, outs, [sds(a.shape, a.dtype) for a in args], **kw)(*args)


def dot(a, b, ca, cb):
    return lax.dot_general(a, b, (((ca,), (cb,)), ((), ())), preferred_element_type=F32)


def copies_of(pairs, sems):
    made = [pltpu.make_async_copy(src, dst, sems.at[i]) for i, (src, dst) in enumerate(pairs)]
    for copy in made:
        copy.start()
    return made


def join(wq, wk, wv, wo, out):
    out[:, :384] = wq[...]
    out[:, 384:512] = wk[...]
    out[:, 512:640] = wv[...]
    out[:, 640:] = wo[...]


def split(total, q_out, k_out, v_out, o_out):
    q_out[...] = total[:, :384]
    k_out[...] = total[:, 384:512]
    v_out[...] = total[:, 512:640]
    o_out[...] = total[:, 640:]


def prep_tokens(gain, x_far, dy_far, out_far, x, dy, out, sems):
    copy_x, copy_dy = copies_of([(x_far, x), (dy_far, dy)], sems)
    copy_x.wait()
    xf = x[...].astype(F32)
    inv = lax.rsqrt(jnp.mean(xf * xf, axis=1, keepdims=True) + EPS)
    n = (xf * inv * gain[...].reshape(1, -1).astype(F32)).astype(BF16)
    copy_dy.wait()
    sent = []
    for q in range(Q):
        cols = [slice((Q * z + q) * 160, (Q * z + q + 1) * 160) for z in range(Z)]
        row = jnp.concatenate([n[:, c] for c in cols] + [dy[:, c] for c in cols], axis=1)
        for t in range(T):
            out[q * T + t] = row
        part = pl.ds(q * T, T)
        copy = pltpu.make_async_copy(out.at[part], out_far.at[part], sems.at[2 + q])
        copy.start()
        sent.append(copy)
    for copy in sent:
        copy.wait()


def project(g_ref, tokens, w, keep, send, held):
    for first, last, at in ((0, 384, 0), (384, 640, 0), (640, 1024, 1280)):
        part = dot(tokens[:, at : at + 1280], w[:, first:last], 1, 0).astype(BF16)
        for g in range(Q):
            held[g_ref[0] ^ g, :, first:last] = part[128 * g : 128 * (g + 1), :]
    for xh in range(2):
        keep[xh] = held[2 * xh]
        send[xh] = held[2 * xh + 1]


def add(keep, pair, out):
    out[...] = (keep[1].astype(F32) + pair[1].astype(F32)).astype(BF16)


def heads_to_rows(a):
    return jnp.concatenate([a[:, HD * h : HD * (h + 1)] for h in range(QPER)], axis=0)


def rows_to_heads(a):
    n = a.shape[0] // QPER
    return jnp.concatenate([a[n * h : n * (h + 1), :] for h in range(QPER)], axis=1)


def attend(limit_ref, mine, pair, far, cosf, sinf, kc, vc, out):
    raw = mine[0].astype(F32) + pair[0].astype(F32) + far[...].astype(F32)
    cos, sin = cosf[...], sinf[...]

    def rotate(v):
        return v * cos + jnp.roll(v, HD // 2, axis=1) * sin

    def unrotate(v):
        return v * cos - jnp.roll(v, HD // 2, axis=1) * sin

    q = jnp.concatenate(
        [rotate(raw[:, HD * h : HD * (h + 1)]) for h in range(QPER)], axis=0
    ).astype(BF16)
    k = rotate(raw[:, 384:512]).astype(BF16)
    v = raw[:, 512:640].astype(BF16)
    da = heads_to_rows(raw[:, 640:].astype(BF16))
    rows, slots, new = q.shape[0], kc.shape[0], k.shape[0]
    scale = 1.0 / math.sqrt(HD)
    old_s = dot(q, kc[...], 1, 1) * scale
    new_s = dot(q, k, 1, 1) * scale
    old_ok = lax.broadcasted_iota(jnp.int32, (rows, slots), 1) < limit_ref[0]
    token = lax.rem(lax.broadcasted_iota(jnp.int32, (rows, new), 0), new)
    new_ok = lax.broadcasted_iota(jnp.int32, (rows, new), 1) <= token
    old_s = jnp.where(old_ok, old_s, -jnp.inf)
    new_s = jnp.where(new_ok, new_s, -jnp.inf)
    top = jnp.maximum(
        jnp.max(old_s, axis=1, keepdims=True), jnp.max(new_s, axis=1, keepdims=True)
    )
    old_e = jnp.exp(old_s - top)
    new_e = jnp.exp(new_s - top)
    total = jnp.sum(old_e, axis=1, keepdims=True) + jnp.sum(new_e, axis=1, keepdims=True)
    share = 1.0 / total
    old_w = old_e * share
    new_w = new_e * share
    new_p = new_w.astype(BF16)
    att = (dot(old_w.astype(BF16), vc[...], 1, 0) + dot(new_p, v, 1, 0)).astype(BF16)
    out[:, 640:] = rows_to_heads(att)

    delta = jnp.sum(da.astype(F32) * att.astype(F32), axis=1, keepdims=True)
    old_ds = (old_w * (dot(da, vc[...], 1, 1) - delta) * scale).astype(BF16)
    new_ds = (new_w * (dot(da, v, 1, 1) - delta) * scale).astype(BF16)
    dq = dot(old_ds, kc[...], 1, 0) + dot(new_ds, k, 1, 0)
    dk = dot(new_ds, q, 0, 0)
    dv = dot(new_p, da, 0, 0)
    for h in range(QPER):
        out[:, HD * h : HD * (h + 1)] = unrotate(dq[128 * h : 128 * (h + 1), :]).astype(BF16)
    out[:, 384:512] = unrotate(dk).astype(BF16)
    out[:, 512:640] = dv.astype(BF16)


def gather_rows(g_ref, cots, cot):
    for d, block in enumerate(cots):
        rows = pl.ds(pl.multiple_of((g_ref[0] ^ d) * 128, 128), 128)
        cot[rows, :] = block[:, : cot.shape[1]]


def weight_grad(g_ref, tokens, c0, c1, c2, c3, out, cot):
    gather_rows(g_ref, (c0, c1, c2, c3), cot)
    for r in range(5):
        cols = slice(256 * r, 256 * (r + 1))
        late = slice(1280 + 256 * r, 1280 + 256 * (r + 1))
        out[cols, :640] = dot(tokens[:, cols], cot[:, :640], 0, 0).astype(BF16)
        out[cols, 640:] = dot(tokens[:, late], cot[:, 640:], 0, 0).astype(BF16)


def input_grad(g_ref, tokens, c0, c1, c2, c3, w, out, cot):
    gather_rows(g_ref, (c0, c1, c2, c3), cot)
    sums = []
    for r in range(5):
        cols = slice(256 * r, 256 * (r + 1))
        dn = dot(cot[...], w[cols, :640], 1, 1)
        sums.append(jnp.sum(dn * tokens[:, cols].astype(F32), axis=0, keepdims=True))
        dn = dn.astype(BF16)
        for b in range(Q * T):
            out[b, :, cols] = dn[16 * b : 16 * (b + 1), :]
    total = jnp.concatenate(sums, axis=1)
    total = jnp.concatenate([total[:, 160 * z : 160 * (z + 1)] for z in range(Z)], axis=0)
    high = total.astype(BF16)
    low = (total - high.astype(F32)).astype(BF16)
    both = jnp.concatenate([high, low], axis=0)
    zero = jnp.zeros((16, 108), BF16)
    for t in range(T):
        tile = jnp.concatenate([both[:, 20 * t : 20 * (t + 1)], zero], axis=1)
        for q in range(Q):
            out[q * T + t, :, 1280:] = tile


def finish(g_ref, parts, x, dy, gain, out, gain_out):
    sums = []
    for q in range(Q):
        a = parts[q, 0, :, :1280].astype(F32)
        for t in range(1, T):
            a = a + parts[q, t, :, :1280].astype(F32)
        sums.append(a)
    tile = parts[g_ref[0], 0, :, 1280:].astype(F32)
    for t in range(1, T):
        tile = tile + parts[g_ref[0], t, :, 1280:].astype(F32)
    gain_out[...] = tile[:8, :] + tile[8:, :]
    dn = jnp.concatenate(
        [sums[q][:, 160 * z : 160 * (z + 1)] for z in range(Z) for q in range(Q)], axis=1
    )
    xf = x[...].astype(F32)
    inv = lax.rsqrt(jnp.mean(xf * xf, axis=1, keepdims=True) + EPS)
    xhat = xf * inv
    scaled = dn * gain[...].reshape(1, -1).astype(F32)
    mean = jnp.mean(scaled * xhat, axis=1, keepdims=True)
    out[...] = (dy[...].astype(F32) + inv * (scaled - xhat * mean)).astype(BF16)


def tie(*arrays):
    return lax.optimization_barrier(arrays)


def swap(a, axis):
    return lax.ppermute(a, axis, [(0, 1), (1, 0)])


def body(x, dy, gain, wq, wk, wv, wo, kc, vc, slab_start, prefix_len):
    z = lax.axis_index("z").astype(jnp.int32)
    gs = lax.axis_index(QUARTER).astype(jnp.int32).reshape(1)
    kc, vc = kc.reshape(1024, HD), vc.reshape(1024, HD)

    (w_own,) = run(
        join,
        [sds((160, 1024))],
        (wq, wk, wv, wo.T),
        grant=ALL,
        nbytes=1 << 20,
    )
    x_in, w_own = tie(x, w_own)
    w = lax.all_gather(w_own, "z", axis=0, tiled=True)
    (sent,) = run(
        prep_tokens,
        [sds((Q * T, 16, 2560))],
        (gain, x_in, dy),
        far=2,
        far_out=1,
        scratch=[
            pltpu.VMEM((16, 5120), BF16),
            pltpu.VMEM((16, 5120), BF16),
            pltpu.VMEM((Q * T, 16, 2560), BF16),
            pltpu.SemaphoreType.DMA((2 + Q,)),
        ],
        grant=ALL,
        nbytes=3 << 20,
    )
    tokens = lax.all_to_all(sent, PLANE, 0, 0).reshape(512, 2560)

    positions = (slab_start[0] + jnp.arange(128, dtype=jnp.int32)).astype(F32)
    freqs = jnp.power(F32(THETA), jnp.arange(HD // 2, dtype=F32) * (-2.0 / HD))
    phase = positions[:, None] * freqs[None, :]
    cos, sin = jnp.cos(phase), jnp.sin(phase)
    cosf = jnp.concatenate([cos, cos], axis=1)
    sinf = jnp.concatenate([-sin, sin], axis=1)
    tokens, cosf, sinf = tie(tokens, cosf, sinf)

    keep, send = run(
        project,
        [sds((2, 128, 1024)), sds((2, 128, 1024))],
        (gs, tokens, w),
        smem=1,
        scratch=[pltpu.VMEM((Q, 128, 1024), BF16)],
        flops=2 * 512 * 1280 * 1024,
        nbytes=7 << 20,
    )
    pair = swap(send, "c")
    (passed,) = run(add, [sds((128, 1024))], (keep, pair), nbytes=1 << 20)
    far = swap(passed, "xh")
    (cot,) = run(
        attend,
        [sds((128, 1024))],
        (prefix_len, keep, pair, far, cosf, sinf, kc, vc),
        smem=1,
        flops=10 * 384 * 1152 * HD,
        nbytes=4 << 20,
        trans=384 * 1152,
    )
    across = swap(cot, "xh")
    cots = (cot, swap(cot, "c"), across, swap(across, "c"))
    (grads,) = run(
        weight_grad,
        [sds((1280, 1024))],
        (gs, tokens, *cots),
        smem=1,
        scratch=[pltpu.VMEM((512, 1024), BF16)],
        flops=2 * 512 * 1280 * 1024,
        nbytes=8 << 20,
    )
    late, grads = tie(tokens, grads)
    total = lax.psum_scatter(grads, "z", scatter_dimension=0, tiled=True)
    (dn,) = run(
        input_grad,
        [sds((Q * T, 16, 1408))],
        (gs, late, *cots, w),
        smem=1,
        scratch=[pltpu.VMEM((512, 640), BF16)],
        flops=2 * 512 * 1280 * 640,
        nbytes=7 << 20,
    )
    dn_parts = lax.all_to_all(dn, PLANE, 0, 0)
    d_input, gain_z = run(
        finish,
        [sds((16, 5120)), sds((8, 128), F32)],
        (gs, dn_parts.reshape(Q, T, 16, 1408), x, dy, gain),
        smem=1,
        nbytes=2 << 20,
    )
    pieces = lax.all_to_all(gain_z.reshape(Z, 1, 128), "z", 0, 0)
    own = (z * Q + lax.axis_index(QUARTER)) * T + lax.axis_index(HEADS)
    own_gain = lax.dynamic_slice_in_dim(gain, own * 20, 20).astype(F32)
    grad_gain = jnp.sum(pieces, axis=(0, 1))[:20] / own_gain

    gq, gk, gv, go = run(
        split,
        [sds((160, 384)), sds((160, 128)), sds((160, 128)), sds((160, 384))],
        (total,),
        grant=ALL,
        nbytes=2 << 20,
    )
    return d_input, gq, gk, gv, go.T, grad_gain


def solution(mesh):
    fine = Mesh(mesh.devices.reshape(8, 2, 2, 4, 2), ("z", "xh", "c", "y", "xl"))
    dp = ("z", "xh", "c")
    both = dp + HEADS
    return jax.shard_map(
        body,
        mesh=fine,
        in_specs=(
            P(both, None),
            P(both, None),
            P(),
            P(dp, HEADS),
            P(dp, HEADS),
            P(dp, HEADS),
            P(HEADS, dp),
            P(dp, None, HEADS),
            P(dp, None, HEADS),
            P(dp),
            P(dp),
        ),
        out_specs=(
            P(both, None),
            P(dp, HEADS),
            P(dp, HEADS),
            P(dp, HEADS),
            P(HEADS, dp),
            P(both),
        ),
        check_vma=False,
    )
```

time: 218 us -> 145 us (0.67)
  starting transfers between devices: 69.8 us -> 17.2 us
  local copies, waits for them, and re-layouts: 29.9 us -> 6.72 us
  blocking collectives: 45.9 us -> 25.7 us
  waiting for transfers between devices: 43.4 us -> 61.4 us
  between operations: 2.47 us -> 15.5 us
  other arithmetic: 10 us -> 1.05 us
    all_to_all x5 -> x2, waiting for transfers between devices: 4.75 us -> 42.8 us  [the longest x1 35.2 us: body(): tokens = lax.all_to_all(sent, PLANE, 0, 0).reshape(512, 2560)]
    ppermute x28 -> x5, starting transfers between devices: 39.7 us -> 3.29 us  [swap(): return lax.ppermute(a, axis, [(0, 1), (1, 0)])]
    ppermute x28 -> x5, waiting for transfers between devices: 38.7 us -> 18.6 us  [swap(): return lax.ppermute(a, axis, [(0, 1), (1, 0)])]
    all_gather x4 -> x0, blocking collectives: 19.9 us -> none  [gather4(): return lax.all_gather(lax.all_gather(a, 'xh'), 'c')]
    unnamed x107 -> x20, local copies, waits for them, and re-layouts: 25.4 us -> 6.72 us
    all_to_all x5 -> x2, starting transfers between devices: 30.1 us -> 13.8 us  [the longest x1 7.54 us: body(): tokens = lax.all_to_all(sent, PLANE, 0, 0).reshape(512, 2560)]
    convert_element_type x7 -> x0, other arithmetic: 4.35 us -> none  [the longest x6 4.26 us: add(): return (a.astype(F32) + b.astype(F32)).astype(BF16)]
    squeeze x2 -> x0, local copies, waits for them, and re-layouts: 2.37 us -> none  [ring_scatter(): back, ahead = (g[4], g[5])]
  transfers between devices with their start and end apart: 33 -> 9, of which waited for: 14 -> 6; matrix products, arithmetic and copies ran while one was open for 6% -> 1% of each run, Pallas kernels for 4% -> 4%
where the time goes in v2:
time: 145 us; the launch traced here: 143 us
  waiting for transfers between devices  61.4 us (42%)
  blocking collectives  25.7 us (18%)
  starting transfers between devices  17.2 us (12%)
  Pallas kernels  15.5 us (11%)
  between operations  15.5 us (11%)
  local copies, waits for them, and re-layouts  6.72 us (5%)
    all_to_all x1, waiting for transfers between devices, body(): tokens = lax.all_to_all(sent, PLANE, 0, 0).reshape(512, 2560)  35.2 us
    all_to_all x1, blocking collectives, body(): dn_parts = lax.all_to_all(dn, PLANE, 0, 0)  25.7 us
    ppermute x5, waiting for transfers between devices, swap(): return lax.ppermute(a, axis, [(0, 1), (1, 0)])  18.6 us
    pallas_call x9, Pallas kernels, run(): call(kernel, outs, [sds(a.shape, a.dtype) for a in args], **kw)(*args)  15.5 us
    all_to_all x1, waiting for transfers between devices, body(): pieces = lax.all_to_all(gain_z.reshape(Z, 1, 128), 'z', 0, 0)  7.6 us
    all_to_all x1, starting transfers between devices, body(): tokens = lax.all_to_all(sent, PLANE, 0, 0).reshape(512, 2560)  7.54 us
    unnamed x20, local copies, waits for them, and re-layouts  6.72 us
    all_to_all x1, starting transfers between devices, body(): pieces = lax.all_to_all(gain_z.reshape(Z, 1, 128), 'z', 0, 0)  6.24 us
  transfers between devices with their start and end apart: 9, of which 6 were waited for; matrix products, arithmetic and copies ran while one was open for 1% of the time, Pallas kernels for 4%

profile of v2, /device:TPU:8, one launch (start us, length us, event | category | flops | bytes accessed | tf_op | source)
XLA Modules:
  0.0 143.1 jit_solution(232531778622492691)
XLA Ops:
  7.2 0.0 all-gather.2.cloned.1.call-start
  7.2 1.8 %shard_map.154 = bf16[160,1024]{1,0:T(8,128)(2,1)} custom-call(bf16[160,384]{1,0:T(8,128)(2,1)} %wq.1, bf16[160,128]{1,0:T(8,128)(2,1)} %wk.1, bf16[160,128]{1,0:T(8,128)(2,1)} %wv.1, bf16[160,384]{1,0:T(8,128)(2,1)} %bitcast.18), custom_call_target="tpu_custom_call" | custom-call | bytes 1048576 | tf_op jit(solution)/shard_map/pallas_call | solution.py:51
  9.0 0.0 all-gather.2.cloned.1.call-update
  9.0 3.5 %shard_map.155 = bf16[32,16,2560]{2,1,0:T(8,128)(2,1)} custom-call(bf16[5120]{0:T(1024)(128)(2,1)} %gain.3, bf16[16,5120]{1,0:T(8,128)(2,1)} %x.1, bf16[16,5120]{1,0:T(8,128)(2,1)} %dy.1), custom_call_target="tpu_custom_call" | custom-call | bytes 3145728 | tf_op jit(solution)/shard_map/pallas_call | solution.py:51
  12.6 7.5 %all-to-all-start = ((bf16[32,16,2560]{2,1,0:T(8,128)(2,1)}), bf16[32,16,2560]{2,1,0:T(8,128)(2,1)S(1)}, u32[]{:S(2)}, u32[]{:S(2)}) async-start(bf16[32,16,2560]{2,1,0:T(8,128)(2,1)} %shard_map.155), calls=%async_computation | async-start | bytes 5242880 | tf_op jit(solution)/shard_map/all_to_all | solution.py:269
  20.1 0.0 reduce-scatter.2.cloned.1.call-start
  20.8 0.3 fusion
  21.2 0.1 pad_maximum_fusion
  21.3 35.2 %all-to-all-done = bf16[32,16,2560]{2,1,0:T(8,128)(2,1)S(1)} async-done(((bf16[32,16,2560]{2,1,0:T(8,128)(2,1)}), bf16[32,16,2560]{2,1,0:T(8,128)(2,1)S(1)}, u32[]{:S(2)}, u32[]{:S(2)}) %all-to-all-start) | async-done | bytes 2621472 | tf_op jit(solution)/shard_map/all_to_all | solution.py:269
  56.4 0.0 all-gather.2.cloned.1.call-done.w
  56.4 0.0 copy-start.1
  56.5 1.7 %copy-done.1 = bf16[1280,1024]{1,0:T(8,128)(2,1)S(1)} copy-done((bf16[1280,1024]{1,0:T(8,128)(2,1)S(1)}, bf16[1280,1024]{1,0:T(8,128)(2,1)}, u32[]{:S(2)}) %copy-start.1) | copy-done | bytes 2621464
  58.2 0.0 copy-start.7
  58.2 0.0 copy-start.8
  58.2 2.0 %shard_map.156 = (bf16[2,128,1024]{2,1,0:T(8,128)(2,1)S(1)}, bf16[2,128,1024]{2,1,0:T(8,128)(2,1)S(1)}) custom-call(s32[1]{0:T(128)} %bitcast.g_ref, bf16[512,2560]{1,0:T(8,128)(2,1)S(1)} %bitcast.12, bf16[1280,1024]{1,0:T(8,128)(2,1)S(1)} %copy-done.1), custom_call_target="tpu_custom_call" | custom-call | flops 1342177280 | bytes 7340032 | tf_op jit(solution)/shard_map/pallas_call | solution.py:51
  60.2 0.1 collective-permute-start
  60.3 1.9 %collective-permute-done.pair = bf16[2,128,1024]{2,1,0:T(8,128)(2,1)S(1)} collective-permute-done((bf16[2,128,1024]{2,1,0:T(8,128)(2,1)S(1)}, bf16[2,128,1024]{2,1,0:T(8,128)(2,1)S(1)}, u32[]{:S(2)}, u32[]{:S(2)}) %collective-permute-start) | collective-permute-done | bytes 524320 | tf_op jit(solution)/shard_map/ppermute | solution.py:237
  62.2 0.1 shard_map.157
  62.3 1.6 %collective-permute-start.1 = (bf16[128,1024]{1,0:T(8,128)(2,1)S(1)}, bf16[128,1024]{1,0:T(8,128)(2,1)S(1)}, u32[]{:S(2)}, u32[]{:S(2)}) collective-permute-start(bf16[128,1024]{1,0:T(8,128)(2,1)S(1)} %shard_map.157), channel_id=1, source_target_pairs={{0,16},{16,0},{1,17},{17,1},{2,18},{18,2},{3,19},{19,3},{4,20},{20... | collective-permute-start | bytes 786440 | tf_op jit(solution)/shard_map/ppermute | solution.py:237
  64.5 7.7 %collective-permute-done.1.far = bf16[128,1024]{1,0:T(8,128)(2,1)S(1)} collective-permute-done((bf16[128,1024]{1,0:T(8,128)(2,1)S(1)}, bf16[128,1024]{1,0:T(8,128)(2,1)S(1)}, u32[]{:S(2)}, u32[]{:S(2)}) %collective-permute-start.1) | collective-permute-done | bytes 262176 | tf_op jit(solution)/shard_map/ppermute | solution.py:237
  72.2 0.0 copy-done.7
  72.2 0.0 copy-done.8
  72.2 2.0 %shard_map.158.c0 = bf16[128,1024]{1,0:T(8,128)(2,1)S(1)} custom-call(s32[1]{0:T(128)S(6)} %copy.19.limit_ref, bf16[2,128,1024]{2,1,0:T(8,128)(2,1)S(1)} %get-tuple-element.24.keep.mine, bf16[2,128,1024]{2,1,0:T(8,128)(2,1)S(1)} %collective-permute-done.pair, bf16[128,1024]{1,0:T(8,128)(2,1)S(1)} %collective-permute-done.1.far, ...), custom_call_target="tpu_custom_call" | custom-call | flops 566231040 | bytes 4194304 | tf_op jit(solution)/shard_map/pallas_call | solution.py:51
  74.2 1.6 %collective-permute-start.3 = (bf16[128,1024]{1,0:T(8,128)(2,1)S(1)}, bf16[128,1024]{1,0:T(8,128)(2,1)S(1)}, u32[]{:S(2)}, u32[]{:S(2)}) collective-permute-start(bf16[128,1024]{1,0:T(8,128)(2,1)S(1)} %shard_map.158.c0), channel_id=1, source_target_pairs={{0,16},{16,0},{1,17},{17,1},{2,18},{18,2},{3,19},{19,3},{4,20},{20... | collective-permute-start | bytes 786440 | tf_op jit(solution)/shard_map/ppermute | solution.py:237
  75.8 0.0 collective-permute-start.2
  75.8 7.5 %collective-permute-done.3.c2 = bf16[128,1024]{1,0:T(8,128)(2,1)S(1)} collective-permute-done((bf16[128,1024]{1,0:T(8,128)(2,1)S(1)}, bf16[128,1024]{1,0:T(8,128)(2,1)S(1)}, u32[]{:S(2)}, u32[]{:S(2)}) %collective-permute-start.3) | collective-permute-done | bytes 262176 | tf_op jit(solution)/shard_map/ppermute | solution.py:237
  83.3 0.0 collective-permute-start.4
  83.3 0.0 collective-permute-done.2.c1
  83.3 1.5 %collective-permute-done.4.c3 = bf16[128,1024]{1,0:T(8,128)(2,1)S(1)} collective-permute-done((bf16[128,1024]{1,0:T(8,128)(2,1)S(1)}, bf16[128,1024]{1,0:T(8,128)(2,1)S(1)}, u32[]{:S(2)}, u32[]{:S(2)}) %collective-permute-start.4) | collective-permute-done | bytes 262176 | tf_op jit(solution)/shard_map/ppermute | solution.py:237
  84.9 2.0 %shard_map.159 = bf16[1280,1024]{1,0:T(8,128)(2,1)S(1)} custom-call(s32[1]{0:T(128)} %bitcast.g_ref, bf16[512,2560]{1,0:T(8,128)(2,1)S(1)} %bitcast.13, bf16[128,1024]{1,0:T(8,128)(2,1)S(1)} %shard_map.158.c0, bf16[128,1024]{1,0:T(8,128)(2,1)S(1)} %collective-permute-done.2.c1, bf16[128,1024]{1,0:T(8,128)(2,1)S(1)} %collective-permute-done.3.c2, ...), custom_call_target="tpu_custom_call" | custom-call | flops 1342177280 | bytes 8388608 | tf_op jit(solution)/shard_map/pallas_call | solution.py:51
  86.8 0.0 copy-start
  86.8 1.6 %copy-done = bf16[1280,1024]{1,0:T(8,128)(2,1)} copy-done((bf16[1280,1024]{1,0:T(8,128)(2,1)}, bf16[1280,1024]{1,0:T(8,128)(2,1)S(1)}, u32[]{:S(2)}) %copy-start) | copy-done | bytes 2621464
  88.4 0.0 copy-start.3
  88.4 0.7 copy-done.3
  89.1 0.0 reduce-scatter.2.cloned.1.call-update
  89.1 0.0 copy-start.2
  89.1 1.7 %copy-done.2 = bf16[1280,1024]{1,0:T(8,128)(2,1)S(1)} copy-done((bf16[1280,1024]{1,0:T(8,128)(2,1)S(1)}, bf16[1280,1024]{1,0:T(8,128)(2,1)}, u32[]{:S(2)}) %copy-start.2) | copy-done | bytes 2621464
  90.9 0.0 copy-start.4
  90.9 0.9 copy-done.4
  91.8 1.4 shard_map.160
  93.2 0.0 copy-start.5
  93.2 0.0 copy-start.6
  93.3 0.0 copy-start.9
  93.3 25.7 %all_to_all.15 = bf16[32,16,1408]{2,1,0:T(8,128)(2,1)S(1)} all-to-all(bf16[32,16,1408]{2,1,0:T(8,128)(2,1)S(1)} %shard_map.160), channel_id=1, replica_groups=mesh['z'=8,'xh'=2,'c'=2,'y'=4,'xl'=2] {'xh','c','y','xl'}, dimensions={0} | all-to-all | bytes 2883584 | tf_op jit(solution)/shard_map/all_to_all | solution.py:322
  119.0 0.0 copy-done.5
  119.0 0.0 copy-done.6
  119.0 0.0 copy-done.9
  119.0 1.1 shard_map.161
  120.1 6.2 %all-to-all-start.2 = ((f32[8,1,128]{2,1,0:T(1,128)}), f32[8,1,128]{2,1,0:T(1,128)S(1)}, u32[]{:S(2)}, u32[]{:S(2)}) async-start(f32[8,1,128]{2,1,0:T(1,128)} %bitcast.9), calls=%async_computation.3 | async-start | bytes 8192 | tf_op jit(solution)/shard_map/all_to_all | solution.py:330
  126.3 7.6 %all-to-all-done.2 = f32[8,1,128]{2,1,0:T(1,128)S(1)} async-done(((f32[8,1,128]{2,1,0:T(1,128)}), f32[8,1,128]{2,1,0:T(1,128)S(1)}, u32[]{:S(2)}, u32[]{:S(2)}) %all-to-all-start.2) | async-done | bytes 4128 | tf_op jit(solution)/shard_map/all_to_all | solution.py:330
  134.0 0.6 convert_divide_fusion
  134.5 0.0 reduce-scatter.2.cloned.1.call-done.total
  134.5 1.7 %shard_map.162 = (bf16[160,384]{1,0:T(8,128)(2,1)}, bf16[160,128]{1,0:T(8,128)(2,1)}, bf16[160,128]{1,0:T(8,128)(2,1)}, bf16[160,384]{1,0:T(8,128)(2,1)}) custom-call(bf16[160,1024]{1,0:T(8,128)(2,1)} %reduce-scatter.2.cloned.1.call-done.total), custom_call_target="tpu_custom_call" | custom-call | bytes 2097152 | tf_op jit(solution)/shard_map/pallas_call | solution.py:51
  (3 shorter events, 0.0 us)
Async XLA Ops:
  7.2 49.3 %all-gather.2.cloned.1.call-start = ((), (), s32[]{:S(2)}) async-start(), calls=%async_computation.4 | async-start | bytes 2949120 | tf_op jit(solution)/shard_map/all_gather | solution.py:253
  12.6 43.9 %all-to-all-start = ((bf16[32,16,2560]{2,1,0:T(8,128)(2,1)}), bf16[32,16,2560]{2,1,0:T(8,128)(2,1)S(1)}, u32[]{:S(2)}, u32[]{:S(2)}) async-start(bf16[32,16,2560]{2,1,0:T(8,128)(2,1)} %shard_map.155), calls=%async_computation | async-start | bytes 5242880 | tf_op jit(solution)/shard_map/all_to_all | solution.py:269
  20.1 114.4 %reduce-scatter.2.cloned.1.call-start = ((), (), s32[]{:S(2)}) async-start(), calls=%async_computation.5 | async-start | bytes 2949120 | tf_op jit(solution)/shard_map/reduce_scatter | solution.py:312
  56.4 1.7 %copy-start.1 = (bf16[1280,1024]{1,0:T(8,128)(2,1)S(1)}, bf16[1280,1024]{1,0:T(8,128)(2,1)}, u32[]{:S(2)}) copy-start(bf16[1280,1024]{1,0:T(8,128)(2,1)} %all-gather.2.cloned.1.call-done.w) | copy-start | bytes 7864324
  58.2 14.0 %copy-start.7 = (bf16[1,1024,128]{2,1,0:T(8,128)(2,1)S(1)}, bf16[1,1024,128]{2,1,0:T(8,128)(2,1)}, u32[]{:S(2)}) copy-start(bf16[1,1024,128]{2,1,0:T(8,128)(2,1)} %param.18) | copy-start | bytes 786436
  58.2 14.0 %copy-start.8 = (bf16[1,1024,128]{2,1,0:T(8,128)(2,1)S(1)}, bf16[1,1024,128]{2,1,0:T(8,128)(2,1)}, u32[]{:S(2)}) copy-start(bf16[1,1024,128]{2,1,0:T(8,128)(2,1)} %param.19) | copy-start | bytes 786436
  60.2 2.0 %collective-permute-start = (bf16[2,128,1024]{2,1,0:T(8,128)(2,1)S(1)}, bf16[2,128,1024]{2,1,0:T(8,128)(2,1)S(1)}, u32[]{:S(2)}, u32[]{:S(2)}) collective-permute-start(bf16[2,128,1024]{2,1,0:T(8,128)(2,1)S(1)} %get-tuple-element.25), channel_id=1, source_target_pairs={{0,8},{8,0},{1,9},{9,1},{2,10},{10,2},{3,11},{11,3},{4,12},{12,4},... | collective-permute-start | bytes 1572872 | tf_op jit(solution)/shard_map/ppermute | solution.py:237
  62.3 9.9 %collective-permute-start.1 = (bf16[128,1024]{1,0:T(8,128)(2,1)S(1)}, bf16[128,1024]{1,0:T(8,128)(2,1)S(1)}, u32[]{:S(2)}, u32[]{:S(2)}) collective-permute-start(bf16[128,1024]{1,0:T(8,128)(2,1)S(1)} %shard_map.157), channel_id=1, source_target_pairs={{0,16},{16,0},{1,17},{17,1},{2,18},{18,2},{3,19},{19,3},{4,20},{20... | collective-permute-start | bytes 786440 | tf_op jit(solution)/shard_map/ppermute | solution.py:237
  74.2 9.1 %collective-permute-start.3 = (bf16[128,1024]{1,0:T(8,128)(2,1)S(1)}, bf16[128,1024]{1,0:T(8,128)(2,1)S(1)}, u32[]{:S(2)}, u32[]{:S(2)}) collective-permute-start(bf16[128,1024]{1,0:T(8,128)(2,1)S(1)} %shard_map.158.c0), channel_id=1, source_target_pairs={{0,16},{16,0},{1,17},{17,1},{2,18},{18,2},{3,19},{19,3},{4,20},{20... | collective-permute-start | bytes 786440 | tf_op jit(solution)/shard_map/ppermute | solution.py:237
  75.8 7.5 %collective-permute-start.2 = (bf16[128,1024]{1,0:T(8,128)(2,1)S(1)}, bf16[128,1024]{1,0:T(8,128)(2,1)S(1)}, u32[]{:S(2)}, u32[]{:S(2)}) collective-permute-start(bf16[128,1024]{1,0:T(8,128)(2,1)S(1)} %shard_map.158.c0), channel_id=1, source_target_pairs={{0,8},{8,0},{1,9},{9,1},{2,10},{10,2},{3,11},{11,3},{4,12},{12,4},... | collective-permute-start | bytes 786440 | tf_op jit(solution)/shard_map/ppermute | solution.py:237
  83.3 1.5 %collective-permute-start.4 = (bf16[128,1024]{1,0:T(8,128)(2,1)S(1)}, bf16[128,1024]{1,0:T(8,128)(2,1)S(1)}, u32[]{:S(2)}, u32[]{:S(2)}) collective-permute-start(bf16[128,1024]{1,0:T(8,128)(2,1)S(1)} %collective-permute-done.3.c2), channel_id=1, source_target_pairs={{0,8},{8,0},{1,9},{9,1},{2,10},{10,2},{3,11},{11,3},{4,12},{12,4},... | collective-permute-start | bytes 786440 | tf_op jit(solution)/shard_map/ppermute | solution.py:237
  86.8 1.6 %copy-start = (bf16[1280,1024]{1,0:T(8,128)(2,1)}, bf16[1280,1024]{1,0:T(8,128)(2,1)S(1)}, u32[]{:S(2)}) copy-start(bf16[1280,1024]{1,0:T(8,128)(2,1)S(1)} %shard_map.159) | copy-start | bytes 7864324
  88.4 0.7 copy-start.3
  89.1 1.7 %copy-start.2 = (bf16[1280,1024]{1,0:T(8,128)(2,1)S(1)}, bf16[1280,1024]{1,0:T(8,128)(2,1)}, u32[]{:S(2)}) copy-start(bf16[1280,1024]{1,0:T(8,128)(2,1)} %all-gather.2.cloned.1.call-done.w) | copy-start | bytes 7864324
  90.9 0.9 copy-start.4
  93.2 25.7 %copy-start.5 = (bf16[16,5120]{1,0:T(8,128)(2,1)S(1)}, bf16[16,5120]{1,0:T(8,128)(2,1)}, u32[]{:S(2)}) copy-start(bf16[16,5120]{1,0:T(8,128)(2,1)} %x.1) | copy-start | bytes 491524
  93.2 25.7 %copy-start.6 = (bf16[16,5120]{1,0:T(8,128)(2,1)S(1)}, bf16[16,5120]{1,0:T(8,128)(2,1)}, u32[]{:S(2)}) copy-start(bf16[16,5120]{1,0:T(8,128)(2,1)} %dy.1) | copy-start | bytes 491524
  93.3 25.7 %copy-start.9 = (bf16[5120]{0:T(1024)(128)(2,1)S(1)}, bf16[5120]{0:T(1024)(128)(2,1)}, u32[]{:S(2)}) copy-start(bf16[5120]{0:T(1024)(128)(2,1)} %gain.3) | copy-start | bytes 30724
  120.1 13.8 %all-to-all-start.2 = ((f32[8,1,128]{2,1,0:T(1,128)}), f32[8,1,128]{2,1,0:T(1,128)S(1)}, u32[]{:S(2)}, u32[]{:S(2)}) async-start(f32[8,1,128]{2,1,0:T(1,128)} %bitcast.9), calls=%async_computation.3 | async-start | bytes 8192 | tf_op jit(solution)/shard_map/all_to_all | solution.py:330
Sparse Core Ops, SparseCore 0:
  9.8 45.2 all-gather.1
  89.2 43.2 reduce-scatter.1

commit v3 on v2

--- a/solution.py
+++ b/solution.py
@@ -21,6 +21,7 @@
 PLANE = ("xh", "c", "y", "xl")
 VMEM = 16 * 1024 * 1024
 ALL = 60 * 1024 * 1024
+LONG = 1 << 35
 F32 = jnp.float32
 BF16 = jnp.bfloat16
 
@@ -31,7 +32,8 @@
     near = len(shapes) - smem - far
     return pl.pallas_call(
         kernel,
-        out_shape=tuple(outs),
+        out_shape=tuple(outs[: len(outs) - far_out])
+        + tuple(pltpu.HBM(o.shape, o.dtype) for o in outs[len(outs) - far_out :]),
         in_specs=[pl.BlockSpec(memory_space=pltpu.SMEM)] * smem
         + [pl.BlockSpec()] * near
         + [pl.BlockSpec(memory_space=pltpu.HBM)] * far,
@@ -47,8 +49,13 @@
     return jax.ShapeDtypeStruct(shape, dtype)
 
 
-def run(kernel, outs, args, **kw):
-    return call(kernel, outs, [sds(a.shape, a.dtype) for a in args], **kw)(*args)
+def run(kernel, outs, args, far=0, **kw):
+    shapes = [sds(a.shape, a.dtype) for a in args]
+    near = len(args) - far
+    args = list(args[:near]) + [
+        pltpu.with_memory_space_constraint(a, pltpu.HBM) for a in args[near:]
+    ]
+    return call(kernel, outs, shapes, far=far, **kw)(*args)
 
 
 def dot(a, b, ca, cb):
@@ -62,11 +69,13 @@
     return made
 
 
-def join(wq, wk, wv, wo, out):
-    out[:, :384] = wq[...]
-    out[:, 384:512] = wk[...]
-    out[:, 512:640] = wv[...]
-    out[:, 640:] = wo[...]
+def join(wq, wk, wv, wo, out_far, out, sems):
+    parts = ((wq, 0, 384), (wk, 384, 512), (wv, 512, 640), (wo, 640, 1024))
+    for copy in copies_of([(src, out.at[:, a:b]) for src, a, b in parts], sems):
+        copy.wait()
+    copy = pltpu.make_async_copy(out, out_far, sems.at[4])
+    copy.start()
+    copy.wait()
 
 
 def split(total, q_out, k_out, v_out, o_out):
@@ -97,14 +106,21 @@
         copy.wait()
 
 
-def project(g_ref, tokens, w, keep, send, held):
-    for first, last, at in ((0, 384, 0), (384, 640, 0), (640, 1024, 1280)):
-        part = dot(tokens[:, at : at + 1280], w[:, first:last], 1, 0).astype(BF16)
-        for g in range(Q):
-            held[g_ref[0] ^ g, :, first:last] = part[128 * g : 128 * (g + 1), :]
+def project(g_ref, tokens, w_far, keep, send, w, total, sems):
+    halves = (slice(0, 640), slice(640, 1280))
+    parts = ((0, 384, 0), (384, 640, 0), (640, 1024, 1280))
+    copies = copies_of([(w_far.at[rows], w.at[rows]) for rows in halves], sems)
+    copies[0].wait()
+    for first, last, at in parts:
+        total[:, first:last] = dot(tokens[:, at : at + 640], w[halves[0], first:last], 1, 0)
+    copies[1].wait()
+    for first, last, at in parts:
+        part = dot(tokens[:, at + 640 : at + 1280], w[halves[1], first:last], 1, 0)
+        total[:, first:last] += part
     for xh in range(2):
-        keep[xh] = held[2 * xh]
-        send[xh] = held[2 * xh + 1]
+        for core, out in ((0, keep), (1, send)):
+            rows = pl.ds(pl.multiple_of((g_ref[0] ^ (2 * xh + core)) * 128, 128), 128)
+            out[xh] = total[rows, :].astype(BF16)
 
 
 def add(keep, pair, out):
@@ -176,25 +192,41 @@
         cot[rows, :] = block[:, : cot.shape[1]]
 
 
-def weight_grad(g_ref, tokens, c0, c1, c2, c3, out, cot):
+def weight_grad(g_ref, tokens, c0, c1, c2, c3, cot_out, grad_far, grad, cot, sems):
     gather_rows(g_ref, (c0, c1, c2, c3), cot)
+    cot_out[...] = cot[:, :640]
+    sent = []
     for r in range(5):
         cols = slice(256 * r, 256 * (r + 1))
         late = slice(1280 + 256 * r, 1280 + 256 * (r + 1))
-        out[cols, :640] = dot(tokens[:, cols], cot[:, :640], 0, 0).astype(BF16)
-        out[cols, 640:] = dot(tokens[:, late], cot[:, 640:], 0, 0).astype(BF16)
-
-
-def input_grad(g_ref, tokens, c0, c1, c2, c3, w, out, cot):
-    gather_rows(g_ref, (c0, c1, c2, c3), cot)
+        grad[cols, :640] = dot(tokens[:, cols], cot[:, :640], 0, 0).astype(BF16)
+        grad[cols, 640:] = dot(tokens[:, late], cot[:, 640:], 0, 0).astype(BF16)
+        copy = pltpu.make_async_copy(grad.at[cols], grad_far.at[cols], sems.at[r])
+        copy.start()
+        sent.append(copy)
+    for copy in sent:
+        copy.wait()
+
+
+def input_grad(tokens, cot, w_far, out_far, w, out, sems):
+    sent = []
+    copy_w, copy_w2 = copies_of(
+        [(w_far.at[:256, :640], w.at[:256]), (w_far.at[256:, :640], w.at[256:])], sems
+    )
+    copy_w.wait()
     sums = []
     for r in range(5):
         cols = slice(256 * r, 256 * (r + 1))
-        dn = dot(cot[...], w[cols, :640], 1, 1)
+        if r == 1:
+            copy_w2.wait()
+        dn = dot(cot[...], w[cols, :], 1, 1)
         sums.append(jnp.sum(dn * tokens[:, cols].astype(F32), axis=0, keepdims=True))
         dn = dn.astype(BF16)
         for b in range(Q * T):
             out[b, :, cols] = dn[16 * b : 16 * (b + 1), :]
+        copy = pltpu.make_async_copy(out.at[:, :, cols], out_far.at[:, :, cols], sems.at[6 + r])
+        copy.start()
+        sent.append(copy)
     total = jnp.concatenate(sums, axis=1)
     total = jnp.concatenate([total[:, 160 * z : 160 * (z + 1)] for z in range(Z)], axis=0)
     high = total.astype(BF16)
@@ -205,28 +237,39 @@
         tile = jnp.concatenate([both[:, 20 * t : 20 * (t + 1)], zero], axis=1)
         for q in range(Q):
             out[q * T + t, :, 1280:] = tile
-
-
-def finish(g_ref, parts, x, dy, gain, out, gain_out):
+    last = pltpu.make_async_copy(out.at[:, :, 1280:], out_far.at[:, :, 1280:], sems.at[11])
+    last.start()
+    for copy in sent + [last]:
+        copy.wait()
+
+
+def normalize(x, xhat, inv):
+    xf = x[...].astype(F32)
+    scale = lax.rsqrt(jnp.mean(xf * xf, axis=1, keepdims=True) + EPS)
+    xhat[...] = xf * scale
+    inv[...] = jnp.broadcast_to(scale, (16, 128))
+
+
+def gain_sum(g_ref, parts, gain_out):
+    tile = parts[g_ref[0], 0, :, 1280:].astype(F32)
+    for t in range(1, T):
+        tile = tile + parts[g_ref[0], t, :, 1280:].astype(F32)
+    gain_out[...] = tile[:8, :] + tile[8:, :]
+
+
+def finish(parts, xhat, inv, dy, gain, out):
     sums = []
     for q in range(Q):
         a = parts[q, 0, :, :1280].astype(F32)
         for t in range(1, T):
             a = a + parts[q, t, :, :1280].astype(F32)
         sums.append(a)
-    tile = parts[g_ref[0], 0, :, 1280:].astype(F32)
-    for t in range(1, T):
-        tile = tile + parts[g_ref[0], t, :, 1280:].astype(F32)
-    gain_out[...] = tile[:8, :] + tile[8:, :]
     dn = jnp.concatenate(
         [sums[q][:, 160 * z : 160 * (z + 1)] for z in range(Z) for q in range(Q)], axis=1
     )
-    xf = x[...].astype(F32)
-    inv = lax.rsqrt(jnp.mean(xf * xf, axis=1, keepdims=True) + EPS)
-    xhat = xf * inv
     scaled = dn * gain[...].reshape(1, -1).astype(F32)
-    mean = jnp.mean(scaled * xhat, axis=1, keepdims=True)
-    out[...] = (dy[...].astype(F32) + inv * (scaled - xhat * mean)).astype(BF16)
+    mean = jnp.mean(scaled * xhat[...], axis=1, keepdims=True)
+    out[...] = (dy[...].astype(F32) + inv[:, :1] * (scaled - xhat[...] * mean)).astype(BF16)
 
 
 def tie(*arrays):
@@ -246,7 +289,9 @@
         join,
         [sds((160, 1024))],
         (wq, wk, wv, wo.T),
-        grant=ALL,
+        far=4,
+        far_out=1,
+        scratch=[pltpu.VMEM((160, 1024), BF16), pltpu.SemaphoreType.DMA((5,))],
         nbytes=1 << 20,
     )
     x_in, w_own = tie(x, w_own)
@@ -281,7 +326,12 @@
         [sds((2, 128, 1024)), sds((2, 128, 1024))],
         (gs, tokens, w),
         smem=1,
-        scratch=[pltpu.VMEM((Q, 128, 1024), BF16)],
+        far=1,
+        scratch=[
+            pltpu.VMEM((1280, 1024), BF16),
+            pltpu.VMEM((512, 1024), F32),
+            pltpu.SemaphoreType.DMA((2,)),
+        ],
         flops=2 * 512 * 1280 * 1024,
         nbytes=7 << 20,
     )
@@ -299,32 +349,44 @@
     )
     across = swap(cot, "xh")
     cots = (cot, swap(cot, "c"), across, swap(across, "c"))
-    (grads,) = run(
+    cot4, grads = run(
         weight_grad,
-        [sds((1280, 1024))],
+        [sds((512, 640)), sds((1280, 1024))],
         (gs, tokens, *cots),
         smem=1,
-        scratch=[pltpu.VMEM((512, 1024), BF16)],
+        far_out=1,
+        scratch=[
+            pltpu.VMEM((1280, 1024), BF16),
+            pltpu.VMEM((512, 1024), BF16),
+            pltpu.SemaphoreType.DMA((5,)),
+        ],
         flops=2 * 512 * 1280 * 1024,
         nbytes=8 << 20,
     )
-    late, grads = tie(tokens, grads)
     total = lax.psum_scatter(grads, "z", scatter_dimension=0, tiled=True)
     (dn,) = run(
         input_grad,
         [sds((Q * T, 16, 1408))],
-        (gs, late, *cots, w),
-        smem=1,
-        scratch=[pltpu.VMEM((512, 640), BF16)],
+        (tokens, cot4, w),
+        far=1,
+        far_out=1,
+        scratch=[
+            pltpu.VMEM((1280, 640), BF16),
+            pltpu.VMEM((Q * T, 16, 1408), BF16),
+            pltpu.SemaphoreType.DMA((12,)),
+        ],
         flops=2 * 512 * 1280 * 640,
         nbytes=7 << 20,
     )
+    x_late, dn = tie(x, dn)
     dn_parts = lax.all_to_all(dn, PLANE, 0, 0)
-    d_input, gain_z = run(
+    xhat, inv = run(normalize, [sds((16, 5120), F32), sds((16, 128), F32)], (x_late,), flops=LONG)
+    dn_parts = dn_parts.reshape(Q, T, 16, 1408)
+    (gain_z,) = run(gain_sum, [sds((8, 128), F32)], (gs, dn_parts), smem=1)
+    (d_input,) = run(
         finish,
-        [sds((16, 5120)), sds((8, 128), F32)],
-        (gs, dn_parts.reshape(Q, T, 16, 1408), x, dy, gain),
-        smem=1,
+        [sds((16, 5120))],
+        (dn_parts, xhat, inv, dy, gain),
         nbytes=2 << 20,
     )
     pieces = lax.all_to_all(gain_z.reshape(Z, 1, 128), "z", 0, 0)

time: 145 us -> 142 us (0.979); the launches traced: 143 us -> 142 us
  blocking collectives: 25.7 us -> 0 us
  waiting for transfers between devices: 61.4 us -> 80 us
  starting transfers between devices: 17.2 us -> 23.4 us
  local copies, waits for them, and re-layouts: 6.72 us -> 0.76 us
  Pallas kernels: 15.5 us -> 20.9 us
    all_to_all x1 -> x0, blocking collectives: 25.7 us -> none  [body(): dn_parts = lax.all_to_all(dn, PLANE, 0, 0)]
    all_to_all x0 -> x1, waiting for transfers between devices: none -> 20.6 us  [body(): dn_parts = lax.all_to_all(dn, PLANE, 0, 0)]
    all_to_all x0 -> x1, starting transfers between devices: none -> 6.11 us  [body(): dn_parts = lax.all_to_all(dn, PLANE, 0, 0)]
    unnamed x20 -> x10, local copies, waits for them, and re-layouts: 6.72 us -> 0.76 us
    pallas_call x9 -> x11, Pallas kernels: 15.5 us -> 20.9 us  [run(): return call(kernel, outs, shapes, far=far, **kw)(*args)]
    all_to_all x1, waiting for transfers between devices: 7.6 us -> 5.61 us  [body(): pieces = lax.all_to_all(gain_z.reshape(Z, 1, 128), 'z', 0, 0)]
  transfers between devices with their start and end apart: 9 -> 10, of which waited for: 6 -> 7; matrix products, arithmetic and copies ran while one was open for 1% -> 1% of each run, Pallas kernels for 4% -> 6%
where the time goes in v3:
time: 142 us
  waiting for transfers between devices  80 us (56%)
  starting transfers between devices  23.4 us (16%)
  Pallas kernels  20.9 us (15%)
  between operations  15.5 us (11%)
    all_to_all x1, waiting for transfers between devices, body(): tokens = lax.all_to_all(sent, PLANE, 0, 0).reshape(512, 2560)  35.2 us
    pallas_call x11, Pallas kernels, run(): return call(kernel, outs, shapes, far=far, **kw)(*args)  20.9 us
    all_to_all x1, waiting for transfers between devices, body(): dn_parts = lax.all_to_all(dn, PLANE, 0, 0)  20.6 us
    ppermute x5, waiting for transfers between devices, swap(): return lax.ppermute(a, axis, [(0, 1), (1, 0)])  18.6 us
    all_to_all x1, starting transfers between devices, body(): tokens = lax.all_to_all(sent, PLANE, 0, 0).reshape(512, 2560)  7.54 us
    all_to_all x1, starting transfers between devices, body(): pieces = lax.all_to_all(gain_z.reshape(Z, 1, 128), 'z', 0, 0)  6.31 us
    all_to_all x1, starting transfers between devices, body(): dn_parts = lax.all_to_all(dn, PLANE, 0, 0)  6.11 us
    all_to_all x1, waiting for transfers between devices, body(): pieces = lax.all_to_all(gain_z.reshape(Z, 1, 128), 'z', 0, 0)  5.61 us
  transfers between devices with their start and end apart: 10, of which 7 were waited for; matrix products, arithmetic and copies ran while one was open for 1% of the time, Pallas kernels for 6%

profile of v3, /device:TPU:8, one launch (start us, length us, event | category | flops | bytes accessed | tf_op | source)
XLA Modules:
  0.0 141.6 jit_solution(3877049273155533058)
XLA Ops:
  7.2 0.0 all-gather.2.cloned.1.call-start
  7.2 1.8 %shard_map.154 = bf16[160,1024]{1,0:T(8,128)(2,1)} custom-call(bf16[160,384]{1,0:T(8,128)(2,1)} %wq.1, bf16[160,128]{1,0:T(8,128)(2,1)} %wk.1, bf16[160,128]{1,0:T(8,128)(2,1)} %wv.1, bf16[160,384]{1,0:T(8,128)(2,1)} %bitcast.19), custom_call_target="tpu_custom_call" | custom-call | bytes 1048576 | tf_op jit(solution)/shard_map/pallas_call | solution.py:58
  9.0 0.0 all-gather.2.cloned.1.call-update
  9.0 3.5 %shard_map.155 = bf16[32,16,2560]{2,1,0:T(8,128)(2,1)} custom-call(bf16[5120]{0:T(1024)(128)(2,1)} %gain.3, bf16[16,5120]{1,0:T(8,128)(2,1)} %x, bf16[16,5120]{1,0:T(8,128)(2,1)} %dy.1), custom_call_target="tpu_custom_call" | custom-call | bytes 3145728 | tf_op jit(solution)/shard_map/pallas_call | solution.py:58
  12.5 7.5 %all-to-all-start = ((bf16[32,16,2560]{2,1,0:T(8,128)(2,1)}), bf16[32,16,2560]{2,1,0:T(8,128)(2,1)S(1)}, u32[]{:S(2)}, u32[]{:S(2)}) async-start(bf16[32,16,2560]{2,1,0:T(8,128)(2,1)} %shard_map.155), calls=%async_computation | async-start | bytes 5242880 | tf_op jit(solution)/shard_map/all_to_all | solution.py:314
  20.1 0.0 reduce-scatter.2.cloned.1.call-start
  20.8 0.3 fusion
  21.1 0.1 pad_maximum_fusion
  21.2 35.2 %all-to-all-done = bf16[32,16,2560]{2,1,0:T(8,128)(2,1)S(1)} async-done(((bf16[32,16,2560]{2,1,0:T(8,128)(2,1)}), bf16[32,16,2560]{2,1,0:T(8,128)(2,1)S(1)}, u32[]{:S(2)}, u32[]{:S(2)}) %all-to-all-start) | async-done | bytes 2621472 | tf_op jit(solution)/shard_map/all_to_all | solution.py:314
  56.4 0.0 all-gather.2.cloned.1.call-done.w_far
  56.4 0.0 copy-start.1
  56.4 0.0 copy-start.2
  56.4 3.7 %shard_map.156 = (bf16[2,128,1024]{2,1,0:T(8,128)(2,1)S(1)}, bf16[2,128,1024]{2,1,0:T(8,128)(2,1)S(1)}) custom-call(s32[1]{0:T(128)} %bitcast.3.g_ref, bf16[512,2560]{1,0:T(8,128)(2,1)S(1)} %bitcast.12, bf16[1280,1024]{1,0:T(8,128)(2,1)} %all-gather.2.cloned.1.call-done.w_far), custom_call_target="tpu_custom_call" | custom-call | flops 1342177280 | bytes 7340032 | tf_op jit(solution)/shard_map/pallas_call | solution.py:58
  60.2 0.1 collective-permute-start
  60.3 1.9 %collective-permute-done.pair = bf16[2,128,1024]{2,1,0:T(8,128)(2,1)S(1)} collective-permute-done((bf16[2,128,1024]{2,1,0:T(8,128)(2,1)S(1)}, bf16[2,128,1024]{2,1,0:T(8,128)(2,1)S(1)}, u32[]{:S(2)}, u32[]{:S(2)}) %collective-permute-start) | collective-permute-done | bytes 524320 | tf_op jit(solution)/shard_map/ppermute | solution.py:280
  62.2 0.1 shard_map.157
  62.2 1.6 %collective-permute-start.1 = (bf16[128,1024]{1,0:T(8,128)(2,1)S(1)}, bf16[128,1024]{1,0:T(8,128)(2,1)S(1)}, u32[]{:S(2)}, u32[]{:S(2)}) collective-permute-start(bf16[128,1024]{1,0:T(8,128)(2,1)S(1)} %shard_map.157), channel_id=1, source_target_pairs={{0,16},{16,0},{1,17},{17,1},{2,18},{18,2},{3,19},{19,3},{4,20},{20... | collective-permute-start | bytes 786440 | tf_op jit(solution)/shard_map/ppermute | solution.py:280
  64.5 7.7 %collective-permute-done.1.far = bf16[128,1024]{1,0:T(8,128)(2,1)S(1)} collective-permute-done((bf16[128,1024]{1,0:T(8,128)(2,1)S(1)}, bf16[128,1024]{1,0:T(8,128)(2,1)S(1)}, u32[]{:S(2)}, u32[]{:S(2)}) %collective-permute-start.1) | collective-permute-done | bytes 262176 | tf_op jit(solution)/shard_map/ppermute | solution.py:280
  72.2 0.0 copy-done.1
  72.2 0.0 copy-done.2
  72.2 2.0 %shard_map.158.c0 = bf16[128,1024]{1,0:T(8,128)(2,1)S(1)} custom-call(s32[1]{0:T(128)S(6)} %copy.19.limit_ref, bf16[2,128,1024]{2,1,0:T(8,128)(2,1)S(1)} %get-tuple-element.26.keep.mine, bf16[2,128,1024]{2,1,0:T(8,128)(2,1)S(1)} %collective-permute-done.pair, bf16[128,1024]{1,0:T(8,128)(2,1)S(1)} %collective-permute-done.1.far, ...), custom_call_target="tpu_custom_call" | custom-call | flops 566231040 | bytes 4194304 | tf_op jit(solution)/shard_map/pallas_call | solution.py:58
  74.2 1.6 %collective-permute-start.3 = (bf16[128,1024]{1,0:T(8,128)(2,1)S(1)}, bf16[128,1024]{1,0:T(8,128)(2,1)S(1)}, u32[]{:S(2)}, u32[]{:S(2)}) collective-permute-start(bf16[128,1024]{1,0:T(8,128)(2,1)S(1)} %shard_map.158.c0), channel_id=1, source_target_pairs={{0,16},{16,0},{1,17},{17,1},{2,18},{18,2},{3,19},{19,3},{4,20},{20... | collective-permute-start | bytes 786440 | tf_op jit(solution)/shard_map/ppermute | solution.py:280
  75.8 0.0 collective-permute-start.2
  75.8 7.5 %collective-permute-done.3.c2 = bf16[128,1024]{1,0:T(8,128)(2,1)S(1)} collective-permute-done((bf16[128,1024]{1,0:T(8,128)(2,1)S(1)}, bf16[128,1024]{1,0:T(8,128)(2,1)S(1)}, u32[]{:S(2)}, u32[]{:S(2)}) %collective-permute-start.3) | collective-permute-done | bytes 262176 | tf_op jit(solution)/shard_map/ppermute | solution.py:280
  83.3 0.0 collective-permute-start.4
  83.3 0.0 collective-permute-done.2.c1
  83.3 1.5 %collective-permute-done.4.c3 = bf16[128,1024]{1,0:T(8,128)(2,1)S(1)} collective-permute-done((bf16[128,1024]{1,0:T(8,128)(2,1)S(1)}, bf16[128,1024]{1,0:T(8,128)(2,1)S(1)}, u32[]{:S(2)}, u32[]{:S(2)}) %collective-permute-start.4) | collective-permute-done | bytes 262176 | tf_op jit(solution)/shard_map/ppermute | solution.py:280
  84.8 2.8 %shard_map.159 = (bf16[512,640]{1,0:T(8,128)(2,1)S(1)}, bf16[1280,1024]{1,0:T(8,128)(2,1)}) custom-call(s32[1]{0:T(128)} %bitcast.3.g_ref, bf16[512,2560]{1,0:T(8,128)(2,1)S(1)} %bitcast.13, bf16[128,1024]{1,0:T(8,128)(2,1)S(1)} %shard_map.158.c0, bf16[128,1024]{1,0:T(8,128)(2,1)S(1)} %collective-permute-done.2.c1, ...), custom_call_target="tpu_custom_call" | custom-call | flops 1342177280 | bytes 8388608 | tf_op jit(solution)/shard_map/pallas_call | solution.py:58
  87.7 0.0 reduce-scatter.2.cloned.1.call-update
  87.7 3.5 %shard_map.160 = bf16[32,16,1408]{2,1,0:T(8,128)(2,1)} custom-call(bf16[512,2560]{1,0:T(8,128)(2,1)S(1)} %bitcast.14, bf16[512,640]{1,0:T(8,128)(2,1)S(1)} %get-tuple-element.30.cot, bf16[1280,1024]{1,0:T(8,128)(2,1)} %all-gather.2.cloned.1.call-done.w_far), custom_call_target="tpu_custom_call" | custom-call | flops 838860800 | bytes 7340032 | tf_op jit(solution)/shard_map/pallas_call | solution.py:58
  91.2 0.0 copy-start.3
  91.2 6.1 %all-to-all-start.1 = ((bf16[32,16,1408]{2,1,0:T(8,128)(2,1)}), bf16[32,16,1408]{2,1,0:T(8,128)(2,1)S(1)}, u32[]{:S(2)}, u32[]{:S(2)}) async-start(bf16[32,16,1408]{2,1,0:T(8,128)(2,1)} %shard_map.160), calls=%async_computation.1 | async-start | bytes 2883584 | tf_op jit(solution)/shard_map/all_to_all | solution.py:382
  97.3 20.6 %all-to-all-done.1 = bf16[32,16,1408]{2,1,0:T(8,128)(2,1)S(1)} async-done(((bf16[32,16,1408]{2,1,0:T(8,128)(2,1)}), bf16[32,16,1408]{2,1,0:T(8,128)(2,1)S(1)}, u32[]{:S(2)}, u32[]{:S(2)}) %all-to-all-start.1) | async-done | bytes 1441824 | tf_op jit(solution)/shard_map/all_to_all | solution.py:382
  118.0 0.6 shard_map.164
  118.6 6.3 %all-to-all-start.2 = ((f32[8,1,128]{2,1,0:T(1,128)}), f32[8,1,128]{2,1,0:T(1,128)S(1)}, u32[]{:S(2)}, u32[]{:S(2)}) async-start(f32[8,1,128]{2,1,0:T(1,128)} %bitcast.9), calls=%async_computation.3 | async-start | bytes 8192 | tf_op jit(solution)/shard_map/all_to_all | solution.py:392
  124.9 0.0 copy-done.3
  124.9 0.0 copy-start
  124.9 0.0 copy-start.4
  124.9 0.1 shard_map.161
  125.1 0.7 copy-done
  125.8 0.0 copy-done.4
  125.8 1.1 shard_map.162
  126.9 5.6 %all-to-all-done.2 = f32[8,1,128]{2,1,0:T(1,128)S(1)} async-done(((f32[8,1,128]{2,1,0:T(1,128)}), f32[8,1,128]{2,1,0:T(1,128)S(1)}, u32[]{:S(2)}, u32[]{:S(2)}) %all-to-all-start.2) | async-done | bytes 4128 | tf_op jit(solution)/shard_map/all_to_all | solution.py:392
  132.5 0.6 convert_divide_fusion
  133.1 0.0 reduce-scatter.2.cloned.1.call-done.total
  133.1 1.7 %shard_map.163 = (bf16[160,384]{1,0:T(8,128)(2,1)}, bf16[160,128]{1,0:T(8,128)(2,1)}, bf16[160,128]{1,0:T(8,128)(2,1)}, bf16[160,384]{1,0:T(8,128)(2,1)}) custom-call(bf16[160,1024]{1,0:T(8,128)(2,1)} %reduce-scatter.2.cloned.1.call-done.total), custom_call_target="tpu_custom_call" | custom-call | bytes 2097152 | tf_op jit(solution)/shard_map/pallas_call | solution.py:58
  (3 shorter events, 0.0 us)
Async XLA Ops:
  7.2 49.3 %all-gather.2.cloned.1.call-start = ((), (), s32[]{:S(2)}) async-start(), calls=%async_computation.4 | async-start | bytes 2949120 | tf_op jit(solution)/shard_map/all_gather | solution.py:298
  12.5 43.9 %all-to-all-start = ((bf16[32,16,2560]{2,1,0:T(8,128)(2,1)}), bf16[32,16,2560]{2,1,0:T(8,128)(2,1)S(1)}, u32[]{:S(2)}, u32[]{:S(2)}) async-start(bf16[32,16,2560]{2,1,0:T(8,128)(2,1)} %shard_map.155), calls=%async_computation | async-start | bytes 5242880 | tf_op jit(solution)/shard_map/all_to_all | solution.py:314
  20.1 113.0 %reduce-scatter.2.cloned.1.call-start = ((), (), s32[]{:S(2)}) async-start(), calls=%async_computation.5 | async-start | bytes 2949120 | tf_op jit(solution)/shard_map/reduce_scatter | solution.py:366
  56.4 15.8 %copy-start.1 = (bf16[1,1024,128]{2,1,0:T(8,128)(2,1)S(1)}, bf16[1,1024,128]{2,1,0:T(8,128)(2,1)}, u32[]{:S(2)}) copy-start(bf16[1,1024,128]{2,1,0:T(8,128)(2,1)} %param.18) | copy-start | bytes 786436
  56.4 15.8 %copy-start.2 = (bf16[1,1024,128]{2,1,0:T(8,128)(2,1)S(1)}, bf16[1,1024,128]{2,1,0:T(8,128)(2,1)}, u32[]{:S(2)}) copy-start(bf16[1,1024,128]{2,1,0:T(8,128)(2,1)} %param.19) | copy-start | bytes 786436
  60.2 2.0 %collective-permute-start = (bf16[2,128,1024]{2,1,0:T(8,128)(2,1)S(1)}, bf16[2,128,1024]{2,1,0:T(8,128)(2,1)S(1)}, u32[]{:S(2)}, u32[]{:S(2)}) collective-permute-start(bf16[2,128,1024]{2,1,0:T(8,128)(2,1)S(1)} %get-tuple-element.27), channel_id=1, source_target_pairs={{0,8},{8,0},{1,9},{9,1},{2,10},{10,2},{3,11},{11,3},{4,12},{12,4},... | collective-permute-start | bytes 1572872 | tf_op jit(solution)/shard_map/ppermute | solution.py:280
  62.2 9.9 %collective-permute-start.1 = (bf16[128,1024]{1,0:T(8,128)(2,1)S(1)}, bf16[128,1024]{1,0:T(8,128)(2,1)S(1)}, u32[]{:S(2)}, u32[]{:S(2)}) collective-permute-start(bf16[128,1024]{1,0:T(8,128)(2,1)S(1)} %shard_map.157), channel_id=1, source_target_pairs={{0,16},{16,0},{1,17},{17,1},{2,18},{18,2},{3,19},{19,3},{4,20},{20... | collective-permute-start | bytes 786440 | tf_op jit(solution)/shard_map/ppermute | solution.py:280
  74.2 9.1 %collective-permute-start.3 = (bf16[128,1024]{1,0:T(8,128)(2,1)S(1)}, bf16[128,1024]{1,0:T(8,128)(2,1)S(1)}, u32[]{:S(2)}, u32[]{:S(2)}) collective-permute-start(bf16[128,1024]{1,0:T(8,128)(2,1)S(1)} %shard_map.158.c0), channel_id=1, source_target_pairs={{0,16},{16,0},{1,17},{17,1},{2,18},{18,2},{3,19},{19,3},{4,20},{20... | collective-permute-start | bytes 786440 | tf_op jit(solution)/shard_map/ppermute | solution.py:280
  75.8 7.5 %collective-permute-start.2 = (bf16[128,1024]{1,0:T(8,128)(2,1)S(1)}, bf16[128,1024]{1,0:T(8,128)(2,1)S(1)}, u32[]{:S(2)}, u32[]{:S(2)}) collective-permute-start(bf16[128,1024]{1,0:T(8,128)(2,1)S(1)} %shard_map.158.c0), channel_id=1, source_target_pairs={{0,8},{8,0},{1,9},{9,1},{2,10},{10,2},{3,11},{11,3},{4,12},{12,4},... | collective-permute-start | bytes 786440 | tf_op jit(solution)/shard_map/ppermute | solution.py:280
  83.3 1.5 %collective-permute-start.4 = (bf16[128,1024]{1,0:T(8,128)(2,1)S(1)}, bf16[128,1024]{1,0:T(8,128)(2,1)S(1)}, u32[]{:S(2)}, u32[]{:S(2)}) collective-permute-start(bf16[128,1024]{1,0:T(8,128)(2,1)S(1)} %collective-permute-done.3.c2), channel_id=1, source_target_pairs={{0,8},{8,0},{1,9},{9,1},{2,10},{10,2},{3,11},{11,3},{4,12},{12,4},... | collective-permute-start | bytes 786440 | tf_op jit(solution)/shard_map/ppermute | solution.py:280
  91.2 33.7 %copy-start.3 = (bf16[16,5120]{1,0:T(8,128)(2,1)S(1)}, bf16[16,5120]{1,0:T(8,128)(2,1)}, u32[]{:S(2)}) copy-start(bf16[16,5120]{1,0:T(8,128)(2,1)} %x) | copy-start | bytes 491524
  91.2 26.7 %all-to-all-start.1 = ((bf16[32,16,1408]{2,1,0:T(8,128)(2,1)}), bf16[32,16,1408]{2,1,0:T(8,128)(2,1)S(1)}, u32[]{:S(2)}, u32[]{:S(2)}) async-start(bf16[32,16,1408]{2,1,0:T(8,128)(2,1)} %shard_map.160), calls=%async_computation.1 | async-start | bytes 2883584 | tf_op jit(solution)/shard_map/all_to_all | solution.py:382
  118.6 13.9 %all-to-all-start.2 = ((f32[8,1,128]{2,1,0:T(1,128)}), f32[8,1,128]{2,1,0:T(1,128)S(1)}, u32[]{:S(2)}, u32[]{:S(2)}) async-start(f32[8,1,128]{2,1,0:T(1,128)} %bitcast.9), calls=%async_computation.3 | async-start | bytes 8192 | tf_op jit(solution)/shard_map/all_to_all | solution.py:392
  124.9 0.9 copy-start
  124.9 0.9 copy-start.4
Sparse Core Ops, SparseCore 0:
  9.8 45.1 all-gather.1
  87.8 43.3 reduce-scatter.1

commit v4 on v3

--- a/solution.py
+++ b/solution.py
@@ -20,7 +20,6 @@
 HEADS = ("y", "xl")
 PLANE = ("xh", "c", "y", "xl")
 VMEM = 16 * 1024 * 1024
-ALL = 60 * 1024 * 1024
 LONG = 1 << 35
 F32 = jnp.float32
 BF16 = jnp.bfloat16
@@ -69,29 +68,38 @@
     return made
 
 
-def join(wq, wk, wv, wo, out_far, out, sems):
+def join(wq, wk, wv, wo, x_far, dy_far, gain_far, n_out, dy_out, w_far, w, x, gain, sems):
     parts = ((wq, 0, 384), (wk, 384, 512), (wv, 512, 640), (wo, 640, 1024))
-    for copy in copies_of([(src, out.at[:, a:b]) for src, a, b in parts], sems):
+    pairs = [(src, w.at[:, a:b]) for src, a, b in parts]
+    pairs += [(gain_far, gain), (x_far, x), (dy_far, dy_out)]
+    copies = copies_of(pairs, sems)
+    for copy in copies[:4]:
         copy.wait()
-    copy = pltpu.make_async_copy(out, out_far, sems.at[4])
-    copy.start()
-    copy.wait()
-
-
-def split(total, q_out, k_out, v_out, o_out):
-    q_out[...] = total[:, :384]
-    k_out[...] = total[:, 384:512]
-    v_out[...] = total[:, 512:640]
-    o_out[...] = total[:, 640:]
-
-
-def prep_tokens(gain, x_far, dy_far, out_far, x, dy, out, sems):
-    copy_x, copy_dy = copies_of([(x_far, x), (dy_far, dy)], sems)
-    copy_x.wait()
+    out_copy = pltpu.make_async_copy(w, w_far, sems.at[7])
+    out_copy.start()
+    copies[4].wait()
+    copies[5].wait()
     xf = x[...].astype(F32)
     inv = lax.rsqrt(jnp.mean(xf * xf, axis=1, keepdims=True) + EPS)
-    n = (xf * inv * gain[...].reshape(1, -1).astype(F32)).astype(BF16)
-    copy_dy.wait()
+    n_out[...] = (xf * inv * gain[...].reshape(1, -1).astype(F32)).astype(BF16)
+    copies[6].wait()
+    out_copy.wait()
+
+
+def split(total, q_out, k_out, v_out, o_out, q, k, v, o, sems):
+    parts = ((q, q_out, 0, 384), (k, k_out, 384, 512), (v, v_out, 512, 640), (o, o_out, 640, 1024))
+    copies = copies_of([(total.at[:, a:b], part) for part, _, a, b in parts], sems)
+    sent = []
+    for i, (part, dst, _, _) in enumerate(parts):
+        copies[i].wait()
+        copy = pltpu.make_async_copy(part, dst, sems.at[4 + i])
+        copy.start()
+        sent.append(copy)
+    for copy in sent:
+        copy.wait()
+
+
+def lay_out(n, dy, out_far, out, sems):
     sent = []
     for q in range(Q):
         cols = [slice((Q * z + q) * 160, (Q * z + q + 1) * 160) for z in range(Z)]
@@ -99,7 +107,7 @@
         for t in range(T):
             out[q * T + t] = row
         part = pl.ds(q * T, T)
-        copy = pltpu.make_async_copy(out.at[part], out_far.at[part], sems.at[2 + q])
+        copy = pltpu.make_async_copy(out.at[part], out_far.at[part], sems.at[q])
         copy.start()
         sent.append(copy)
     for copy in sent:
@@ -210,15 +218,13 @@
 
 def input_grad(tokens, cot, w_far, out_far, w, out, sems):
     sent = []
-    copy_w, copy_w2 = copies_of(
-        [(w_far.at[:256, :640], w.at[:256]), (w_far.at[256:, :640], w.at[256:])], sems
-    )
-    copy_w.wait()
+    halves = (slice(0, 256), slice(256, 1280))
+    copies = copies_of([(w_far.at[rows, :640], w.at[rows]) for rows in halves], sems)
     sums = []
     for r in range(5):
         cols = slice(256 * r, 256 * (r + 1))
-        if r == 1:
-            copy_w2.wait()
+        if r < 2:
+            copies[r].wait()
         dn = dot(cot[...], w[cols, :], 1, 1)
         sums.append(jnp.sum(dn * tokens[:, cols].astype(F32), axis=0, keepdims=True))
         dn = dn.astype(BF16)
@@ -285,30 +291,27 @@
     gs = lax.axis_index(QUARTER).astype(jnp.int32).reshape(1)
     kc, vc = kc.reshape(1024, HD), vc.reshape(1024, HD)
 
-    (w_own,) = run(
+    n_own, dy_own, w_own = run(
         join,
-        [sds((160, 1024))],
-        (wq, wk, wv, wo.T),
-        far=4,
+        [sds((16, 5120)), sds((16, 5120)), sds((160, 1024))],
+        (wq, wk, wv, wo.T, x, dy, gain),
+        far=7,
         far_out=1,
-        scratch=[pltpu.VMEM((160, 1024), BF16), pltpu.SemaphoreType.DMA((5,))],
+        scratch=[
+            pltpu.VMEM((160, 1024), BF16),
+            pltpu.VMEM((16, 5120), BF16),
+            pltpu.VMEM((5120,), BF16),
+            pltpu.SemaphoreType.DMA((8,)),
+        ],
         nbytes=1 << 20,
     )
-    x_in, w_own = tie(x, w_own)
     w = lax.all_gather(w_own, "z", axis=0, tiled=True)
     (sent,) = run(
-        prep_tokens,
+        lay_out,
         [sds((Q * T, 16, 2560))],
-        (gain, x_in, dy),
-        far=2,
+        (n_own, dy_own),
         far_out=1,
-        scratch=[
-            pltpu.VMEM((16, 5120), BF16),
-            pltpu.VMEM((16, 5120), BF16),
-            pltpu.VMEM((Q * T, 16, 2560), BF16),
-            pltpu.SemaphoreType.DMA((2 + Q,)),
-        ],
-        grant=ALL,
+        scratch=[pltpu.VMEM((Q * T, 16, 2560), BF16), pltpu.SemaphoreType.DMA((Q,))],
         nbytes=3 << 20,
     )
     tokens = lax.all_to_all(sent, PLANE, 0, 0).reshape(512, 2560)
@@ -390,17 +393,26 @@
         nbytes=2 << 20,
     )
     pieces = lax.all_to_all(gain_z.reshape(Z, 1, 128), "z", 0, 0)
-    own = (z * Q + lax.axis_index(QUARTER)) * T + lax.axis_index(HEADS)
-    own_gain = lax.dynamic_slice_in_dim(gain, own * 20, 20).astype(F32)
-    grad_gain = jnp.sum(pieces, axis=(0, 1))[:20] / own_gain
-
     gq, gk, gv, go = run(
         split,
         [sds((160, 384)), sds((160, 128)), sds((160, 128)), sds((160, 384))],
         (total,),
-        grant=ALL,
+        far=1,
+        far_out=4,
+        scratch=[
+            pltpu.VMEM((160, 384), BF16),
+            pltpu.VMEM((160, 128), BF16),
+            pltpu.VMEM((160, 128), BF16),
+            pltpu.VMEM((160, 384), BF16),
+            pltpu.SemaphoreType.DMA((8,)),
+        ],
         nbytes=2 << 20,
     )
+    pieces, gq = tie(pieces, gq)
+    own = (z * Q + lax.axis_index(QUARTER)) * T + lax.axis_index(HEADS)
+    own_gain = lax.dynamic_slice_in_dim(gain, own * 20, 20).astype(F32)
+    grad_gain = jnp.sum(pieces, axis=(0, 1))[:20] / own_gain
+
     return d_input, gq, gk, gv, go.T, grad_gain
 
 

time: 142 us -> 139 us (0.979)
  waiting for transfers between devices: 80 us -> 76.2 us
  starting transfers between devices: 23.4 us -> 25.9 us
  Pallas kernels: 20.9 us -> 19.1 us
    all_to_all x1, waiting for transfers between devices: 5.61 us -> 0.01 us  [body(): pieces = lax.all_to_all(gain_z.reshape(Z, 1, 128), 'z', 0, 0)]
    reduce_scatter x1, waiting for transfers between devices: 0.01 us -> 4.26 us  [body(): total = lax.psum_scatter(grads, 'z', scatter_dimension=0, tiled=True)]
    ppermute x5, starting transfers between devices: 3.36 us -> 6.21 us  [swap(): return lax.ppermute(a, axis, [(0, 1), (1, 0)])]
    ppermute x5, waiting for transfers between devices: 18.6 us -> 15.7 us  [swap(): return lax.ppermute(a, axis, [(0, 1), (1, 0)])]
    pallas_call x11, Pallas kernels: 20.9 us -> 19.1 us  [run(): return call(kernel, outs, shapes, far=far, **kw)(*args)]
    all_to_all x1, starting transfers between devices: 6.31 us -> 4.51 us  [body(): pieces = lax.all_to_all(gain_z.reshape(Z, 1, 128), 'z', 0, 0)]
    all_to_all x1, starting transfers between devices: 6.11 us -> 7.55 us  [body(): dn_parts = lax.all_to_all(dn, PLANE, 0, 0)]
  transfers between devices with their start and end apart: 10 -> 10, of which waited for: 7 -> 8; matrix products, arithmetic and copies ran while one was open for 1% -> 0% of each run, Pallas kernels for 6% -> 6%
where the time goes in v4:
time: 139 us
  waiting for transfers between devices  76.2 us (55%)
  starting transfers between devices  25.9 us (19%)
  Pallas kernels  19.1 us (14%)
  between operations  15.5 us (11%)
    all_to_all x1, waiting for transfers between devices, body(): tokens = lax.all_to_all(sent, PLANE, 0, 0).reshape(512, 2560)  35.2 us
    all_to_all x1, waiting for transfers between devices, body(): dn_parts = lax.all_to_all(dn, PLANE, 0, 0)  20.6 us
    pallas_call x11, Pallas kernels, run(): return call(kernel, outs, shapes, far=far, **kw)(*args)  19.1 us
    ppermute x5, waiting for transfers between devices, swap(): return lax.ppermute(a, axis, [(0, 1), (1, 0)])  15.7 us
    all_to_all x1, starting transfers between devices, body(): dn_parts = lax.all_to_all(dn, PLANE, 0, 0)  7.55 us
    all_to_all x1, starting transfers between devices, body(): tokens = lax.all_to_all(sent, PLANE, 0, 0).reshape(512, 2560)  7.54 us
    ppermute x5, starting transfers between devices, swap(): return lax.ppermute(a, axis, [(0, 1), (1, 0)])  6.21 us
    all_to_all x1, starting transfers between devices, body(): pieces = lax.all_to_all(gain_z.reshape(Z, 1, 128), 'z', 0, 0)  4.51 us
  transfers between devices with their start and end apart: 10, of which 8 were waited for; matrix products, arithmetic and copies ran while one was open for 0% of the time, Pallas kernels for 6%

profile of v4, /device:TPU:8, one launch (start us, length us, event | category | flops | bytes accessed | tf_op | source)
XLA Modules:
  0.0 138.5 jit_solution(14959183115104099119)
XLA Ops:
  7.2 0.0 all-gather.2.cloned.1.call-start
  7.2 1.8 %shard_map.154 = (bf16[16,5120]{1,0:T(8,128)(2,1)S(1)}, bf16[16,5120]{1,0:T(8,128)(2,1)S(1)}, bf16[160,1024]{1,0:T(8,128)(2,1)}) custom-call(bf16[160,384]{1,0:T(8,128)(2,1)} %wq.1, bf16[160,128]{1,0:T(8,128)(2,1)} %wk.1, bf16[160,128]{1,0:T(8,128)(2,1)} %wv.1, bf16[160,384]{1,0:T(8,128)(2,1)} %bitcast.19, bf16[16,5120]{1,0:T(8,128)(2,1)} %x, ...), custom_call_target="tpu_custom_call" | custom-call | bytes 1048576 | tf_op jit(solution)/shard_map/pallas_call | solution.py:57
  9.0 0.0 all-gather.2.cloned.1.call-update
  9.1 1.7 %shard_map.155 = bf16[32,16,2560]{2,1,0:T(8,128)(2,1)} custom-call(bf16[16,5120]{1,0:T(8,128)(2,1)S(1)} %get-tuple-element.26.n, bf16[16,5120]{1,0:T(8,128)(2,1)S(1)} %get-tuple-element.27.dy), custom_call_target="tpu_custom_call" | custom-call | bytes 3145728 | tf_op jit(solution)/shard_map/pallas_call | solution.py:57
  10.7 7.5 %all-to-all-start = ((bf16[32,16,2560]{2,1,0:T(8,128)(2,1)}), bf16[32,16,2560]{2,1,0:T(8,128)(2,1)S(1)}, u32[]{:S(2)}, u32[]{:S(2)}) async-start(bf16[32,16,2560]{2,1,0:T(8,128)(2,1)} %shard_map.155), calls=%async_computation | async-start | bytes 5242880 | tf_op jit(solution)/shard_map/all_to_all | solution.py:317
  18.3 0.0 reduce-scatter.2.cloned.1.call-start
  19.0 0.3 fusion
  19.3 0.1 pad_maximum_fusion
  19.5 35.2 %all-to-all-done = bf16[32,16,2560]{2,1,0:T(8,128)(2,1)S(1)} async-done(((bf16[32,16,2560]{2,1,0:T(8,128)(2,1)}), bf16[32,16,2560]{2,1,0:T(8,128)(2,1)S(1)}, u32[]{:S(2)}, u32[]{:S(2)}) %all-to-all-start) | async-done | bytes 2621472 | tf_op jit(solution)/shard_map/all_to_all | solution.py:317
  54.6 0.4 all-gather.2.cloned.1.call-done.w_far
  55.0 0.0 copy-start.1
  55.0 0.0 copy-start.2
  55.0 3.7 %shard_map.156 = (bf16[2,128,1024]{2,1,0:T(8,128)(2,1)S(1)}, bf16[2,128,1024]{2,1,0:T(8,128)(2,1)S(1)}) custom-call(s32[1]{0:T(128)} %bitcast.3.g_ref, bf16[512,2560]{1,0:T(8,128)(2,1)S(1)} %bitcast.12, bf16[1280,1024]{1,0:T(8,128)(2,1)} %all-gather.2.cloned.1.call-done.w_far), custom_call_target="tpu_custom_call" | custom-call | flops 1342177280 | bytes 7340032 | tf_op jit(solution)/shard_map/pallas_call | solution.py:57
  58.7 0.1 collective-permute-start
  58.8 1.9 %collective-permute-done.pair = bf16[2,128,1024]{2,1,0:T(8,128)(2,1)S(1)} collective-permute-done((bf16[2,128,1024]{2,1,0:T(8,128)(2,1)S(1)}, bf16[2,128,1024]{2,1,0:T(8,128)(2,1)S(1)}, u32[]{:S(2)}, u32[]{:S(2)}) %collective-permute-start) | collective-permute-done | bytes 524320 | tf_op jit(solution)/shard_map/ppermute | solution.py:286
  60.7 0.1 shard_map.157
  60.8 3.1 %collective-permute-start.1 = (bf16[128,1024]{1,0:T(8,128)(2,1)S(1)}, bf16[128,1024]{1,0:T(8,128)(2,1)S(1)}, u32[]{:S(2)}, u32[]{:S(2)}) collective-permute-start(bf16[128,1024]{1,0:T(8,128)(2,1)S(1)} %shard_map.157), channel_id=1, source_target_pairs={{0,16},{16,0},{1,17},{17,1},{2,18},{18,2},{3,19},{19,3},{4,20},{20... | collective-permute-start | bytes 786440 | tf_op jit(solution)/shard_map/ppermute | solution.py:286
  64.5 6.2 %collective-permute-done.1.far = bf16[128,1024]{1,0:T(8,128)(2,1)S(1)} collective-permute-done((bf16[128,1024]{1,0:T(8,128)(2,1)S(1)}, bf16[128,1024]{1,0:T(8,128)(2,1)S(1)}, u32[]{:S(2)}, u32[]{:S(2)}) %collective-permute-start.1) | collective-permute-done | bytes 262176 | tf_op jit(solution)/shard_map/ppermute | solution.py:286
  70.7 0.0 copy-done.1
  70.8 0.0 copy-done.2
  70.8 2.0 %shard_map.158.c0 = bf16[128,1024]{1,0:T(8,128)(2,1)S(1)} custom-call(s32[1]{0:T(128)S(6)} %copy.19.limit_ref, bf16[2,128,1024]{2,1,0:T(8,128)(2,1)S(1)} %get-tuple-element.30.keep.mine, bf16[2,128,1024]{2,1,0:T(8,128)(2,1)S(1)} %collective-permute-done.pair, bf16[128,1024]{1,0:T(8,128)(2,1)S(1)} %collective-permute-done.1.far, ...), custom_call_target="tpu_custom_call" | custom-call | flops 566231040 | bytes 4194304 | tf_op jit(solution)/shard_map/pallas_call | solution.py:57
  72.8 3.1 %collective-permute-start.3 = (bf16[128,1024]{1,0:T(8,128)(2,1)S(1)}, bf16[128,1024]{1,0:T(8,128)(2,1)S(1)}, u32[]{:S(2)}, u32[]{:S(2)}) collective-permute-start(bf16[128,1024]{1,0:T(8,128)(2,1)S(1)} %shard_map.158.c0), channel_id=1, source_target_pairs={{0,16},{16,0},{1,17},{17,1},{2,18},{18,2},{3,19},{19,3},{4,20},{20... | collective-permute-start | bytes 786440 | tf_op jit(solution)/shard_map/ppermute | solution.py:286
  75.8 0.0 collective-permute-start.2
  75.8 6.1 %collective-permute-done.3.c2 = bf16[128,1024]{1,0:T(8,128)(2,1)S(1)} collective-permute-done((bf16[128,1024]{1,0:T(8,128)(2,1)S(1)}, bf16[128,1024]{1,0:T(8,128)(2,1)S(1)}, u32[]{:S(2)}, u32[]{:S(2)}) %collective-permute-start.3) | collective-permute-done | bytes 262176 | tf_op jit(solution)/shard_map/ppermute | solution.py:286
  81.9 0.0 collective-permute-start.4
  81.9 0.0 collective-permute-done.2.c1
  81.9 1.5 %collective-permute-done.4.c3 = bf16[128,1024]{1,0:T(8,128)(2,1)S(1)} collective-permute-done((bf16[128,1024]{1,0:T(8,128)(2,1)S(1)}, bf16[128,1024]{1,0:T(8,128)(2,1)S(1)}, u32[]{:S(2)}, u32[]{:S(2)}) %collective-permute-start.4) | collective-permute-done | bytes 262176 | tf_op jit(solution)/shard_map/ppermute | solution.py:286
  83.4 2.8 %shard_map.159 = (bf16[512,640]{1,0:T(8,128)(2,1)S(1)}, bf16[1280,1024]{1,0:T(8,128)(2,1)}) custom-call(s32[1]{0:T(128)} %bitcast.3.g_ref, bf16[512,2560]{1,0:T(8,128)(2,1)S(1)} %bitcast.13, bf16[128,1024]{1,0:T(8,128)(2,1)S(1)} %shard_map.158.c0, bf16[128,1024]{1,0:T(8,128)(2,1)S(1)} %collective-permute-done.2.c1, ...), custom_call_target="tpu_custom_call" | custom-call | flops 1342177280 | bytes 8388608 | tf_op jit(solution)/shard_map/pallas_call | solution.py:57
  86.2 0.0 reduce-scatter.2.cloned.1.call-update
  86.2 3.5 %shard_map.160 = bf16[32,16,1408]{2,1,0:T(8,128)(2,1)} custom-call(bf16[512,2560]{1,0:T(8,128)(2,1)S(1)} %bitcast.14, bf16[512,640]{1,0:T(8,128)(2,1)S(1)} %get-tuple-element.34.cot, bf16[1280,1024]{1,0:T(8,128)(2,1)} %all-gather.2.cloned.1.call-done.w_far), custom_call_target="tpu_custom_call" | custom-call | flops 838860800 | bytes 7340032 | tf_op jit(solution)/shard_map/pallas_call | solution.py:57
  89.7 0.0 copy-start.3
  89.7 7.5 %all-to-all-start.1 = ((bf16[32,16,1408]{2,1,0:T(8,128)(2,1)}), bf16[32,16,1408]{2,1,0:T(8,128)(2,1)S(1)}, u32[]{:S(2)}, u32[]{:S(2)}) async-start(bf16[32,16,1408]{2,1,0:T(8,128)(2,1)} %shard_map.160), calls=%async_computation.1 | async-start | bytes 2883584 | tf_op jit(solution)/shard_map/all_to_all | solution.py:385
  97.3 20.6 %all-to-all-done.1 = bf16[32,16,1408]{2,1,0:T(8,128)(2,1)S(1)} async-done(((bf16[32,16,1408]{2,1,0:T(8,128)(2,1)}), bf16[32,16,1408]{2,1,0:T(8,128)(2,1)S(1)}, u32[]{:S(2)}, u32[]{:S(2)}) %all-to-all-start.1) | async-done | bytes 1441824 | tf_op jit(solution)/shard_map/all_to_all | solution.py:385
  117.9 0.6 shard_map.163
  118.5 4.5 %all-to-all-start.2 = ((f32[8,1,128]{2,1,0:T(1,128)}), f32[8,1,128]{2,1,0:T(1,128)S(1)}, u32[]{:S(2)}, u32[]{:S(2)}) async-start(f32[8,1,128]{2,1,0:T(1,128)} %bitcast.8), calls=%async_computation.2 | async-start | bytes 8192 | tf_op jit(solution)/shard_map/all_to_all | solution.py:395
  123.0 0.0 copy-done.3
  123.1 0.0 copy-start
  123.1 0.0 copy-start.4
  123.1 0.1 shard_map.161
  123.2 0.7 copy-done
  124.0 0.0 copy-done.4
  124.0 1.1 shard_map.162
  125.0 4.3 %reduce-scatter.2.cloned.1.call-done.total = bf16[160,1024]{1,0:T(8,128)(2,1)} async-done(((bf16[1280,1024]{1,0:T(8,128)(2,1)}), bf16[160,1024]{1,0:T(8,128)(2,1)}) %reduce-scatter.2.cloned.1.call-update) | async-done | bytes 327696 | tf_op jit(solution)/shard_map/reduce_scatter | solution.py:369
  129.3 1.7 %shard_map.164 = (bf16[160,384]{1,0:T(8,128)(2,1)}, bf16[160,128]{1,0:T(8,128)(2,1)}, bf16[160,128]{1,0:T(8,128)(2,1)}, bf16[160,384]{1,0:T(8,128)(2,1)}) custom-call(bf16[160,1024]{1,0:T(8,128)(2,1)} %reduce-scatter.2.cloned.1.call-done.total), custom_call_target="tpu_custom_call" | custom-call | bytes 2097152 | tf_op jit(solution)/shard_map/pallas_call | solution.py:57
  131.0 0.0 all-to-all-done.2
  131.1 0.6 convert_divide_fusion
  (3 shorter events, 0.0 us)
Async XLA Ops:
  7.2 47.8 %all-gather.2.cloned.1.call-start = ((), (), s32[]{:S(2)}) async-start(), calls=%async_computation.4 | async-start | bytes 2949120 | tf_op jit(solution)/shard_map/all_gather | solution.py:308
  10.7 43.9 %all-to-all-start = ((bf16[32,16,2560]{2,1,0:T(8,128)(2,1)}), bf16[32,16,2560]{2,1,0:T(8,128)(2,1)S(1)}, u32[]{:S(2)}, u32[]{:S(2)}) async-start(bf16[32,16,2560]{2,1,0:T(8,128)(2,1)} %shard_map.155), calls=%async_computation | async-start | bytes 5242880 | tf_op jit(solution)/shard_map/all_to_all | solution.py:317
  18.3 111.0 %reduce-scatter.2.cloned.1.call-start = ((), (), s32[]{:S(2)}) async-start(), calls=%async_computation.5 | async-start | bytes 2949120 | tf_op jit(solution)/shard_map/reduce_scatter | solution.py:369
  55.0 15.8 %copy-start.1 = (bf16[1,1024,128]{2,1,0:T(8,128)(2,1)S(1)}, bf16[1,1024,128]{2,1,0:T(8,128)(2,1)}, u32[]{:S(2)}) copy-start(bf16[1,1024,128]{2,1,0:T(8,128)(2,1)} %param.18) | copy-start | bytes 786436
  55.0 15.8 %copy-start.2 = (bf16[1,1024,128]{2,1,0:T(8,128)(2,1)S(1)}, bf16[1,1024,128]{2,1,0:T(8,128)(2,1)}, u32[]{:S(2)}) copy-start(bf16[1,1024,128]{2,1,0:T(8,128)(2,1)} %param.19) | copy-start | bytes 786436
  58.7 2.0 %collective-permute-start = (bf16[2,128,1024]{2,1,0:T(8,128)(2,1)S(1)}, bf16[2,128,1024]{2,1,0:T(8,128)(2,1)S(1)}, u32[]{:S(2)}, u32[]{:S(2)}) collective-permute-start(bf16[2,128,1024]{2,1,0:T(8,128)(2,1)S(1)} %get-tuple-element.31), channel_id=1, source_target_pairs={{0,8},{8,0},{1,9},{9,1},{2,10},{10,2},{3,11},{11,3},{4,12},{12,4},... | collective-permute-start | bytes 1572872 | tf_op jit(solution)/shard_map/ppermute | solution.py:286
  60.8 9.9 %collective-permute-start.1 = (bf16[128,1024]{1,0:T(8,128)(2,1)S(1)}, bf16[128,1024]{1,0:T(8,128)(2,1)S(1)}, u32[]{:S(2)}, u32[]{:S(2)}) collective-permute-start(bf16[128,1024]{1,0:T(8,128)(2,1)S(1)} %shard_map.157), channel_id=1, source_target_pairs={{0,16},{16,0},{1,17},{17,1},{2,18},{18,2},{3,19},{19,3},{4,20},{20... | collective-permute-start | bytes 786440 | tf_op jit(solution)/shard_map/ppermute | solution.py:286
  72.8 9.1 %collective-permute-start.3 = (bf16[128,1024]{1,0:T(8,128)(2,1)S(1)}, bf16[128,1024]{1,0:T(8,128)(2,1)S(1)}, u32[]{:S(2)}, u32[]{:S(2)}) collective-permute-start(bf16[128,1024]{1,0:T(8,128)(2,1)S(1)} %shard_map.158.c0), channel_id=1, source_target_pairs={{0,16},{16,0},{1,17},{17,1},{2,18},{18,2},{3,19},{19,3},{4,20},{20... | collective-permute-start | bytes 786440 | tf_op jit(solution)/shard_map/ppermute | solution.py:286
  75.8 6.1 %collective-permute-start.2 = (bf16[128,1024]{1,0:T(8,128)(2,1)S(1)}, bf16[128,1024]{1,0:T(8,128)(2,1)S(1)}, u32[]{:S(2)}, u32[]{:S(2)}) collective-permute-start(bf16[128,1024]{1,0:T(8,128)(2,1)S(1)} %shard_map.158.c0), channel_id=1, source_target_pairs={{0,8},{8,0},{1,9},{9,1},{2,10},{10,2},{3,11},{11,3},{4,12},{12,4},... | collective-permute-start | bytes 786440 | tf_op jit(solution)/shard_map/ppermute | solution.py:286
  81.9 1.5 %collective-permute-start.4 = (bf16[128,1024]{1,0:T(8,128)(2,1)S(1)}, bf16[128,1024]{1,0:T(8,128)(2,1)S(1)}, u32[]{:S(2)}, u32[]{:S(2)}) collective-permute-start(bf16[128,1024]{1,0:T(8,128)(2,1)S(1)} %collective-permute-done.3.c2), channel_id=1, source_target_pairs={{0,8},{8,0},{1,9},{9,1},{2,10},{10,2},{3,11},{11,3},{4,12},{12,4},... | collective-permute-start | bytes 786440 | tf_op jit(solution)/shard_map/ppermute | solution.py:286
  89.7 33.3 %copy-start.3 = (bf16[16,5120]{1,0:T(8,128)(2,1)S(1)}, bf16[16,5120]{1,0:T(8,128)(2,1)}, u32[]{:S(2)}) copy-start(bf16[16,5120]{1,0:T(8,128)(2,1)} %x) | copy-start | bytes 491524
  89.7 28.2 %all-to-all-start.1 = ((bf16[32,16,1408]{2,1,0:T(8,128)(2,1)}), bf16[32,16,1408]{2,1,0:T(8,128)(2,1)S(1)}, u32[]{:S(2)}, u32[]{:S(2)}) async-start(bf16[32,16,1408]{2,1,0:T(8,128)(2,1)} %shard_map.160), calls=%async_computation.1 | async-start | bytes 2883584 | tf_op jit(solution)/shard_map/all_to_all | solution.py:385
  118.5 12.5 %all-to-all-start.2 = ((f32[8,1,128]{2,1,0:T(1,128)}), f32[8,1,128]{2,1,0:T(1,128)S(1)}, u32[]{:S(2)}, u32[]{:S(2)}) async-start(f32[8,1,128]{2,1,0:T(1,128)} %bitcast.8), calls=%async_computation.2 | async-start | bytes 8192 | tf_op jit(solution)/shard_map/all_to_all | solution.py:395
  123.1 0.9 copy-start
  123.1 0.9 copy-start.4
Sparse Core Ops, SparseCore 0:
  9.8 45.1 all-gather.1
  86.4 42.8 reduce-scatter.1

commit v5 on v4

--- a/solution.py
+++ b/solution.py
@@ -68,22 +68,33 @@
     return made
 
 
-def join(wq, wk, wv, wo, x_far, dy_far, gain_far, n_out, dy_out, w_far, w, x, gain, sems):
+def prepare(
+    wq, wk, wv, wo, x_far, dy_far, gain_far, w_far, out_far, w, x, dy, gain, out, sems
+):
     parts = ((wq, 0, 384), (wk, 384, 512), (wv, 512, 640), (wo, 640, 1024))
     pairs = [(src, w.at[:, a:b]) for src, a, b in parts]
-    pairs += [(gain_far, gain), (x_far, x), (dy_far, dy_out)]
+    pairs += [(x_far, x), (gain_far, gain), (dy_far, dy)]
     copies = copies_of(pairs, sems)
     for copy in copies[:4]:
         copy.wait()
-    out_copy = pltpu.make_async_copy(w, w_far, sems.at[7])
-    out_copy.start()
-    copies[4].wait()
-    copies[5].wait()
+    sent = [pltpu.make_async_copy(w, w_far, sems.at[7])]
+    sent[0].start()
+    for copy in copies[4:]:
+        copy.wait()
     xf = x[...].astype(F32)
     inv = lax.rsqrt(jnp.mean(xf * xf, axis=1, keepdims=True) + EPS)
-    n_out[...] = (xf * inv * gain[...].reshape(1, -1).astype(F32)).astype(BF16)
-    copies[6].wait()
-    out_copy.wait()
+    n = (xf * inv * gain[...].reshape(1, -1).astype(F32)).astype(BF16)
+    for q in range(Q):
+        cols = [slice((Q * z + q) * 160, (Q * z + q + 1) * 160) for z in range(Z)]
+        row = jnp.concatenate([n[:, c] for c in cols] + [dy[:, c] for c in cols], axis=1)
+        for t in range(T):
+            out[q * T + t] = row
+        part = pl.ds(q * T, T)
+        copy = pltpu.make_async_copy(out.at[part], out_far.at[part], sems.at[8 + q])
+        copy.start()
+        sent.append(copy)
+    for copy in sent:
+        copy.wait()
 
 
 def split(total, q_out, k_out, v_out, o_out, q, k, v, o, sems):
@@ -93,21 +104,6 @@
     for i, (part, dst, _, _) in enumerate(parts):
         copies[i].wait()
         copy = pltpu.make_async_copy(part, dst, sems.at[4 + i])
-        copy.start()
-        sent.append(copy)
-    for copy in sent:
-        copy.wait()
-
-
-def lay_out(n, dy, out_far, out, sems):
-    sent = []
-    for q in range(Q):
-        cols = [slice((Q * z + q) * 160, (Q * z + q + 1) * 160) for z in range(Z)]
-        row = jnp.concatenate([n[:, c] for c in cols] + [dy[:, c] for c in cols], axis=1)
-        for t in range(T):
-            out[q * T + t] = row
-        part = pl.ds(q * T, T)
-        copy = pltpu.make_async_copy(out.at[part], out_far.at[part], sems.at[q])
         copy.start()
         sent.append(copy)
     for copy in sent:
@@ -200,15 +196,31 @@
         cot[rows, :] = block[:, : cot.shape[1]]
 
 
-def weight_grad(g_ref, tokens, c0, c1, c2, c3, cot_out, grad_far, grad, cot, sems):
+def weight_grad_near(g_ref, tokens, c0, c1, out, cot):
+    core = lax.rem(g_ref[0], 2)
+    cot[pl.ds(pl.multiple_of(core * 128, 128), 128), :] = c0[...]
+    cot[pl.ds(pl.multiple_of((1 - core) * 128, 128), 128), :] = c1[...]
+    rows = pl.ds(pl.multiple_of((g_ref[0] - core) * 128, 256), 256)
+    for r in range(5):
+        cols = slice(256 * r, 256 * (r + 1))
+        late = slice(1280 + 256 * r, 1280 + 256 * (r + 1))
+        out[cols, :640] = dot(tokens[rows, cols], cot[:, :640], 0, 0).astype(BF16)
+        out[cols, 640:] = dot(tokens[rows, late], cot[:, 640:], 0, 0).astype(BF16)
+
+
+def weight_grad(g_ref, tokens, near, c0, c1, c2, c3, cot_out, grad_far, grad, cot, sems):
     gather_rows(g_ref, (c0, c1, c2, c3), cot)
     cot_out[...] = cot[:, :640]
+    first = g_ref[0] - lax.rem(g_ref[0], 2)
+    rows = pl.ds(pl.multiple_of((2 - first) * 128, 256), 256)
     sent = []
     for r in range(5):
         cols = slice(256 * r, 256 * (r + 1))
         late = slice(1280 + 256 * r, 1280 + 256 * (r + 1))
-        grad[cols, :640] = dot(tokens[:, cols], cot[:, :640], 0, 0).astype(BF16)
-        grad[cols, 640:] = dot(tokens[:, late], cot[:, 640:], 0, 0).astype(BF16)
+        part = dot(tokens[rows, cols], cot[rows, :640], 0, 0)
+        grad[cols, :640] = (near[cols, :640].astype(F32) + part).astype(BF16)
+        part = dot(tokens[rows, late], cot[rows, 640:], 0, 0)
+        grad[cols, 640:] = (near[cols, 640:].astype(F32) + part).astype(BF16)
         copy = pltpu.make_async_copy(grad.at[cols], grad_far.at[cols], sems.at[r])
         copy.start()
         sent.append(copy)
@@ -291,29 +303,23 @@
     gs = lax.axis_index(QUARTER).astype(jnp.int32).reshape(1)
     kc, vc = kc.reshape(1024, HD), vc.reshape(1024, HD)
 
-    n_own, dy_own, w_own = run(
-        join,
-        [sds((16, 5120)), sds((16, 5120)), sds((160, 1024))],
+    w_own, sent = run(
+        prepare,
+        [sds((160, 1024)), sds((Q * T, 16, 2560))],
         (wq, wk, wv, wo.T, x, dy, gain),
         far=7,
-        far_out=1,
+        far_out=2,
         scratch=[
             pltpu.VMEM((160, 1024), BF16),
             pltpu.VMEM((16, 5120), BF16),
+            pltpu.VMEM((16, 5120), BF16),
             pltpu.VMEM((5120,), BF16),
-            pltpu.SemaphoreType.DMA((8,)),
+            pltpu.VMEM((Q * T, 16, 2560), BF16),
+            pltpu.SemaphoreType.DMA((8 + Q,)),
         ],
-        nbytes=1 << 20,
+        nbytes=4 << 20,
     )
     w = lax.all_gather(w_own, "z", axis=0, tiled=True)
-    (sent,) = run(
-        lay_out,
-        [sds((Q * T, 16, 2560))],
-        (n_own, dy_own),
-        far_out=1,
-        scratch=[pltpu.VMEM((Q * T, 16, 2560), BF16), pltpu.SemaphoreType.DMA((Q,))],
-        nbytes=3 << 20,
-    )
     tokens = lax.all_to_all(sent, PLANE, 0, 0).reshape(512, 2560)
 
     positions = (slab_start[0] + jnp.arange(128, dtype=jnp.int32)).astype(F32)
@@ -352,10 +358,19 @@
     )
     across = swap(cot, "xh")
     cots = (cot, swap(cot, "c"), across, swap(across, "c"))
+    (near,) = run(
+        weight_grad_near,
+        [sds((1280, 1024))],
+        (gs, tokens, cots[0], cots[1]),
+        smem=1,
+        scratch=[pltpu.VMEM((256, 1024), BF16)],
+        flops=512 * 1280 * 1024,
+        nbytes=6 << 20,
+    )
     cot4, grads = run(
         weight_grad,
         [sds((512, 640)), sds((1280, 1024))],
-        (gs, tokens, *cots),
+        (gs, tokens, near, *cots),
         smem=1,
         far_out=1,
         scratch=[
@@ -363,7 +378,7 @@
             pltpu.VMEM((512, 1024), BF16),
             pltpu.SemaphoreType.DMA((5,)),
         ],
-        flops=2 * 512 * 1280 * 1024,
+        flops=512 * 1280 * 1024,
         nbytes=8 << 20,
     )
     total = lax.psum_scatter(grads, "z", scatter_dimension=0, tiled=True)

time: 139 us -> 139 us (level)
  no operation moved by 1% of the time
where the time goes in v5:
time: 139 us; the launch traced here: 138 us
  waiting for transfers between devices  75.9 us (55%)
  starting transfers between devices  25.7 us (18%)
  Pallas kernels  19.1 us (14%)
  between operations  15.5 us (11%)
    all_to_all x1, waiting for transfers between devices, body(): tokens = lax.all_to_all(sent, PLANE, 0, 0).reshape(512, 2560)  35.2 us
    all_to_all x1, waiting for transfers between devices, body(): dn_parts = lax.all_to_all(dn, PLANE, 0, 0)  20.6 us
    pallas_call x11, Pallas kernels, run(): return call(kernel, outs, shapes, far=far, **kw)(*args)  19.1 us
    ppermute x5, waiting for transfers between devices, swap(): return lax.ppermute(a, axis, [(0, 1), (1, 0)])  14.6 us
    all_to_all x1, starting transfers between devices, body(): dn_parts = lax.all_to_all(dn, PLANE, 0, 0)  7.55 us
    all_to_all x1, starting transfers between devices, body(): tokens = lax.all_to_all(sent, PLANE, 0, 0).reshape(512, 2560)  7.55 us
    ppermute x5, starting transfers between devices, swap(): return lax.ppermute(a, axis, [(0, 1), (1, 0)])  6.21 us
    all_to_all x1, starting transfers between devices, body(): pieces = lax.all_to_all(gain_z.reshape(Z, 1, 128), 'z', 0, 0)  4.35 us
  transfers between devices with their start and end apart: 10, of which 8 were waited for; matrix products, arithmetic and copies ran while one was open for 0% of the time, Pallas kernels for 6%

profile of v5, /device:TPU:8, one launch (start us, length us, event | category | flops | bytes accessed | tf_op | source)
XLA Modules:
  0.0 138.1 jit_solution(12612229282513270931)
XLA Ops:
  7.2 0.0 all-gather.2.cloned.1.call-start
  7.2 3.1 %shard_map.154 = (bf16[160,1024]{1,0:T(8,128)(2,1)}, bf16[32,16,2560]{2,1,0:T(8,128)(2,1)}) custom-call(bf16[160,384]{1,0:T(8,128)(2,1)} %wq.1, bf16[160,128]{1,0:T(8,128)(2,1)} %wk.1, bf16[160,128]{1,0:T(8,128)(2,1)} %wv.1, bf16[160,384]{1,0:T(8,128)(2,1)} %bitcast.20, bf16[16,5120]{1,0:T(8,128)(2,1)} %x, bf16[16,5120]{1,0:T(8,128)(2,1)} %dy.1, ...), custom_call_target="tpu_custom_call" | custom-call | bytes 4194304 | tf_op jit(solution)/shard_map/pallas_call | solution.py:57
  10.3 0.0 all-gather.2.cloned.1.call-update
  10.3 7.5 %all-to-all-start = ((bf16[32,16,2560]{2,1,0:T(8,128)(2,1)}), bf16[32,16,2560]{2,1,0:T(8,128)(2,1)S(1)}, u32[]{:S(2)}, u32[]{:S(2)}) async-start(bf16[32,16,2560]{2,1,0:T(8,128)(2,1)} %get-tuple-element.25), calls=%async_computation | async-start | bytes 5242880 | tf_op jit(solution)/shard_map/all_to_all | solution.py:323
  17.9 0.0 reduce-scatter.2.cloned.1.call-start
  18.6 0.3 fusion
  18.9 0.1 pad_maximum_fusion
  19.0 35.2 %all-to-all-done = bf16[32,16,2560]{2,1,0:T(8,128)(2,1)S(1)} async-done(((bf16[32,16,2560]{2,1,0:T(8,128)(2,1)}), bf16[32,16,2560]{2,1,0:T(8,128)(2,1)S(1)}, u32[]{:S(2)}, u32[]{:S(2)}) %all-to-all-start) | async-done | bytes 2621472 | tf_op jit(solution)/shard_map/all_to_all | solution.py:323
  54.2 1.4 %all-gather.2.cloned.1.call-done.w_far = bf16[1280,1024]{1,0:T(8,128)(2,1)} async-done(((bf16[160,1024]{1,0:T(8,128)(2,1)}), bf16[1280,1024]{1,0:T(8,128)(2,1)}) %all-gather.2.cloned.1.call-update) | async-done | bytes 2621456 | tf_op jit(solution)/shard_map/all_gather | solution.py:322
  55.6 0.0 copy-start.1
  55.6 0.0 copy-start.2
  55.6 3.7 %shard_map.155 = (bf16[2,128,1024]{2,1,0:T(8,128)(2,1)S(1)}, bf16[2,128,1024]{2,1,0:T(8,128)(2,1)S(1)}) custom-call(s32[1]{0:T(128)} %bitcast.3.g_ref, bf16[512,2560]{1,0:T(8,128)(2,1)S(1)} %bitcast.12, bf16[1280,1024]{1,0:T(8,128)(2,1)} %all-gather.2.cloned.1.call-done.w_far), custom_call_target="tpu_custom_call" | custom-call | flops 1342177280 | bytes 7340032 | tf_op jit(solution)/shard_map/pallas_call | solution.py:57
  59.4 0.1 collective-permute-start
  59.5 1.9 %collective-permute-done.pair = bf16[2,128,1024]{2,1,0:T(8,128)(2,1)S(1)} collective-permute-done((bf16[2,128,1024]{2,1,0:T(8,128)(2,1)S(1)}, bf16[2,128,1024]{2,1,0:T(8,128)(2,1)S(1)}, u32[]{:S(2)}, u32[]{:S(2)}) %collective-permute-start) | collective-permute-done | bytes 524320 | tf_op jit(solution)/shard_map/ppermute | solution.py:298
  61.4 0.1 shard_map.156
  61.5 3.1 %collective-permute-start.1 = (bf16[128,1024]{1,0:T(8,128)(2,1)S(1)}, bf16[128,1024]{1,0:T(8,128)(2,1)S(1)}, u32[]{:S(2)}, u32[]{:S(2)}) collective-permute-start(bf16[128,1024]{1,0:T(8,128)(2,1)S(1)} %shard_map.156), channel_id=1, source_target_pairs={{0,16},{16,0},{1,17},{17,1},{2,18},{18,2},{3,19},{19,3},{4,20},{20... | collective-permute-start | bytes 786440 | tf_op jit(solution)/shard_map/ppermute | solution.py:298
  65.2 6.2 %collective-permute-done.1.far = bf16[128,1024]{1,0:T(8,128)(2,1)S(1)} collective-permute-done((bf16[128,1024]{1,0:T(8,128)(2,1)S(1)}, bf16[128,1024]{1,0:T(8,128)(2,1)S(1)}, u32[]{:S(2)}, u32[]{:S(2)}) %collective-permute-start.1) | collective-permute-done | bytes 262176 | tf_op jit(solution)/shard_map/ppermute | solution.py:298
  71.4 0.0 copy-done.1
  71.4 0.0 copy-done.2
  71.4 2.0 %shard_map.157.c0 = bf16[128,1024]{1,0:T(8,128)(2,1)S(1)} custom-call(s32[1]{0:T(128)S(6)} %copy.19.limit_ref, bf16[2,128,1024]{2,1,0:T(8,128)(2,1)S(1)} %get-tuple-element.28.keep.mine, bf16[2,128,1024]{2,1,0:T(8,128)(2,1)S(1)} %collective-permute-done.pair, bf16[128,1024]{1,0:T(8,128)(2,1)S(1)} %collective-permute-done.1.far, ...), custom_call_target="tpu_custom_call" | custom-call | flops 566231040 | bytes 4194304 | tf_op jit(solution)/shard_map/pallas_call | solution.py:57
  73.4 3.1 %collective-permute-start.3 = (bf16[128,1024]{1,0:T(8,128)(2,1)S(1)}, bf16[128,1024]{1,0:T(8,128)(2,1)S(1)}, u32[]{:S(2)}, u32[]{:S(2)}) collective-permute-start(bf16[128,1024]{1,0:T(8,128)(2,1)S(1)} %shard_map.157.c0), channel_id=1, source_target_pairs={{0,16},{16,0},{1,17},{17,1},{2,18},{18,2},{3,19},{19,3},{4,20},{20... | collective-permute-start | bytes 786440 | tf_op jit(solution)/shard_map/ppermute | solution.py:298
  76.5 0.0 collective-permute-start.2
  76.5 6.0 %collective-permute-done.3.c2 = bf16[128,1024]{1,0:T(8,128)(2,1)S(1)} collective-permute-done((bf16[128,1024]{1,0:T(8,128)(2,1)S(1)}, bf16[128,1024]{1,0:T(8,128)(2,1)S(1)}, u32[]{:S(2)}, u32[]{:S(2)}) %collective-permute-start.3) | collective-permute-done | bytes 262176 | tf_op jit(solution)/shard_map/ppermute | solution.py:298
  82.5 0.0 collective-permute-start.4
  82.5 0.0 collective-permute-done.2.c1
  82.5 1.1 shard_map.158.near
  83.7 0.4 collective-permute-done.4.c3
  84.0 2.1 %shard_map.159 = (bf16[512,640]{1,0:T(8,128)(2,1)S(1)}, bf16[1280,1024]{1,0:T(8,128)(2,1)}) custom-call(s32[1]{0:T(128)} %bitcast.3.g_ref, bf16[512,2560]{1,0:T(8,128)(2,1)S(1)} %bitcast.14, bf16[1280,1024]{1,0:T(8,128)(2,1)S(1)} %shard_map.158.near, bf16[128,1024]{1,0:T(8,128)(2,1)S(1)} %shard_map.157.c0, bf16[128,1024]{1,0:T(8,128)(2,1)S(1)} %collective-permute-done.2.c1, ...), custom_call_target="tpu_custom_call" | custom-call | flops 671088640 | bytes 8388608 | tf_op jit(solution)/shard_map/pallas_call | solution.py:57
  86.1 0.0 reduce-scatter.2.cloned.1.call-update
  86.2 3.5 %shard_map.160 = bf16[32,16,1408]{2,1,0:T(8,128)(2,1)} custom-call(bf16[512,2560]{1,0:T(8,128)(2,1)S(1)} %bitcast.15, bf16[512,640]{1,0:T(8,128)(2,1)S(1)} %get-tuple-element.32.cot, bf16[1280,1024]{1,0:T(8,128)(2,1)} %all-gather.2.cloned.1.call-done.w_far), custom_call_target="tpu_custom_call" | custom-call | flops 838860800 | bytes 7340032 | tf_op jit(solution)/shard_map/pallas_call | solution.py:57
  89.6 0.0 copy-start.3
  89.7 7.6 %all-to-all-start.1 = ((bf16[32,16,1408]{2,1,0:T(8,128)(2,1)}), bf16[32,16,1408]{2,1,0:T(8,128)(2,1)S(1)}, u32[]{:S(2)}, u32[]{:S(2)}) async-start(bf16[32,16,1408]{2,1,0:T(8,128)(2,1)} %shard_map.160), calls=%async_computation.1 | async-start | bytes 2883584 | tf_op jit(solution)/shard_map/all_to_all | solution.py:400
  97.2 20.6 %all-to-all-done.1 = bf16[32,16,1408]{2,1,0:T(8,128)(2,1)S(1)} async-done(((bf16[32,16,1408]{2,1,0:T(8,128)(2,1)}), bf16[32,16,1408]{2,1,0:T(8,128)(2,1)S(1)}, u32[]{:S(2)}, u32[]{:S(2)}) %all-to-all-start.1) | async-done | bytes 1441824 | tf_op jit(solution)/shard_map/all_to_all | solution.py:400
  117.8 0.6 shard_map.163
  118.4 4.3 %all-to-all-start.2 = ((f32[8,1,128]{2,1,0:T(1,128)}), f32[8,1,128]{2,1,0:T(1,128)S(1)}, u32[]{:S(2)}, u32[]{:S(2)}) async-start(f32[8,1,128]{2,1,0:T(1,128)} %bitcast.8), calls=%async_computation.2 | async-start | bytes 8192 | tf_op jit(solution)/shard_map/all_to_all | solution.py:410
  122.8 0.0 copy-done.3
  122.8 0.0 copy-start
  122.8 0.0 copy-start.4
  122.8 0.1 shard_map.161
  123.0 0.7 copy-done
  123.7 0.0 copy-done.4
  123.7 1.1 shard_map.162
  124.8 4.1 %reduce-scatter.2.cloned.1.call-done.total = bf16[160,1024]{1,0:T(8,128)(2,1)} async-done(((bf16[1280,1024]{1,0:T(8,128)(2,1)}), bf16[160,1024]{1,0:T(8,128)(2,1)}) %reduce-scatter.2.cloned.1.call-update) | async-done | bytes 327696 | tf_op jit(solution)/shard_map/reduce_scatter | solution.py:384
  128.9 1.7 %shard_map.164 = (bf16[160,384]{1,0:T(8,128)(2,1)}, bf16[160,128]{1,0:T(8,128)(2,1)}, bf16[160,128]{1,0:T(8,128)(2,1)}, bf16[160,384]{1,0:T(8,128)(2,1)}) custom-call(bf16[160,1024]{1,0:T(8,128)(2,1)} %reduce-scatter.2.cloned.1.call-done.total), custom_call_target="tpu_custom_call" | custom-call | bytes 2097152 | tf_op jit(solution)/shard_map/pallas_call | solution.py:57
  130.6 0.0 all-to-all-done.2
  130.7 0.6 convert_divide_fusion
  (3 shorter events, 0.0 us)
Async XLA Ops:
  7.2 48.5 %all-gather.2.cloned.1.call-start = ((), (), s32[]{:S(2)}) async-start(), calls=%async_computation.4 | async-start | bytes 2949120 | tf_op jit(solution)/shard_map/all_gather | solution.py:322
  10.3 43.9 %all-to-all-start = ((bf16[32,16,2560]{2,1,0:T(8,128)(2,1)}), bf16[32,16,2560]{2,1,0:T(8,128)(2,1)S(1)}, u32[]{:S(2)}, u32[]{:S(2)}) async-start(bf16[32,16,2560]{2,1,0:T(8,128)(2,1)} %get-tuple-element.25), calls=%async_computation | async-start | bytes 5242880 | tf_op jit(solution)/shard_map/all_to_all | solution.py:323
  17.9 111.0 %reduce-scatter.2.cloned.1.call-start = ((), (), s32[]{:S(2)}) async-start(), calls=%async_computation.5 | async-start | bytes 2949120 | tf_op jit(solution)/shard_map/reduce_scatter | solution.py:384
  55.6 15.8 %copy-start.1 = (bf16[1,1024,128]{2,1,0:T(8,128)(2,1)S(1)}, bf16[1,1024,128]{2,1,0:T(8,128)(2,1)}, u32[]{:S(2)}) copy-start(bf16[1,1024,128]{2,1,0:T(8,128)(2,1)} %param.18) | copy-start | bytes 786436
  55.6 15.8 %copy-start.2 = (bf16[1,1024,128]{2,1,0:T(8,128)(2,1)S(1)}, bf16[1,1024,128]{2,1,0:T(8,128)(2,1)}, u32[]{:S(2)}) copy-start(bf16[1,1024,128]{2,1,0:T(8,128)(2,1)} %param.19) | copy-start | bytes 786436
  59.4 2.0 %collective-permute-start = (bf16[2,128,1024]{2,1,0:T(8,128)(2,1)S(1)}, bf16[2,128,1024]{2,1,0:T(8,128)(2,1)S(1)}, u32[]{:S(2)}, u32[]{:S(2)}) collective-permute-start(bf16[2,128,1024]{2,1,0:T(8,128)(2,1)S(1)} %get-tuple-element.29), channel_id=1, source_target_pairs={{0,8},{8,0},{1,9},{9,1},{2,10},{10,2},{3,11},{11,3},{4,12},{12,4},... | collective-permute-start | bytes 1572872 | tf_op jit(solution)/shard_map/ppermute | solution.py:298
  61.5 9.9 %collective-permute-start.1 = (bf16[128,1024]{1,0:T(8,128)(2,1)S(1)}, bf16[128,1024]{1,0:T(8,128)(2,1)S(1)}, u32[]{:S(2)}, u32[]{:S(2)}) collective-permute-start(bf16[128,1024]{1,0:T(8,128)(2,1)S(1)} %shard_map.156), channel_id=1, source_target_pairs={{0,16},{16,0},{1,17},{17,1},{2,18},{18,2},{3,19},{19,3},{4,20},{20... | collective-permute-start | bytes 786440 | tf_op jit(solution)/shard_map/ppermute | solution.py:298
  73.4 9.1 %collective-permute-start.3 = (bf16[128,1024]{1,0:T(8,128)(2,1)S(1)}, bf16[128,1024]{1,0:T(8,128)(2,1)S(1)}, u32[]{:S(2)}, u32[]{:S(2)}) collective-permute-start(bf16[128,1024]{1,0:T(8,128)(2,1)S(1)} %shard_map.157.c0), channel_id=1, source_target_pairs={{0,16},{16,0},{1,17},{17,1},{2,18},{18,2},{3,19},{19,3},{4,20},{20... | collective-permute-start | bytes 786440 | tf_op jit(solution)/shard_map/ppermute | solution.py:298
  76.5 6.1 %collective-permute-start.2 = (bf16[128,1024]{1,0:T(8,128)(2,1)S(1)}, bf16[128,1024]{1,0:T(8,128)(2,1)S(1)}, u32[]{:S(2)}, u32[]{:S(2)}) collective-permute-start(bf16[128,1024]{1,0:T(8,128)(2,1)S(1)} %shard_map.157.c0), channel_id=1, source_target_pairs={{0,8},{8,0},{1,9},{9,1},{2,10},{10,2},{3,11},{11,3},{4,12},{12,4},... | collective-permute-start | bytes 786440 | tf_op jit(solution)/shard_map/ppermute | solution.py:298
  82.5 1.5 %collective-permute-start.4 = (bf16[128,1024]{1,0:T(8,128)(2,1)S(1)}, bf16[128,1024]{1,0:T(8,128)(2,1)S(1)}, u32[]{:S(2)}, u32[]{:S(2)}) collective-permute-start(bf16[128,1024]{1,0:T(8,128)(2,1)S(1)} %collective-permute-done.3.c2), channel_id=1, source_target_pairs={{0,8},{8,0},{1,9},{9,1},{2,10},{10,2},{3,11},{11,3},{4,12},{12,4},... | collective-permute-start | bytes 786440 | tf_op jit(solution)/shard_map/ppermute | solution.py:298
  89.6 33.2 %copy-start.3 = (bf16[16,5120]{1,0:T(8,128)(2,1)S(1)}, bf16[16,5120]{1,0:T(8,128)(2,1)}, u32[]{:S(2)}) copy-start(bf16[16,5120]{1,0:T(8,128)(2,1)} %x) | copy-start | bytes 491524
  89.7 28.2 %all-to-all-start.1 = ((bf16[32,16,1408]{2,1,0:T(8,128)(2,1)}), bf16[32,16,1408]{2,1,0:T(8,128)(2,1)S(1)}, u32[]{:S(2)}, u32[]{:S(2)}) async-start(bf16[32,16,1408]{2,1,0:T(8,128)(2,1)} %shard_map.160), calls=%async_computation.1 | async-start | bytes 2883584 | tf_op jit(solution)/shard_map/all_to_all | solution.py:400
  118.4 12.2 %all-to-all-start.2 = ((f32[8,1,128]{2,1,0:T(1,128)}), f32[8,1,128]{2,1,0:T(1,128)S(1)}, u32[]{:S(2)}, u32[]{:S(2)}) async-start(f32[8,1,128]{2,1,0:T(1,128)} %bitcast.8), calls=%async_computation.2 | async-start | bytes 8192 | tf_op jit(solution)/shard_map/all_to_all | solution.py:410
  122.8 0.9 copy-start
  122.8 0.9 copy-start.4
Sparse Core Ops, SparseCore 0:
  10.4 45.1 all-gather.1
  86.3 42.5 reduce-scatter.1

commit v6 on v5

--- a/solution.py
+++ b/solution.py
@@ -72,18 +72,18 @@
     wq, wk, wv, wo, x_far, dy_far, gain_far, w_far, out_far, w, x, dy, gain, out, sems
 ):
     parts = ((wq, 0, 384), (wk, 384, 512), (wv, 512, 640), (wo, 640, 1024))
-    pairs = [(src, w.at[:, a:b]) for src, a, b in parts]
-    pairs += [(x_far, x), (gain_far, gain), (dy_far, dy)]
+    pairs = [(x_far, x), (gain_far, gain), (dy_far, dy)]
+    pairs += [(src, w.at[:, a:b]) for src, a, b in parts]
     copies = copies_of(pairs, sems)
-    for copy in copies[:4]:
+    copies[0].wait()
+    xf = x[...].astype(F32)
+    inv = lax.rsqrt(jnp.mean(xf * xf, axis=1, keepdims=True) + EPS)
+    copies[1].wait()
+    n = (xf * inv * gain[...].reshape(1, -1).astype(F32)).astype(BF16)
+    for copy in copies[2:]:
         copy.wait()
     sent = [pltpu.make_async_copy(w, w_far, sems.at[7])]
     sent[0].start()
-    for copy in copies[4:]:
-        copy.wait()
-    xf = x[...].astype(F32)
-    inv = lax.rsqrt(jnp.mean(xf * xf, axis=1, keepdims=True) + EPS)
-    n = (xf * inv * gain[...].reshape(1, -1).astype(F32)).astype(BF16)
     for q in range(Q):
         cols = [slice((Q * z + q) * 160, (Q * z + q + 1) * 160) for z in range(Z)]
         row = jnp.concatenate([n[:, c] for c in cols] + [dy[:, c] for c in cols], axis=1)
@@ -110,21 +110,17 @@
         copy.wait()
 
 
-def project(g_ref, tokens, w_far, keep, send, w, total, sems):
-    halves = (slice(0, 640), slice(640, 1280))
-    parts = ((0, 384, 0), (384, 640, 0), (640, 1024, 1280))
-    copies = copies_of([(w_far.at[rows], w.at[rows]) for rows in halves], sems)
-    copies[0].wait()
-    for first, last, at in parts:
-        total[:, first:last] = dot(tokens[:, at : at + 640], w[halves[0], first:last], 1, 0)
-    copies[1].wait()
-    for first, last, at in parts:
-        part = dot(tokens[:, at + 640 : at + 1280], w[halves[1], first:last], 1, 0)
-        total[:, first:last] += part
+def project(g_ref, tokens, w_far, keep, send, w, held, sems):
+    pieces = [slice(160 * z, 160 * (z + 1)) for z in range(Z)]
+    for copy in copies_of([(w_far.at[rows], w.at[rows]) for rows in pieces], sems):
+        copy.wait()
+    for first, last, at in ((0, 384, 0), (384, 640, 0), (640, 1024, 1280)):
+        part = dot(tokens[:, at : at + 1280], w[:, first:last], 1, 0).astype(BF16)
+        for g in range(Q):
+            held[g_ref[0] ^ g, :, first:last] = part[128 * g : 128 * (g + 1), :]
     for xh in range(2):
-        for core, out in ((0, keep), (1, send)):
-            rows = pl.ds(pl.multiple_of((g_ref[0] ^ (2 * xh + core)) * 128, 128), 128)
-            out[xh] = total[rows, :].astype(BF16)
+        keep[xh] = held[2 * xh]
+        send[xh] = held[2 * xh + 1]
 
 
 def add(keep, pair, out):
@@ -338,8 +334,8 @@
         far=1,
         scratch=[
             pltpu.VMEM((1280, 1024), BF16),
-            pltpu.VMEM((512, 1024), F32),
-            pltpu.SemaphoreType.DMA((2,)),
+            pltpu.VMEM((Q, 128, 1024), BF16),
+            pltpu.SemaphoreType.DMA((Z,)),
         ],
         flops=2 * 512 * 1280 * 1024,
         nbytes=7 << 20,

time: 139 us -> 139 us (level)
  no operation moved by 1% of the time
where the time goes in v6:
time: 139 us; the launch traced here: 138 us
  waiting for transfers between devices  76.1 us (55%)
  starting transfers between devices  25.7 us (18%)
  Pallas kernels  19 us (14%)
  between operations  15.5 us (11%)
    all_to_all x1, waiting for transfers between devices, body(): tokens = lax.all_to_all(sent, PLANE, 0, 0).reshape(512, 2560)  35.2 us
    all_to_all x1, waiting for transfers between devices, body(): dn_parts = lax.all_to_all(dn, PLANE, 0, 0)  20.6 us
    pallas_call x11, Pallas kernels, run(): return call(kernel, outs, shapes, far=far, **kw)(*args)  19 us
    ppermute x5, waiting for transfers between devices, swap(): return lax.ppermute(a, axis, [(0, 1), (1, 0)])  14.6 us
    all_to_all x1, starting transfers between devices, body(): dn_parts = lax.all_to_all(dn, PLANE, 0, 0)  7.55 us
    all_to_all x1, starting transfers between devices, body(): tokens = lax.all_to_all(sent, PLANE, 0, 0).reshape(512, 2560)  7.55 us
    ppermute x5, starting transfers between devices, swap(): return lax.ppermute(a, axis, [(0, 1), (1, 0)])  6.21 us
    all_to_all x1, starting transfers between devices, body(): pieces = lax.all_to_all(gain_z.reshape(Z, 1, 128), 'z', 0, 0)  4.35 us
  transfers between devices with their start and end apart: 10, of which 8 were waited for; matrix products, arithmetic and copies ran while one was open for 0% of the time, Pallas kernels for 6%

profile of v6, /device:TPU:8, one launch (start us, length us, event | category | flops | bytes accessed | tf_op | source)
XLA Modules:
  0.0 138.2 jit_solution(4713181997792656987)
XLA Ops:
  7.2 0.0 all-gather.2.cloned.1.call-start
  7.2 2.9 %shard_map.154 = (bf16[160,1024]{1,0:T(8,128)(2,1)}, bf16[32,16,2560]{2,1,0:T(8,128)(2,1)}) custom-call(bf16[160,384]{1,0:T(8,128)(2,1)} %wq.1, bf16[160,128]{1,0:T(8,128)(2,1)} %wk.1, bf16[160,128]{1,0:T(8,128)(2,1)} %wv.1, bf16[160,384]{1,0:T(8,128)(2,1)} %bitcast.20, bf16[16,5120]{1,0:T(8,128)(2,1)} %x, bf16[16,5120]{1,0:T(8,128)(2,1)} %dy.1, ...), custom_call_target="tpu_custom_call" | custom-call | bytes 4194304 | tf_op jit(solution)/shard_map/pallas_call | solution.py:57
  10.2 0.0 all-gather.2.cloned.1.call-update
  10.2 7.5 %all-to-all-start = ((bf16[32,16,2560]{2,1,0:T(8,128)(2,1)}), bf16[32,16,2560]{2,1,0:T(8,128)(2,1)S(1)}, u32[]{:S(2)}, u32[]{:S(2)}) async-start(bf16[32,16,2560]{2,1,0:T(8,128)(2,1)} %get-tuple-element.25), calls=%async_computation | async-start | bytes 5242880 | tf_op jit(solution)/shard_map/all_to_all | solution.py:319
  17.7 0.0 reduce-scatter.2.cloned.1.call-start
  18.5 0.3 fusion
  18.8 0.1 pad_maximum_fusion
  18.9 35.2 %all-to-all-done = bf16[32,16,2560]{2,1,0:T(8,128)(2,1)S(1)} async-done(((bf16[32,16,2560]{2,1,0:T(8,128)(2,1)}), bf16[32,16,2560]{2,1,0:T(8,128)(2,1)S(1)}, u32[]{:S(2)}, u32[]{:S(2)}) %all-to-all-start) | async-done | bytes 2621472 | tf_op jit(solution)/shard_map/all_to_all | solution.py:319
  54.1 1.4 %all-gather.2.cloned.1.call-done.w_far = bf16[1280,1024]{1,0:T(8,128)(2,1)} async-done(((bf16[160,1024]{1,0:T(8,128)(2,1)}), bf16[1280,1024]{1,0:T(8,128)(2,1)}) %all-gather.2.cloned.1.call-update) | async-done | bytes 2621456 | tf_op jit(solution)/shard_map/all_gather | solution.py:318
  55.5 0.0 copy-start.1
  55.5 0.0 copy-start.2
  55.5 3.8 %shard_map.155 = (bf16[2,128,1024]{2,1,0:T(8,128)(2,1)S(1)}, bf16[2,128,1024]{2,1,0:T(8,128)(2,1)S(1)}) custom-call(s32[1]{0:T(128)} %bitcast.3.g_ref, bf16[512,2560]{1,0:T(8,128)(2,1)S(1)} %bitcast.12, bf16[1280,1024]{1,0:T(8,128)(2,1)} %all-gather.2.cloned.1.call-done.w_far), custom_call_target="tpu_custom_call" | custom-call | flops 1342177280 | bytes 7340032 | tf_op jit(solution)/shard_map/pallas_call | solution.py:57
  59.3 0.1 collective-permute-start
  59.4 1.9 %collective-permute-done.pair = bf16[2,128,1024]{2,1,0:T(8,128)(2,1)S(1)} collective-permute-done((bf16[2,128,1024]{2,1,0:T(8,128)(2,1)S(1)}, bf16[2,128,1024]{2,1,0:T(8,128)(2,1)S(1)}, u32[]{:S(2)}, u32[]{:S(2)}) %collective-permute-start) | collective-permute-done | bytes 524320 | tf_op jit(solution)/shard_map/ppermute | solution.py:294
  61.3 0.1 shard_map.156
  61.4 3.1 %collective-permute-start.1 = (bf16[128,1024]{1,0:T(8,128)(2,1)S(1)}, bf16[128,1024]{1,0:T(8,128)(2,1)S(1)}, u32[]{:S(2)}, u32[]{:S(2)}) collective-permute-start(bf16[128,1024]{1,0:T(8,128)(2,1)S(1)} %shard_map.156), channel_id=1, source_target_pairs={{0,16},{16,0},{1,17},{17,1},{2,18},{18,2},{3,19},{19,3},{4,20},{20... | collective-permute-start | bytes 786440 | tf_op jit(solution)/shard_map/ppermute | solution.py:294
  65.1 6.2 %collective-permute-done.1.far = bf16[128,1024]{1,0:T(8,128)(2,1)S(1)} collective-permute-done((bf16[128,1024]{1,0:T(8,128)(2,1)S(1)}, bf16[128,1024]{1,0:T(8,128)(2,1)S(1)}, u32[]{:S(2)}, u32[]{:S(2)}) %collective-permute-start.1) | collective-permute-done | bytes 262176 | tf_op jit(solution)/shard_map/ppermute | solution.py:294
  71.3 0.0 copy-done.1
  71.3 0.0 copy-done.2
  71.3 2.0 %shard_map.157.c0 = bf16[128,1024]{1,0:T(8,128)(2,1)S(1)} custom-call(s32[1]{0:T(128)S(6)} %copy.19.limit_ref, bf16[2,128,1024]{2,1,0:T(8,128)(2,1)S(1)} %get-tuple-element.28.keep.mine, bf16[2,128,1024]{2,1,0:T(8,128)(2,1)S(1)} %collective-permute-done.pair, bf16[128,1024]{1,0:T(8,128)(2,1)S(1)} %collective-permute-done.1.far, ...), custom_call_target="tpu_custom_call" | custom-call | flops 566231040 | bytes 4194304 | tf_op jit(solution)/shard_map/pallas_call | solution.py:57
  73.3 3.1 %collective-permute-start.3 = (bf16[128,1024]{1,0:T(8,128)(2,1)S(1)}, bf16[128,1024]{1,0:T(8,128)(2,1)S(1)}, u32[]{:S(2)}, u32[]{:S(2)}) collective-permute-start(bf16[128,1024]{1,0:T(8,128)(2,1)S(1)} %shard_map.157.c0), channel_id=1, source_target_pairs={{0,16},{16,0},{1,17},{17,1},{2,18},{18,2},{3,19},{19,3},{4,20},{20... | collective-permute-start | bytes 786440 | tf_op jit(solution)/shard_map/ppermute | solution.py:294
  76.4 0.0 collective-permute-start.2
  76.4 6.0 %collective-permute-done.3.c2 = bf16[128,1024]{1,0:T(8,128)(2,1)S(1)} collective-permute-done((bf16[128,1024]{1,0:T(8,128)(2,1)S(1)}, bf16[128,1024]{1,0:T(8,128)(2,1)S(1)}, u32[]{:S(2)}, u32[]{:S(2)}) %collective-permute-start.3) | collective-permute-done | bytes 262176 | tf_op jit(solution)/shard_map/ppermute | solution.py:294
  82.4 0.0 collective-permute-start.4
  82.4 0.0 collective-permute-done.2.c1
  82.4 1.1 shard_map.158.near
  83.6 0.4 collective-permute-done.4.c3
  84.0 2.1 %shard_map.159 = (bf16[512,640]{1,0:T(8,128)(2,1)S(1)}, bf16[1280,1024]{1,0:T(8,128)(2,1)}) custom-call(s32[1]{0:T(128)} %bitcast.3.g_ref, bf16[512,2560]{1,0:T(8,128)(2,1)S(1)} %bitcast.14, bf16[1280,1024]{1,0:T(8,128)(2,1)S(1)} %shard_map.158.near, bf16[128,1024]{1,0:T(8,128)(2,1)S(1)} %shard_map.157.c0, bf16[128,1024]{1,0:T(8,128)(2,1)S(1)} %collective-permute-done.2.c1, ...), custom_call_target="tpu_custom_call" | custom-call | flops 671088640 | bytes 8388608 | tf_op jit(solution)/shard_map/pallas_call | solution.py:57
  86.1 0.0 reduce-scatter.2.cloned.1.call-update
  86.1 3.5 %shard_map.160 = bf16[32,16,1408]{2,1,0:T(8,128)(2,1)} custom-call(bf16[512,2560]{1,0:T(8,128)(2,1)S(1)} %bitcast.15, bf16[512,640]{1,0:T(8,128)(2,1)S(1)} %get-tuple-element.32.cot, bf16[1280,1024]{1,0:T(8,128)(2,1)} %all-gather.2.cloned.1.call-done.w_far), custom_call_target="tpu_custom_call" | custom-call | flops 838860800 | bytes 7340032 | tf_op jit(solution)/shard_map/pallas_call | solution.py:57
  89.6 0.0 copy-start.3
  89.6 7.6 %all-to-all-start.1 = ((bf16[32,16,1408]{2,1,0:T(8,128)(2,1)}), bf16[32,16,1408]{2,1,0:T(8,128)(2,1)S(1)}, u32[]{:S(2)}, u32[]{:S(2)}) async-start(bf16[32,16,1408]{2,1,0:T(8,128)(2,1)} %shard_map.160), calls=%async_computation.1 | async-start | bytes 2883584 | tf_op jit(solution)/shard_map/all_to_all | solution.py:396
  97.2 20.6 %all-to-all-done.1 = bf16[32,16,1408]{2,1,0:T(8,128)(2,1)S(1)} async-done(((bf16[32,16,1408]{2,1,0:T(8,128)(2,1)}), bf16[32,16,1408]{2,1,0:T(8,128)(2,1)S(1)}, u32[]{:S(2)}, u32[]{:S(2)}) %all-to-all-start.1) | async-done | bytes 1441824 | tf_op jit(solution)/shard_map/all_to_all | solution.py:396
  117.8 0.6 shard_map.163
  118.4 4.3 %all-to-all-start.2 = ((f32[8,1,128]{2,1,0:T(1,128)}), f32[8,1,128]{2,1,0:T(1,128)S(1)}, u32[]{:S(2)}, u32[]{:S(2)}) async-start(f32[8,1,128]{2,1,0:T(1,128)} %bitcast.8), calls=%async_computation.2 | async-start | bytes 8192 | tf_op jit(solution)/shard_map/all_to_all | solution.py:406
  122.7 0.0 copy-done.3
  122.7 0.0 copy-start
  122.7 0.0 copy-start.4
  122.7 0.1 shard_map.161
  122.9 0.7 copy-done
  123.6 0.0 copy-done.4
  123.6 1.1 shard_map.162
  124.7 4.3 %reduce-scatter.2.cloned.1.call-done.total = bf16[160,1024]{1,0:T(8,128)(2,1)} async-done(((bf16[1280,1024]{1,0:T(8,128)(2,1)}), bf16[160,1024]{1,0:T(8,128)(2,1)}) %reduce-scatter.2.cloned.1.call-update) | async-done | bytes 327696 | tf_op jit(solution)/shard_map/reduce_scatter | solution.py:380
  129.0 1.7 %shard_map.164 = (bf16[160,384]{1,0:T(8,128)(2,1)}, bf16[160,128]{1,0:T(8,128)(2,1)}, bf16[160,128]{1,0:T(8,128)(2,1)}, bf16[160,384]{1,0:T(8,128)(2,1)}) custom-call(bf16[160,1024]{1,0:T(8,128)(2,1)} %reduce-scatter.2.cloned.1.call-done.total), custom_call_target="tpu_custom_call" | custom-call | bytes 2097152 | tf_op jit(solution)/shard_map/pallas_call | solution.py:57
  130.7 0.0 all-to-all-done.2
  130.7 0.6 convert_divide_fusion
  (3 shorter events, 0.0 us)
Async XLA Ops:
  7.2 48.3 %all-gather.2.cloned.1.call-start = ((), (), s32[]{:S(2)}) async-start(), calls=%async_computation.4 | async-start | bytes 2949120 | tf_op jit(solution)/shard_map/all_gather | solution.py:318
  10.2 43.9 %all-to-all-start = ((bf16[32,16,2560]{2,1,0:T(8,128)(2,1)}), bf16[32,16,2560]{2,1,0:T(8,128)(2,1)S(1)}, u32[]{:S(2)}, u32[]{:S(2)}) async-start(bf16[32,16,2560]{2,1,0:T(8,128)(2,1)} %get-tuple-element.25), calls=%async_computation | async-start | bytes 5242880 | tf_op jit(solution)/shard_map/all_to_all | solution.py:319
  17.7 111.2 %reduce-scatter.2.cloned.1.call-start = ((), (), s32[]{:S(2)}) async-start(), calls=%async_computation.5 | async-start | bytes 2949120 | tf_op jit(solution)/shard_map/reduce_scatter | solution.py:380
  55.5 15.8 %copy-start.1 = (bf16[1,1024,128]{2,1,0:T(8,128)(2,1)S(1)}, bf16[1,1024,128]{2,1,0:T(8,128)(2,1)}, u32[]{:S(2)}) copy-start(bf16[1,1024,128]{2,1,0:T(8,128)(2,1)} %param.18) | copy-start | bytes 786436
  55.5 15.8 %copy-start.2 = (bf16[1,1024,128]{2,1,0:T(8,128)(2,1)S(1)}, bf16[1,1024,128]{2,1,0:T(8,128)(2,1)}, u32[]{:S(2)}) copy-start(bf16[1,1024,128]{2,1,0:T(8,128)(2,1)} %param.19) | copy-start | bytes 786436
  59.3 2.0 %collective-permute-start = (bf16[2,128,1024]{2,1,0:T(8,128)(2,1)S(1)}, bf16[2,128,1024]{2,1,0:T(8,128)(2,1)S(1)}, u32[]{:S(2)}, u32[]{:S(2)}) collective-permute-start(bf16[2,128,1024]{2,1,0:T(8,128)(2,1)S(1)} %get-tuple-element.29), channel_id=1, source_target_pairs={{0,8},{8,0},{1,9},{9,1},{2,10},{10,2},{3,11},{11,3},{4,12},{12,4},... | collective-permute-start | bytes 1572872 | tf_op jit(solution)/shard_map/ppermute | solution.py:294
  61.4 9.9 %collective-permute-start.1 = (bf16[128,1024]{1,0:T(8,128)(2,1)S(1)}, bf16[128,1024]{1,0:T(8,128)(2,1)S(1)}, u32[]{:S(2)}, u32[]{:S(2)}) collective-permute-start(bf16[128,1024]{1,0:T(8,128)(2,1)S(1)} %shard_map.156), channel_id=1, source_target_pairs={{0,16},{16,0},{1,17},{17,1},{2,18},{18,2},{3,19},{19,3},{4,20},{20... | collective-permute-start | bytes 786440 | tf_op jit(solution)/shard_map/ppermute | solution.py:294
  73.3 9.1 %collective-permute-start.3 = (bf16[128,1024]{1,0:T(8,128)(2,1)S(1)}, bf16[128,1024]{1,0:T(8,128)(2,1)S(1)}, u32[]{:S(2)}, u32[]{:S(2)}) collective-permute-start(bf16[128,1024]{1,0:T(8,128)(2,1)S(1)} %shard_map.157.c0), channel_id=1, source_target_pairs={{0,16},{16,0},{1,17},{17,1},{2,18},{18,2},{3,19},{19,3},{4,20},{20... | collective-permute-start | bytes 786440 | tf_op jit(solution)/shard_map/ppermute | solution.py:294
  76.4 6.1 %collective-permute-start.2 = (bf16[128,1024]{1,0:T(8,128)(2,1)S(1)}, bf16[128,1024]{1,0:T(8,128)(2,1)S(1)}, u32[]{:S(2)}, u32[]{:S(2)}) collective-permute-start(bf16[128,1024]{1,0:T(8,128)(2,1)S(1)} %shard_map.157.c0), channel_id=1, source_target_pairs={{0,8},{8,0},{1,9},{9,1},{2,10},{10,2},{3,11},{11,3},{4,12},{12,4},... | collective-permute-start | bytes 786440 | tf_op jit(solution)/shard_map/ppermute | solution.py:294
  82.4 1.5 %collective-permute-start.4 = (bf16[128,1024]{1,0:T(8,128)(2,1)S(1)}, bf16[128,1024]{1,0:T(8,128)(2,1)S(1)}, u32[]{:S(2)}, u32[]{:S(2)}) collective-permute-start(bf16[128,1024]{1,0:T(8,128)(2,1)S(1)} %collective-permute-done.3.c2), channel_id=1, source_target_pairs={{0,8},{8,0},{1,9},{9,1},{2,10},{10,2},{3,11},{11,3},{4,12},{12,4},... | collective-permute-start | bytes 786440 | tf_op jit(solution)/shard_map/ppermute | solution.py:294
  89.6 33.1 %copy-start.3 = (bf16[16,5120]{1,0:T(8,128)(2,1)S(1)}, bf16[16,5120]{1,0:T(8,128)(2,1)}, u32[]{:S(2)}) copy-start(bf16[16,5120]{1,0:T(8,128)(2,1)} %x) | copy-start | bytes 491524
  89.6 28.2 %all-to-all-start.1 = ((bf16[32,16,1408]{2,1,0:T(8,128)(2,1)}), bf16[32,16,1408]{2,1,0:T(8,128)(2,1)S(1)}, u32[]{:S(2)}, u32[]{:S(2)}) async-start(bf16[32,16,1408]{2,1,0:T(8,128)(2,1)} %shard_map.160), calls=%async_computation.1 | async-start | bytes 2883584 | tf_op jit(solution)/shard_map/all_to_all | solution.py:396
  118.4 12.3 %all-to-all-start.2 = ((f32[8,1,128]{2,1,0:T(1,128)}), f32[8,1,128]{2,1,0:T(1,128)S(1)}, u32[]{:S(2)}, u32[]{:S(2)}) async-start(f32[8,1,128]{2,1,0:T(1,128)} %bitcast.8), calls=%async_computation.2 | async-start | bytes 8192 | tf_op jit(solution)/shard_map/all_to_all | solution.py:406
  122.7 0.9 copy-start
  122.7 0.9 copy-start.4
Sparse Core Ops, SparseCore 0:
  10.3 45.1 all-gather.1
  86.2 42.7 reduce-scatter.1
